TPU v7x, 512 devices: a whole 4x8x8 slice. The times are simulated.
512 devices in a mesh: query: 8 (over y_lo, x), mem: 64 (over z, y_hi, core).
Axes of the slice: x: 4, y: 8 (y_hi: 4, y_lo: 2; y = y_hi * 2 + y_lo), z: 8, core: 2. Of those that a mesh axis runs over, the one named last changes fastest.
Arguments:
- queries: bfloat16 [8, 256, 2560], P('query', 'mem'), may hold values from -6 to 6
- grad_out: bfloat16 [8, 256, 2560], P('query', 'mem'), may hold values from -6 to 6
- attn_out: bfloat16 [8, 256, 2560], P('query', 'mem'), may hold values from -3 to 3
- lse: float32 [8, 256, 20], P('query', 'mem'), may hold values from 2 to 5
- keys: bfloat16 [64, 128, 2560], P('mem'), may hold values from -6 to 6
- values: bfloat16 [64, 128, 2560], P('mem'), may hold values from -6 to 6
- frame_ids: int32 [8, 64], replicated, may hold values from 0 to 63, as said below
- counts: int32 [8], replicated, may hold values from 8 to 64, as said below
Outputs:
- grad_queries: bfloat16 [8, 256, 2560], P('query', 'mem')
- grad_keys: bfloat16 [64, 128, 2560], P('mem', 'query')
- grad_values: bfloat16 [64, 128, 2560], P('mem', 'query')
Inputs may be any that keep to these rules, and one draw needn't show every extreme that they name: `frame_ids`: each row lists 64 different memory frames; only the first counts[f] entries of row f count. `counts`: some frame has exactly 64 and some exactly 8.
All inputs are finite; a program needn't handle non-finite values.
Results may differ from a plain program's by a relative error of at most 0.015.
Values may be sent and summed in bfloat16 or wider, within the bound.
No kernel may reach another device: no remote copies, remote signals or barrier semaphores. Data moves between devices by JAX's collectives and lax.ppermute only.
A program may use at most 64 MiB of HBM per device.

v0:
```python
import jax
import jax.numpy as jnp
from jax import lax
from jax.sharding import PartitionSpec as P

HS = 128


def block_terms(query_rows, grad_rows, lse_rows, delta_rows, key_rows, value_rows, key_mask):
    score_scale = HS ** (-0.5)
    scores = (
        jnp.einsum("qhd,khd->hqk", query_rows, key_rows, preferred_element_type=jnp.float32)
        * score_scale
    )
    attn_probs = jnp.exp(scores - jnp.transpose(lse_rows)[:, :, None]) * key_mask[None, None, :]
    probs_low = attn_probs.astype(jnp.bfloat16)
    value_term = jnp.einsum(
        "hqk,qhd->khd", probs_low, grad_rows, preferred_element_type=jnp.float32
    )
    grad_probs = jnp.einsum(
        "qhd,khd->hqk", grad_rows, value_rows, preferred_element_type=jnp.float32
    )
    grad_scores = (attn_probs * (grad_probs - jnp.transpose(delta_rows)[:, :, None])).astype(
        jnp.bfloat16
    )
    query_term = (
        jnp.einsum("hqk,khd->qhd", grad_scores, key_rows, preferred_element_type=jnp.float32)
        * score_scale
    )
    key_term = (
        jnp.einsum("hqk,qhd->khd", grad_scores, query_rows, preferred_element_type=jnp.float32)
        * score_scale
    )
    return (query_term, key_term, value_term)


def on_device(queries, grad_out, attn_out, lse, keys, values, frame_ids, counts):
    query_pos = lax.axis_index("query")
    mem_pos = lax.axis_index("mem")
    frames_here = queries.shape[0]
    mem_here = keys.shape[0]
    frame_tokens = keys.shape[1]
    heads = lse.shape[2]
    head_size = queries.shape[2] // heads
    query_all, grad_all, output_all = (
        lax.all_gather(queries, "mem", axis=1, tiled=True),
        lax.all_gather(grad_out, "mem", axis=1, tiled=True),
        lax.all_gather(attn_out, "mem", axis=1, tiled=True),
    )
    lse_all = lax.all_gather(lse, "mem", axis=1, tiled=True)
    query_all = query_all.reshape(frames_here, -1, heads, head_size)
    grad_all = grad_all.reshape(frames_here, -1, heads, head_size)
    output_all = output_all.reshape(frames_here, -1, heads, head_size)
    delta_all = jnp.sum(grad_all.astype(jnp.float32) * output_all.astype(jnp.float32), axis=-1)
    rows_all = query_all.shape[1]
    ids_here = lax.dynamic_slice_in_dim(frame_ids, query_pos * frames_here, frames_here, 0)
    counts_here = lax.dynamic_slice_in_dim(counts, query_pos * frames_here, frames_here, 0)
    within = jnp.arange(frame_ids.shape[1], dtype=jnp.int32)[None, :] < counts_here[:, None]
    owned = mem_pos * mem_here + jnp.arange(mem_here, dtype=jnp.int32)
    matches = (ids_here[:, :, None] == owned[None, None, :]) & within[:, :, None]
    retrieved = jnp.any(matches, axis=1)
    retrieved_weight = jnp.where(retrieved, 1.0, 0.0).astype(jnp.float32)
    key_heads = keys.reshape(mem_here, frame_tokens, heads, head_size)
    value_heads = values.reshape(mem_here, frame_tokens, heads, head_size)
    key_flat = key_heads.reshape(mem_here * frame_tokens, heads, head_size)
    value_flat = value_heads.reshape(mem_here * frame_tokens, heads, head_size)
    key_mask = jnp.repeat(retrieved_weight[0], frame_tokens)
    query_term, key_term, value_term = block_terms(
        query_all[0], grad_all[0], lse_all[0], delta_all[0], key_flat, value_flat, key_mask
    )
    query_terms = [query_term]
    keys_part = key_term.reshape(mem_here, frame_tokens, heads, head_size)
    values_part = value_term.reshape(mem_here, frame_tokens, heads, head_size)
    query_sum_terms = jnp.stack(query_terms).reshape(frames_here, rows_all, heads * head_size)
    grad_queries = lax.psum_scatter(query_sum_terms, "mem", scatter_dimension=1, tiled=True).astype(
        jnp.bfloat16
    )
    grad_keys, grad_values = (
        lax.psum_scatter(
            keys_part.reshape(mem_here, frame_tokens, heads * head_size).astype(jnp.bfloat16),
            "query",
            scatter_dimension=1,
            tiled=True,
        ).astype(jnp.float32),
        lax.psum_scatter(
            values_part.reshape(mem_here, frame_tokens, heads * head_size).astype(jnp.bfloat16),
            "query",
            scatter_dimension=1,
            tiled=True,
        ).astype(jnp.float32),
    )
    return (grad_queries, grad_keys.astype(jnp.bfloat16), grad_values.astype(jnp.bfloat16))


def solution(mesh):
    placed = (
        P("query", "mem", None),
        P("query", "mem", None),
        P("query", "mem", None),
        P("query", "mem", None),
        P("mem", None, None),
        P("mem", None, None),
        P(),
        P(),
    )
    return jax.shard_map(
        on_device,
        mesh=mesh,
        in_specs=placed,
        out_specs=(P("query", "mem", None), P("mem", "query", None), P("mem", "query", None)),
        check_vma=False,
    )
```

profile of v0, /device:TPU:6, one launch (start us, length us, event | category | flops | bytes accessed | tf_op | source)
XLA Modules:
  0.0 844.9 jit_solution(4895777326158244927)
XLA Ops:
  7.2 0.0 copy-start.3
  7.2 0.0 all-gather.4.cloned.1.call-start
  7.2 1.4 copy.35
  8.6 0.0 all-gather.4.cloned.1.call-update
  8.6 0.0 all-gather.6.cloned.1.call-start
  8.7 1.4 copy.42
  10.1 0.0 all-gather.6.cloned.1.call-update
  10.1 0.0 all-gather.8.cloned.1.call-start
  10.1 1.4 copy.48
  11.5 0.0 all-gather.8.cloned.1.call-update
  11.5 0.0 reduce-scatter.5.cloned.1.call-start
  11.6 89.5 %all_gather.13 = f32[1,256,20]{2,0,1:T(1,128)S(1)} all-gather(f32[1,4,20]{2,0,1:T(1,128)} %bitcast.43), channel_id=1, replica_groups=mesh['query'=8,'mem'=64] {'mem'}, dimensions={1}, use_global_device_ids=true | all-gather | bytes 20800 | tf_op jit(solution)/shard_map/all_gather | solution.py:50
  101.1 0.1 copy.41
  101.2 1.4 copy.37
  102.6 2.2 copy.44
  104.8 1.3 dynamic-slice
  106.7 0.0 copy-done.3
  106.7 0.6 dynamic_slice.7
  107.3 2.0 and_reduce_fusion
  110.0 0.0 all-gather.4.cloned.1.call-done
  110.0 6.2 copy.36
  116.2 70.5 %all-gather.6.cloned.1.call-done = bf16[1,256,2560]{2,0,1:T(2,128)(2,1)} async-done(((bf16[1,4,2560]{2,0,1:T(2,128)(2,1)}), bf16[1,256,2560]{2,0,1:T(2,128)(2,1)}) %all-gather.6.cloned.1.call-update) | async-done | bytes 1310736 | tf_op jit(solution)/shard_map/all_gather | solution.py:47
  186.7 6.1 copy.43
  192.8 0.0 copy-start
  192.8 2.0 fusion.7
  194.8 0.0 copy-done
  194.8 2.1 convolution_convert_fusion
  196.9 2.2 copy.54
  199.1 0.0 reduce-scatter.5.cloned.1.call-update
  199.1 0.0 reduce-scatter.3.cloned.1.call-start
  199.1 71.9 %all-gather.8.cloned.1.call-done = bf16[1,256,2560]{2,0,1:T(2,128)(2,1)} async-done(((bf16[1,4,2560]{2,0,1:T(2,128)(2,1)}), bf16[1,256,2560]{2,0,1:T(2,128)(2,1)}) %all-gather.8.cloned.1.call-update) | async-done | bytes 1310736 | tf_op jit(solution)/shard_map/all_gather | solution.py:48
  271.1 6.1 copy.49
  277.2 3.5 convert_multiply_fusion
  280.7 1.9 reduce_sum.9
  282.6 0.0 copy-start.1
  282.6 3.4 multiply_convert_fusion
  286.0 0.0 copy-done.1
  286.0 0.0 copy-start.2
  286.0 0.5 fusion.1
  286.5 0.6 copy-done.2
  287.1 1.1 copy.53
  288.2 1.8 multiply_bitcast_fusion
  290.0 2.1 copy.51
  292.1 5.0 copy.52
  297.1 0.0 reduce-scatter.3.cloned.1.call-update
  297.1 539.7 %all-reduce.2 = bf16[1,256,2560]{2,0,1:T(2,128)(2,1)} all-reduce(f32[1,256,2560]{2,0,1:T(1,128)S(1)} %copy.52), channel_id=2, replica_groups=mesh['query'=8,'mem'=64] {'mem'}, use_global_device_ids=true, to_apply=%region_2.3.clone | all-reduce | flops 655360 | bytes 3932160
  836.9 0.8 dynamic-slice_convert_fusion
  837.7 0.6 copy.55
  838.3 0.0 reduce-scatter.5.cloned.1.call-done
  838.3 0.0 reduce-scatter.3.cloned.1.call-done
Async XLA Ops:
  7.2 99.6 %copy-start.3 = (s32[8]{0:T(128)S(1)}, s32[8]{0:T(128)}, u32[]{:S(2)}) copy-start(s32[8]{0:T(128)} %param.15) | copy-start | bytes 100
  7.2 102.8 %all-gather.4.cloned.1.call-start = ((), (), s32[]{:S(2)}) async-start(), calls=%async_computation.2 | async-start | bytes 2662400 | tf_op jit(solution)/shard_map/all_gather | solution.py:46
  8.6 178.1 %all-gather.6.cloned.1.call-start = ((), (), s32[]{:S(2)}) async-start(), calls=%async_computation.3 | async-start | bytes 2662400 | tf_op jit(solution)/shard_map/all_gather | solution.py:47
  10.1 261.0 %all-gather.8.cloned.1.call-start = ((), (), s32[]{:S(2)}) async-start(), calls=%async_computation.4 | async-start | bytes 2662400 | tf_op jit(solution)/shard_map/all_gather | solution.py:48
  11.5 826.8 %reduce-scatter.5.cloned.1.call-start = ((), (), s32[]{:S(2)}) async-start(), calls=%async_computation.6 | async-start | bytes 737280 | tf_op jit(solution)/shard_map/reduce_scatter | solution.py:85
  192.8 2.0 copy-start
  199.1 639.2 %reduce-scatter.3.cloned.1.call-start = ((), (), s32[]{:S(2)}) async-start(), calls=%async_computation.5 | async-start | bytes 737280 | tf_op jit(solution)/shard_map/reduce_scatter | solution.py:79
  282.6 3.4 copy-start.1
  286.0 1.1 copy-start.2
Sparse Core Ops, SparseCore 0:
  11.9 89.6 all-gather.3
  105.5 81.1 all-gather.5
  190.0 80.9 all-gather.7
  274.3 40.4 reduce-scatter.4
  318.1 55.6 reduce-scatter.2
where the time goes:
time: 846 us; the launch traced here: 845 us
  blocking collectives  629 us (74%)
  waiting for transfers between devices  143 us (17%)
  local copies, waits for them, and re-layouts  40.5 us (5%)
  between operations  15.2 us (2%)
  matrix products  9.75 us (1%)
    unnamed x1, blocking collectives  540 us
    all_gather x1, blocking collectives, on_device(): lse_all = lax.all_gather(lse, 'mem', axis=1, tiled=True)  89.5 us
    all_gather x1, waiting for transfers between devices, on_device(): lax.all_gather(attn_out, 'mem', axis=1, tiled=True)  71.9 us
    all_gather x1, waiting for transfers between devices, on_device(): lax.all_gather(grad_out, 'mem', axis=1, tiled=True)  70.5 us
  transfers between devices with their start and end apart: 5, of which 2 were waited for; matrix products, arithmetic and copies ran while one was open for 7% of the time, Pallas kernels for 0%

commit v1 on v0

v1 whole, which is shorter than its diff:
```python
import functools
import math

import jax
import jax.numpy as jnp
from jax import lax
from jax.experimental import pallas as pl
from jax.experimental.pallas import tpu as pltpu
from jax.sharding import Mesh, PartitionSpec as P

HS = 128
GROUPS = 4
LANES = 128
MASKED = -1e30


def split_low(value):
    high = lax.reduce_precision(value, 8, 7)
    return high.astype(jnp.bfloat16), (value - high).astype(jnp.bfloat16)


def attention_kernel(
    place, amounts, ids, rows, kv_own, kv_core, kv_z, kv_both, dq, own_part, far_part, *, heads
):
    bf16, f32 = jnp.bfloat16, jnp.float32
    score_scale = HS ** (-0.5)
    exponent_scale = score_scale * math.log2(math.e)
    width = heads * HS
    low_frame, low_z = place[0], place[1]
    blocks = (kv_own, kv_core, kv_z, kv_both)
    tokens = kv_own.shape[1]

    frame = lax.broadcasted_iota(jnp.int32, ids.shape, 0)
    entry = lax.broadcasted_iota(jnp.int32, ids.shape, 1)
    limit = jnp.zeros(ids.shape, jnp.int32)
    for f in range(ids.shape[0]):
        limit = jnp.where(frame == f, amounts[f], limit)
    listed = entry < limit
    row8 = lax.broadcasted_iota(jnp.int32, (ids.shape[0], LANES), 0) - low_frame
    lane8 = lax.broadcasted_iota(jnp.int32, (ids.shape[0], LANES), 1)
    spot = (lane8 == 4 * heads + row8) & (row8 >= 0) & (row8 < GROUPS)
    biases = []
    for d in range(4):
        hit = jnp.where((ids[...] == place[2 + d]) & listed, 1.0, 0.0)
        found = jnp.max(hit, axis=1, keepdims=True)
        bias = jnp.sum(jnp.where(spot, (1.0 - found) * MASKED, 0.0), axis=0, keepdims=True)
        biases.append(jnp.broadcast_to(bias, (tokens, LANES)))
    bias_all = jnp.concatenate(biases, axis=0)
    lane = lax.broadcasted_iota(jnp.int32, bias_all.shape, 1)
    extra = rows[:, 2 * width :]

    for h in range(heads):
        cols = slice(h * HS, (h + 1) * HS)
        q = rows[:, cols]
        g = rows[:, width + h * HS : width + (h + 1) * HS]
        k = jnp.concatenate([b[0, :, cols] for b in blocks], axis=0)
        v = jnp.concatenate([b[1, :, cols] for b in blocks], axis=0)
        k_pick = jnp.where((lane == h) | (lane == heads + h), -1.0, bias_all).astype(bf16)
        v_pick = jnp.where((lane == 2 * heads + h) | (lane == 3 * heads + h), -1.0, 0.0).astype(bf16)
        contract = (((1,), (1,)), ((), ()))
        scores = lax.dot_general(
            jnp.concatenate([k, k_pick], axis=1),
            jnp.concatenate([q, extra], axis=1),
            contract,
            preferred_element_type=f32,
        )
        probs = jnp.exp2(scores * exponent_scale)
        grad_probs = lax.dot_general(
            jnp.concatenate([v, v_pick], axis=1),
            jnp.concatenate([g, extra], axis=1),
            contract,
            preferred_element_type=f32,
        )
        grad_scores = (probs * grad_probs).astype(bf16)
        dv = jnp.dot(probs.astype(bf16), g, preferred_element_type=f32).astype(bf16)
        dk = (jnp.dot(grad_scores, q, preferred_element_type=f32) * score_scale).astype(bf16)
        dq_h = lax.dot_general(
            grad_scores, k, (((0,), (0,)), ((), ())), preferred_element_type=f32
        )
        dq[:, cols] = (dq_h * score_scale).astype(bf16)
        for d, out in enumerate((own_part, far_part, own_part, far_part)):
            z = low_z if d < 2 else 1 - low_z
            part = slice(d * tokens, (d + 1) * tokens)
            piece = (out.shape[0], out.shape[3], HS)
            out[:, z, 0, :, cols] = dk[part].reshape(piece)
            out[:, z, 1, :, cols] = dv[part].reshape(piece)


def on_device(sizes, queries, grad_out, attn_out, lse, keys, values, frame_ids, counts):
    f32, bf16 = jnp.float32, jnp.bfloat16
    low_y, x = lax.axis_index("yl"), lax.axis_index("x")
    high_z, low_z = lax.axis_index("zh"), lax.axis_index("zl")
    high_y, core = lax.axis_index("yh"), lax.axis_index("c")
    tokens_here, columns = queries.shape[1], queries.shape[2]
    heads = lse.shape[2] // GROUPS
    width = heads * HS
    frame_tokens = keys.shape[1]
    spread = sizes["zh"] * sizes["yh"]
    members = GROUPS * spread
    blocks_q = sizes["yl"] * sizes["x"]

    kv = jnp.stack(
        [lax.dynamic_slice_in_dim(a[0], x * width, width, 1) for a in (keys, values)]
    )
    flip = [(0, 1), (1, 0)]
    both = [(a * 2 + b, (1 - a) * 2 + (1 - b)) for a in range(2) for b in range(2)]
    kv_core = lax.ppermute(kv, "c", flip)
    kv_z = lax.ppermute(kv, "zl", flip)
    kv_both = lax.ppermute(kv, ("zl", "c"), both)

    delta = jnp.sum(
        (grad_out[0].astype(f32) * attn_out[0].astype(f32)).reshape(tokens_here, -1, HS), axis=-1
    )
    lse_high, lse_low = split_low(lse[0] * HS**0.5)
    delta_high, delta_low = split_low(delta)
    by_group = lambda a: a.reshape(tokens_here, GROUPS, -1).transpose(1, 0, 2)
    frame_spot = (jnp.arange(LANES - 4 * heads) == x).astype(bf16)
    packed = jnp.concatenate(
        [
            by_group(queries[0]),
            by_group(grad_out[0]),
            by_group(lse_high),
            by_group(lse_low),
            by_group(delta_high),
            by_group(delta_low),
            jnp.broadcast_to(frame_spot, (GROUPS, tokens_here, LANES - 4 * heads)),
        ],
        axis=2,
    )
    packed = jnp.broadcast_to(
        packed[:, None], (GROUPS, spread, tokens_here, packed.shape[2])
    ).reshape(members, tokens_here, -1)
    rows = lax.all_to_all(packed, ("x", "zh", "yh"), 0, 0, tiled=True)
    rows = rows.reshape(members * tokens_here, -1)

    def memory_frame(z, c):
        return ((high_z * 2 + z) * sizes["yh"] + high_y) * 2 + c

    place = jnp.stack(
        [
            low_y * GROUPS,
            low_z,
            memory_frame(low_z, core),
            memory_frame(low_z, 1 - core),
            memory_frame(1 - low_z, core),
            memory_frame(1 - low_z, 1 - core),
        ]
    ).astype(jnp.int32)
    in_vmem = pl.BlockSpec(memory_space=pltpu.VMEM)
    in_smem = pl.BlockSpec(memory_space=pltpu.SMEM)
    part = jax.ShapeDtypeStruct((blocks_q, 2, 2, frame_tokens // blocks_q, width), bf16)
    dq, own_part, far_part = pl.pallas_call(
        functools.partial(attention_kernel, heads=heads),
        out_shape=(jax.ShapeDtypeStruct((rows.shape[0], width), bf16), part, part),
        in_specs=[in_smem, in_smem] + [in_vmem] * 6,
        out_specs=(in_vmem,) * 3,
        compiler_params=pltpu.CompilerParams(vmem_limit_bytes=40 * 2**20),
        name="attention_grads",
    )(place, counts, frame_ids, rows, kv, kv_core, kv_z, kv_both)

    far_part = lax.ppermute(far_part, "c", flip)

    dq = lax.all_to_all(
        dq.reshape(members, tokens_here, width), ("x", "zh", "yh"), 0, 0, tiled=True
    )
    dq = jnp.sum(dq.reshape(GROUPS, spread, tokens_here, width).astype(f32), axis=1)
    grad_queries = dq.transpose(1, 0, 2).reshape(1, tokens_here, columns).astype(bf16)

    pair = (own_part.astype(f32) + far_part.astype(f32)).astype(bf16)
    pair = pair.reshape(blocks_q * 2, 2, frame_tokens // blocks_q, width)
    pair = lax.all_to_all(pair, ("yl", "x", "zl"), 0, 0, tiled=True)
    pair = pair.reshape(sizes["yl"], GROUPS, 2, 2, frame_tokens // blocks_q, width)
    total = jnp.sum(pair.astype(f32), axis=(0, 2))
    total = total.transpose(1, 2, 0, 3).reshape(2, 1, frame_tokens // blocks_q, columns)
    total = total.astype(bf16)
    return grad_queries, total[0], total[1]


def solution(mesh):
    query, mem = mesh.shape["query"], mesh.shape["mem"]
    sizes = {"yl": query // GROUPS, "x": GROUPS, "zh": mem // 16, "zl": 2, "yh": 4, "c": 2}
    if mem < 16:
        sizes.update(zh=1, yh=mem // 4)
    fine = Mesh(mesh.devices.reshape(tuple(sizes.values())), tuple(sizes))
    q_axes, m_axes = ("yl", "x"), ("zh", "zl", "yh", "c")
    rows = P(q_axes, m_axes, None)
    frames = P(m_axes, None, None)
    return jax.shard_map(
        functools.partial(on_device, sizes),
        mesh=fine,
        in_specs=(rows, rows, rows, rows, frames, frames, P(), P()),
        out_specs=(rows, P(m_axes, q_axes, None), P(m_axes, q_axes, None)),
        check_vma=False,
    )
```

time: 846 us -> 111 us (0.13)
  blocking collectives: 629 us -> 0 us
  waiting for transfers between devices: 143 us -> 46.2 us
  starting transfers between devices: 0.21 us -> 48.9 us
  local copies, waits for them, and re-layouts: 40.5 us -> 7.64 us
  between operations: 15.2 us -> 0.8 us
  matrix products: 9.75 us -> 0 us
    unnamed x1 -> x0, blocking collectives: 540 us -> none
    all_gather x3 -> x0, waiting for transfers between devices: 142 us -> none  [the longest x1 71.9 us: on_device(): lax.all_gather(attn_out, 'mem', axis=1, tiled=True)]
    all_gather x1 -> x0, blocking collectives: 89.5 us -> none  [on_device(): lse_all = lax.all_gather(lse, 'mem', axis=1, tiled=True)]
    all_to_all x0 -> x3, waiting for transfers between devices: none -> 42 us  [the longest x1 16.5 us: on_device(): rows = lax.all_to_all(packed, ('x', 'zh', 'yh'), 0, 0, tiled=True)]
    all_to_all x0 -> x3, starting transfers between devices: none -> 39.3 us  [the longest x1 19.4 us: on_device(): rows = lax.all_to_all(packed, ('x', 'zh', 'yh'), 0, 0, tiled=True)]
    all_gather x3 -> x0, local copies, waits for them, and re-layouts: 18.4 us -> none  [the longest x1 6.17 us: on_device(): lax.all_gather(queries, 'mem', axis=1, tiled=True)]
    unnamed x15 -> x5, local copies, waits for them, and re-layouts: 10.2 us -> 0.02 us
    dot_general x5 -> x0, matrix products: 9.75 us -> none  [the longest x1 3.39 us: block_terms(): jnp.einsum('qhd,khd->hqk', grad_rows, value_rows, preferred_element_type=...]
  transfers between devices with their start and end apart: 5 -> 7, of which waited for: 2 -> 4; matrix products, arithmetic and copies ran while one was open for 7% -> 5% of each run, Pallas kernels for 0% -> 0%
where the time goes in v1:
time: 111 us; the launch traced here: 110 us
  starting transfers between devices  48.9 us (44%)
  waiting for transfers between devices  46.2 us (42%)
  local copies, waits for them, and re-layouts  7.64 us (7%)
  other arithmetic  3.43 us (3%)
  Pallas kernels  3.32 us (3%)
    all_to_all x1, starting transfers between devices, on_device(): rows = lax.all_to_all(packed, ('x', 'zh', 'yh'), 0, 0, tiled=True)  19.4 us
    all_to_all x1, waiting for transfers between devices, on_device(): rows = lax.all_to_all(packed, ('x', 'zh', 'yh'), 0, 0, tiled=True)  16.5 us
    all_to_all x1, waiting for transfers between devices, on_device(): lax.all_to_all(dq.reshape(members, tokens_here, width), ('x', 'zh', 'yh')...  16.2 us
    all_to_all x1, starting transfers between devices, on_device(): lax.all_to_all(dq.reshape(members, tokens_here, width), ('x', 'zh', 'yh')...  14 us
    all_to_all x1, waiting for transfers between devices, on_device(): pair = lax.all_to_all(pair, ('yl', 'x', 'zl'), 0, 0, tiled=True)  9.29 us
    all_to_all x1, starting transfers between devices, on_device(): pair = lax.all_to_all(pair, ('yl', 'x', 'zl'), 0, 0, tiled=True)  5.9 us
    ppermute x1, waiting for transfers between devices, on_device(): kv_z = lax.ppermute(kv, 'zl', flip)  4.16 us
    pallas_call x1, Pallas kernels, on_device(): pl.pallas_call(functools.partial(attention_kernel, heads=heads), out_shap...  3.32 us
  transfers between devices with their start and end apart: 7, of which 4 were waited for; matrix products, arithmetic and copies ran while one was open for 5% of the time, Pallas kernels for 0%

profile of v1, /device:TPU:6, one launch (start us, length us, event | category | flops | bytes accessed | tf_op | source)
XLA Modules:
  0.0 110.2 jit_solution(2579123203513602735)
XLA Ops:
  0.6 0.7 broadcast_multiply_fusion
  1.3 0.1 mul.59
  1.4 0.7 reshape_squeeze.6
  2.2 0.7 reshape_squeeze.7
  2.9 0.8 convert_multiply_fusion
  3.7 0.1 reduce_sum.29
  3.8 0.1 reduce_sum.30
  3.9 0.1 concatenate.3
  4.0 1.1 broadcast_in_dim.10
  5.1 19.4 %all-to-all-start = ((bf16[64,4,1408]{2,1,0:T(4,128)(2,1)}), bf16[64,4,1408]{2,1,0:T(4,128)(2,1)}, u32[]{:S(2)}, u32[]{:S(2)}) async-start(bf16[64,4,1408]{2,1,0:T(4,128)(2,1)} %bitcast.12), calls=%async_computation | async-start | bytes 1441792 | tf_op jit(solution)/shard_map/all_to_all | solution.py:133
  24.6 1.0 constant_dynamic-slice_fusion
  25.6 2.3 %collective-permute-start.2 = (bf16[2,128,640]{2,1,0:T(8,128)(2,1)S(1)}, bf16[2,128,640]{2,1,0:T(8,128)(2,1)S(1)}, u32[]{:S(2)}, u32[]{:S(2)}) collective-permute-start(bf16[2,128,640]{2,1,0:T(8,128)(2,1)S(1)} %pad_maximum_fusion.kv_own), channel_id=1, source_target_pairs={{0,9},{1,8},{8,1},{9,0},{2,11},{3,10},{10,3},{11,2},{4,13},{5,12},... | collective-permute-start | bytes 983048 | tf_op jit(solution)/shard_map/ppermute | solution.py:109
  27.9 3.0 %collective-permute-start.1 = (bf16[2,128,640]{2,1,0:T(8,128)(2,1)S(1)}, bf16[2,128,640]{2,1,0:T(8,128)(2,1)S(1)}, u32[]{:S(2)}, u32[]{:S(2)}) collective-permute-start(bf16[2,128,640]{2,1,0:T(8,128)(2,1)S(1)} %pad_maximum_fusion.kv_own), channel_id=1, source_target_pairs={{0,8},{8,0},{1,9},{9,1},{2,10},{10,2},{3,11},{11,3},{4,12},{12,4},... | collective-permute-start | bytes 983048 | tf_op jit(solution)/shard_map/ppermute | solution.py:108
  31.0 2.3 %collective-permute-start = (bf16[2,128,640]{2,1,0:T(8,128)(2,1)S(1)}, bf16[2,128,640]{2,1,0:T(8,128)(2,1)S(1)}, u32[]{:S(2)}, u32[]{:S(2)}) collective-permute-start(bf16[2,128,640]{2,1,0:T(8,128)(2,1)S(1)} %pad_maximum_fusion.kv_own), channel_id=1, source_target_pairs={{0,1},{1,0},{2,3},{3,2},{4,5},{5,4},{6,7},{7,6},{8,9},{9,8},{10,11... | collective-permute-start | bytes 983048 | tf_op jit(solution)/shard_map/ppermute | solution.py:107
  33.3 0.1 stack.32.place
  33.4 0.0 copy-start
  33.4 0.0 copy-start.1
  33.4 16.5 %all-to-all-done = bf16[64,4,1408]{2,1,0:T(4,128)(2,1)} async-done(((bf16[64,4,1408]{2,1,0:T(4,128)(2,1)}), bf16[64,4,1408]{2,1,0:T(4,128)(2,1)}, u32[]{:S(2)}, u32[]{:S(2)}) %all-to-all-start) | async-done | bytes 720928 | tf_op jit(solution)/shard_map/all_to_all | solution.py:133
  49.9 1.5 %reshape.78.rows = bf16[256,1408]{1,0:T(8,128)(2,1)S(1)} reshape(bf16[64,4,1408]{2,1,0:T(4,128)(2,1)} %all-to-all-done) | data formatting | bytes 1441792 | tf_op jit(solution)/shard_map/reshape | solution.py:134
  51.4 0.0 collective-permute-done.2.kv_both
  51.4 4.2 %collective-permute-done.1.kv_z = bf16[2,128,640]{2,1,0:T(8,128)(2,1)S(1)} collective-permute-done((bf16[2,128,640]{2,1,0:T(8,128)(2,1)S(1)}, bf16[2,128,640]{2,1,0:T(8,128)(2,1)S(1)}, u32[]{:S(2)}, u32[]{:S(2)}) %collective-permute-start.1) | collective-permute-done | bytes 327712 | tf_op jit(solution)/shard_map/ppermute | solution.py:108
  55.6 0.0 collective-permute-done.kv_core
  55.6 0.0 copy-done
  55.6 0.0 copy-done.1
  55.6 3.3 %attention_grads.1 = (bf16[256,640]{1,0:T(8,128)(2,1)S(1)}, bf16[8,2,2,16,640]{4,3,2,1,0:T(8,128)(2,1)S(1)}, bf16[8,2,2,16,640]{4,3,2,1,0:T(8,128)(2,1)}) custom-call(s32[6]{0:T(128)S(1)} %stack.32.place, s32[8]{0:T(128)S(1)} %copy-done.1, s32[8,64]{1,0:T(8,128)S(1)} %copy-done, bf16[256,1408]{1,0:T(8,128)(2,1)S(1)} %reshape.78.rows, ...), custom_call_target="tpu_custom_call" | custom-call | tf_op jit(solution)/shard_map/attention_grads/pallas_call | solution.py:152
  58.9 2.0 %collective-permute-start.3 = (bf16[8,2,2,16,640]{4,3,2,1,0:T(8,128)(2,1)}, bf16[8,2,2,16,640]{4,3,2,1,0:T(8,128)(2,1)S(1)}, u32[]{:S(2)}, u32[]{:S(2)}) collective-permute-start(bf16[8,2,2,16,640]{4,3,2,1,0:T(8,128)(2,1)} %get-tuple-element.8), channel_id=1, source_target_pairs={{0,1},{1,0},{2,3},{3,2},{4,5},{5,4},{6,7},{7,6},{8,9},{9,8},{10,11... | collective-permute-start | bytes 1966088 | tf_op jit(solution)/shard_map/ppermute | solution.py:161
  60.9 0.8 reshape.79
  61.7 14.0 %all-to-all-start.1 = ((bf16[64,4,640]{2,1,0:T(4,128)(2,1)}), bf16[64,4,640]{2,1,0:T(4,128)(2,1)S(1)}, u32[]{:S(2)}, u32[]{:S(2)}) async-start(bf16[64,4,640]{2,1,0:T(4,128)(2,1)} %reshape.79), calls=%async_computation.1 | async-start | bytes 655360 | tf_op jit(solution)/shard_map/all_to_all | solution.py:163
  75.7 0.0 collective-permute-done.3
  75.7 1.0 add_convert_fusion
  76.7 16.2 %all-to-all-done.1 = bf16[64,4,640]{2,1,0:T(4,128)(2,1)S(1)} async-done(((bf16[64,4,640]{2,1,0:T(4,128)(2,1)}), bf16[64,4,640]{2,1,0:T(4,128)(2,1)S(1)}, u32[]{:S(2)}, u32[]{:S(2)}) %all-to-all-start.1) | async-done | bytes 327712 | tf_op jit(solution)/shard_map/all_to_all | solution.py:163
  92.9 5.9 %all-to-all-start.2 = ((bf16[16,2,16,640]{3,2,1,0:T(8,128)(2,1)}), bf16[16,2,16,640]{3,2,1,0:T(8,128)(2,1)S(1)}, u32[]{:S(2)}, u32[]{:S(2)}) async-start(bf16[16,2,16,640]{3,2,1,0:T(8,128)(2,1)} %bitcast.16), calls=%async_computation.2 | async-start | bytes 1310720 | tf_op jit(solution)/shard_map/all_to_all | solution.py:171
  98.8 0.7 bitcast_reduce_fusion
  99.5 9.3 %all-to-all-done.2 = bf16[16,2,16,640]{3,2,1,0:T(8,128)(2,1)S(1)} async-done(((bf16[16,2,16,640]{3,2,1,0:T(8,128)(2,1)}), bf16[16,2,16,640]{3,2,1,0:T(8,128)(2,1)S(1)}, u32[]{:S(2)}, u32[]{:S(2)}) %all-to-all-start.2) | async-done | bytes 655392 | tf_op jit(solution)/shard_map/all_to_all | solution.py:171
  108.8 0.1 reduce.1
  109.0 0.6 copy.18
  109.6 0.6 copy.17
  (7 shorter events, 0.1 us)
Async XLA Ops:
  5.1 44.7 %all-to-all-start = ((bf16[64,4,1408]{2,1,0:T(4,128)(2,1)}), bf16[64,4,1408]{2,1,0:T(4,128)(2,1)}, u32[]{:S(2)}, u32[]{:S(2)}) async-start(bf16[64,4,1408]{2,1,0:T(4,128)(2,1)} %bitcast.12), calls=%async_computation | async-start | bytes 1441792 | tf_op jit(solution)/shard_map/all_to_all | solution.py:133
  25.6 25.8 %collective-permute-start.2 = (bf16[2,128,640]{2,1,0:T(8,128)(2,1)S(1)}, bf16[2,128,640]{2,1,0:T(8,128)(2,1)S(1)}, u32[]{:S(2)}, u32[]{:S(2)}) collective-permute-start(bf16[2,128,640]{2,1,0:T(8,128)(2,1)S(1)} %pad_maximum_fusion.kv_own), channel_id=1, source_target_pairs={{0,9},{1,8},{8,1},{9,0},{2,11},{3,10},{10,3},{11,2},{4,13},{5,12},... | collective-permute-start | bytes 983048 | tf_op jit(solution)/shard_map/ppermute | solution.py:109
  27.9 27.7 %collective-permute-start.1 = (bf16[2,128,640]{2,1,0:T(8,128)(2,1)S(1)}, bf16[2,128,640]{2,1,0:T(8,128)(2,1)S(1)}, u32[]{:S(2)}, u32[]{:S(2)}) collective-permute-start(bf16[2,128,640]{2,1,0:T(8,128)(2,1)S(1)} %pad_maximum_fusion.kv_own), channel_id=1, source_target_pairs={{0,8},{8,0},{1,9},{9,1},{2,10},{10,2},{3,11},{11,3},{4,12},{12,4},... | collective-permute-start | bytes 983048 | tf_op jit(solution)/shard_map/ppermute | solution.py:108
  31.0 24.6 %collective-permute-start = (bf16[2,128,640]{2,1,0:T(8,128)(2,1)S(1)}, bf16[2,128,640]{2,1,0:T(8,128)(2,1)S(1)}, u32[]{:S(2)}, u32[]{:S(2)}) collective-permute-start(bf16[2,128,640]{2,1,0:T(8,128)(2,1)S(1)} %pad_maximum_fusion.kv_own), channel_id=1, source_target_pairs={{0,1},{1,0},{2,3},{3,2},{4,5},{5,4},{6,7},{7,6},{8,9},{9,8},{10,11... | collective-permute-start | bytes 983048 | tf_op jit(solution)/shard_map/ppermute | solution.py:107
  33.4 22.2 %copy-start = (s32[8,64]{1,0:T(8,128)S(1)}, s32[8,64]{1,0:T(8,128)}, u32[]{:S(2)}) copy-start(s32[8,64]{1,0:T(8,128)} %ids.1) | copy-start | bytes 6148
  33.4 22.2 %copy-start.1 = (s32[8]{0:T(128)S(1)}, s32[8]{0:T(128)}, u32[]{:S(2)}) copy-start(s32[8]{0:T(128)} %amounts.1) | copy-start | bytes 100
  58.9 16.8 %collective-permute-start.3 = (bf16[8,2,2,16,640]{4,3,2,1,0:T(8,128)(2,1)}, bf16[8,2,2,16,640]{4,3,2,1,0:T(8,128)(2,1)S(1)}, u32[]{:S(2)}, u32[]{:S(2)}) collective-permute-start(bf16[8,2,2,16,640]{4,3,2,1,0:T(8,128)(2,1)} %get-tuple-element.8), channel_id=1, source_target_pairs={{0,1},{1,0},{2,3},{3,2},{4,5},{5,4},{6,7},{7,6},{8,9},{9,8},{10,11... | collective-permute-start | bytes 1966088 | tf_op jit(solution)/shard_map/ppermute | solution.py:161
  61.7 31.2 %all-to-all-start.1 = ((bf16[64,4,640]{2,1,0:T(4,128)(2,1)}), bf16[64,4,640]{2,1,0:T(4,128)(2,1)S(1)}, u32[]{:S(2)}, u32[]{:S(2)}) async-start(bf16[64,4,640]{2,1,0:T(4,128)(2,1)} %reshape.79), calls=%async_computation.1 | async-start | bytes 655360 | tf_op jit(solution)/shard_map/all_to_all | solution.py:163
  92.9 15.9 %all-to-all-start.2 = ((bf16[16,2,16,640]{3,2,1,0:T(8,128)(2,1)}), bf16[16,2,16,640]{3,2,1,0:T(8,128)(2,1)S(1)}, u32[]{:S(2)}, u32[]{:S(2)}) async-start(bf16[16,2,16,640]{3,2,1,0:T(8,128)(2,1)} %bitcast.16), calls=%async_computation.2 | async-start | bytes 1310720 | tf_op jit(solution)/shard_map/all_to_all | solution.py:171

commit v2 on v1

v2 whole, which is shorter than its diff:
```python
import functools
import math

import jax
import jax.numpy as jnp
from jax import lax
from jax.experimental import pallas as pl
from jax.experimental.pallas import tpu as pltpu
from jax.sharding import Mesh, PartitionSpec as P

HS = 128
GROUPS = 4
LANES = 128
MASKED = -1e30
F32, BF16 = jnp.float32, jnp.bfloat16
IN_VMEM = pl.BlockSpec(memory_space=pltpu.VMEM)
IN_SMEM = pl.BlockSpec(memory_space=pltpu.SMEM)


def call(body, name, out_shape, in_specs, *args):
    return pl.pallas_call(
        body,
        out_shape=out_shape,
        in_specs=in_specs,
        out_specs=jax.tree.map(lambda _: IN_VMEM, out_shape),
        compiler_params=pltpu.CompilerParams(vmem_limit_bytes=40 * 2**20),
        name=name,
    )(*args)


def pack_rows(place, queries, grad_out, attn_out, lse, out, *, heads):
    width = heads * HS
    tokens = queries.shape[1]
    lane = lax.broadcasted_iota(jnp.int32, (tokens, LANES), 1)
    lse_scaled = lse[0] * HS**0.5
    for group in range(GROUPS):
        extra = jnp.where(lane == 4 * heads + place[0], 1.0, 0.0).astype(F32)
        for h in range(heads):
            head = group * heads + h
            cols = slice(head * HS, (head + 1) * HS)
            product = grad_out[0, :, cols].astype(F32) * attn_out[0, :, cols].astype(F32)
            delta = jnp.sum(product, axis=1, keepdims=True)
            for i, value in enumerate((lse_scaled[:, head : head + 1], delta)):
                high = value.astype(BF16).astype(F32)
                extra = jnp.where(lane == 2 * i * heads + h, high, extra)
                extra = jnp.where(lane == (2 * i + 1) * heads + h, value - high, extra)
        cols = slice(group * width, (group + 1) * width)
        row = jnp.concatenate(
            [queries[0, :, cols], grad_out[0, :, cols], extra.astype(BF16)], axis=1
        )
        for s in range(out.shape[0] // GROUPS):
            out[s * GROUPS + group] = row


def attention_grads(
    place, amounts, ids, rows, kv_own, kv_core, kv_z, kv_both, dq, near, far, *, heads
):
    score_scale = HS ** (-0.5)
    exponent_scale = score_scale * math.log2(math.e)
    width = heads * HS
    blocks = (kv_own, kv_core, kv_z, kv_both)
    tokens = kv_own.shape[1]

    frame = lax.broadcasted_iota(jnp.int32, ids.shape, 0)
    entry = lax.broadcasted_iota(jnp.int32, ids.shape, 1)
    limit = jnp.zeros(ids.shape, jnp.int32)
    for f in range(ids.shape[0]):
        limit = jnp.where(frame == f, amounts[f], limit)
    listed = entry < limit
    row8 = lax.broadcasted_iota(jnp.int32, (ids.shape[0], LANES), 0) - place[1] * GROUPS
    lane8 = lax.broadcasted_iota(jnp.int32, (ids.shape[0], LANES), 1)
    spot = (lane8 == 4 * heads + row8) & (row8 >= 0) & (row8 < GROUPS)
    biases = []
    for d in range(4):
        hit = jnp.where((ids[...] == place[2 + d]) & listed, 1.0, 0.0)
        found = jnp.max(hit, axis=1, keepdims=True)
        bias = jnp.sum(jnp.where(spot, (1.0 - found) * MASKED, 0.0), axis=0, keepdims=True)
        biases.append(jnp.broadcast_to(bias, (tokens, LANES)))
    bias_all = jnp.concatenate(biases, axis=0)
    lane = lax.broadcasted_iota(jnp.int32, bias_all.shape, 1)
    extra = rows[:, 2 * width :]

    for h in range(heads):
        cols = slice(h * HS, (h + 1) * HS)
        q = rows[:, cols]
        g = rows[:, width + h * HS : width + (h + 1) * HS]
        k = jnp.concatenate([b[0, :, cols] for b in blocks], axis=0)
        v = jnp.concatenate([b[1, :, cols] for b in blocks], axis=0)
        k_pick = jnp.where((lane == h) | (lane == heads + h), -1.0, bias_all).astype(BF16)
        v_pick = jnp.where((lane == 2 * heads + h) | (lane == 3 * heads + h), -1.0, 0.0).astype(BF16)
        contract = (((1,), (1,)), ((), ()))
        scores = lax.dot_general(
            jnp.concatenate([k, k_pick], axis=1),
            jnp.concatenate([q, extra], axis=1),
            contract,
            preferred_element_type=F32,
        )
        probs = jnp.exp2(scores * exponent_scale)
        grad_probs = lax.dot_general(
            jnp.concatenate([v, v_pick], axis=1),
            jnp.concatenate([g, extra], axis=1),
            contract,
            preferred_element_type=F32,
        )
        grad_scores = (probs * grad_probs).astype(BF16)
        dv = jnp.dot(probs.astype(BF16), g, preferred_element_type=F32).astype(BF16)
        dk = (jnp.dot(grad_scores, q, preferred_element_type=F32) * score_scale).astype(BF16)
        dq_h = lax.dot_general(
            grad_scores, k, (((0,), (0,)), ((), ())), preferred_element_type=F32
        )
        dq[:, cols] = (dq_h * score_scale).astype(BF16)
        for d, out in enumerate((near, far, near, far)):
            part = slice(d * tokens, (d + 1) * tokens)
            piece = (out.shape[1], out.shape[3], HS)
            out[d // 2, :, 0, :, cols] = dk[part].reshape(piece)
            out[d // 2, :, 1, :, cols] = dv[part].reshape(piece)


def pack_terms(dq, near, from_core, from_z, out):
    share = near.shape[3]
    dq_sum = dq[0].astype(F32)
    for s in range(1, dq.shape[0]):
        dq_sum = dq_sum + dq[s].astype(F32)
    tokens = dq.shape[1] // GROUPS
    for b in range(out.shape[0]):
        for kind in range(2):
            total = near[0, b, kind].astype(F32) + from_core[0, b, kind].astype(F32)
            total = total + from_z[b, kind].astype(F32)
            out[b, kind * share : (kind + 1) * share] = total.astype(BF16)
        x = b % GROUPS
        piece = dq_sum[x * tokens : (x + 1) * tokens]
        rest = jnp.zeros((out.shape[1] - 2 * share - tokens, piece.shape[1]), F32)
        out[b, 2 * share :] = jnp.concatenate([piece, rest], axis=0).astype(BF16)


def unpack_terms(place, terms, grad_queries, grad_keys, grad_values):
    share, tokens = grad_keys.shape[1], grad_queries.shape[1]
    width = terms.shape[2]
    for x in range(GROUPS):
        cols = slice(x * width, (x + 1) * width)
        for kind, out in enumerate((grad_keys, grad_values)):
            part = slice(kind * share, (kind + 1) * share)
            total = terms[x, part].astype(F32)
            for y in range(1, terms.shape[0] // GROUPS):
                total = total + terms[y * GROUPS + x, part].astype(F32)
            out[0, :, cols] = total.astype(BF16)
        mine = terms[place[1] * GROUPS + x, 2 * share :].astype(F32)
        grad_queries[0, :, cols] = mine[:tokens].astype(BF16)


def on_device(sizes, queries, grad_out, attn_out, lse, keys, values, frame_ids, counts):
    low_y, x = lax.axis_index("yl"), lax.axis_index("x")
    high_z, low_z = lax.axis_index("zh"), lax.axis_index("zl")
    high_y, core = lax.axis_index("yh"), lax.axis_index("c")
    tokens_here = queries.shape[1]
    heads = lse.shape[2] // GROUPS
    width = heads * HS
    frame_tokens = keys.shape[1]
    spread = sizes["zh"] * sizes["yh"]
    members = GROUPS * spread
    blocks_q = sizes["yl"] * sizes["x"]
    share = frame_tokens // blocks_q

    def memory_frame(z, c):
        return ((high_z * 2 + z) * sizes["yh"] + high_y) * 2 + c

    place = jnp.stack(
        [
            x,
            low_y,
            memory_frame(low_z, core),
            memory_frame(low_z, 1 - core),
            memory_frame(1 - low_z, core),
            memory_frame(1 - low_z, 1 - core),
        ]
    ).astype(jnp.int32)

    packed = call(
        functools.partial(pack_rows, heads=heads),
        "pack_rows",
        jax.ShapeDtypeStruct((members, tokens_here, 2 * width + LANES), BF16),
        [IN_SMEM] + [IN_VMEM] * 4,
        place,
        queries,
        grad_out,
        attn_out,
        lse,
    )
    rows = lax.all_to_all(packed, ("zh", "yh", "x"), 0, 0, tiled=True)
    rows = rows.reshape(members * tokens_here, -1)

    kv = jnp.stack(
        [lax.dynamic_slice_in_dim(a[0], x * width, width, 1) for a in (keys, values)]
    )
    flip = [(0, 1), (1, 0)]
    kv_z = lax.ppermute(kv, "zl", flip)
    kv_core = lax.ppermute(kv, "c", flip)
    kv_both = lax.ppermute(kv_z, "c", flip)

    part = jax.ShapeDtypeStruct((2, blocks_q, 2, share, width), BF16)
    dq, near, far = call(
        functools.partial(attention_grads, heads=heads),
        "attention_grads",
        (jax.ShapeDtypeStruct((rows.shape[0], width), BF16), part, part),
        [IN_SMEM] * 2 + [IN_VMEM] * 6,
        place,
        counts,
        frame_ids,
        rows,
        kv,
        kv_core,
        kv_z,
        kv_both,
    )

    from_core = lax.ppermute(far, "c", flip)
    dq = lax.all_to_all(
        dq.reshape(spread, GROUPS * tokens_here, width), ("zh", "yh"), 0, 0, tiled=True
    )
    other_z = (near[1].astype(F32) + from_core[1].astype(F32)).astype(BF16)
    from_z = lax.ppermute(other_z, "zl", flip)
    terms = call(
        pack_terms,
        "pack_terms",
        jax.ShapeDtypeStruct((blocks_q, 2 * share + 2 * tokens_here, width), BF16),
        [IN_VMEM] * 4,
        dq,
        near,
        from_core,
        from_z,
    )
    terms = lax.all_to_all(terms, ("yl", "x"), 0, 0, tiled=True)
    return call(
        unpack_terms,
        "unpack_terms",
        (
            jax.ShapeDtypeStruct(queries.shape, BF16),
            jax.ShapeDtypeStruct((1, share, keys.shape[2]), BF16),
            jax.ShapeDtypeStruct((1, share, keys.shape[2]), BF16),
        ),
        [IN_SMEM, IN_VMEM],
        place,
        terms,
    )


def solution(mesh):
    query, mem = mesh.shape["query"], mesh.shape["mem"]
    sizes = {"yl": query // GROUPS, "x": GROUPS, "zh": mem // 16, "zl": 2, "yh": 4, "c": 2}
    if mem < 16:
        sizes.update(zh=1, yh=mem // 4)
    fine = Mesh(mesh.devices.reshape(tuple(sizes.values())), tuple(sizes))
    q_axes, m_axes = ("yl", "x"), ("zh", "zl", "yh", "c")
    rows = P(q_axes, m_axes, None)
    frames = P(m_axes, None, None)
    return jax.shard_map(
        functools.partial(on_device, sizes),
        mesh=fine,
        in_specs=(rows, rows, rows, rows, frames, frames, P(), P()),
        out_specs=(rows, P(m_axes, q_axes, None), P(m_axes, q_axes, None)),
        check_vma=False,
    )
```

time: 111 us -> 97.8 us (0.88)
  waiting for transfers between devices: 46.2 us -> 33.2 us
  blocking collectives: 0 us -> 11.3 us
  starting transfers between devices: 48.9 us -> 42.5 us
  local copies, waits for them, and re-layouts: 7.64 us -> 1.94 us
  other arithmetic: 3.43 us -> 0.12 us
  Pallas kernels: 3.32 us -> 6.4 us
    all_to_all x3 -> x2, waiting for transfers between devices: 42 us -> 12.8 us  [the longest x1 12.8 us: on_device(): lax.all_to_all(dq.reshape(spread, GROUPS * tokens_here, width), ('zh', 'y...]
    ppermute x1, waiting for transfers between devices: 4.16 us -> 17.5 us  [on_device(): kv_z = lax.ppermute(kv, 'zl', flip)]
    all_to_all x0 -> x1, blocking collectives: none -> 11.3 us  [on_device(): terms = lax.all_to_all(terms, ('yl', 'x'), 0, 0, tiled=True)]
    all_to_all x3 -> x2, starting transfers between devices: 39.3 us -> 30.3 us  [the longest x1 19.1 us: on_device(): rows = lax.all_to_all(packed, ('zh', 'yh', 'x'), 0, 0, tiled=True)]
    pallas_call x1 -> x4, Pallas kernels: 3.32 us -> 6.4 us  [call(): pl.pallas_call(body, out_shape=out_shape, in_specs=in_specs, out_specs=ja...]
    ppermute x2 -> x3, waiting for transfers between devices: 0.01 us -> 2.91 us  [the longest x1 1.51 us: on_device(): from_z = lax.ppermute(other_z, 'zl', flip)]
    ppermute x2 -> x3, starting transfers between devices: 4.27 us -> 6.9 us  [the longest x1 2.96 us: on_device(): from_z = lax.ppermute(other_z, 'zl', flip)]
    another operation x3 -> x1, local copies, waits for them, and re-layouts: 1.57 us -> 0.08 us  [on_device(): jnp.stack([x, low_y, memory_frame(low_z, core), memory_frame(low_z, 1 - c...]
  transfers between devices with their start and end apart: 7 -> 7, of which waited for: 4 -> 4; matrix products, arithmetic and copies ran while one was open for 5% -> 1% of each run, Pallas kernels for 0% -> 0%
where the time goes in v2:
time: 97.8 us; the launch traced here: 96.3 us
  starting transfers between devices  42.5 us (43%)
  waiting for transfers between devices  33.2 us (34%)
  blocking collectives  11.3 us (12%)
  Pallas kernels  6.4 us (7%)
  local copies, waits for them, and re-layouts  1.94 us (2%)
    all_to_all x1, starting transfers between devices, on_device(): rows = lax.all_to_all(packed, ('zh', 'yh', 'x'), 0, 0, tiled=True)  19.1 us
    ppermute x1, waiting for transfers between devices, on_device(): kv_z = lax.ppermute(kv, 'zl', flip)  17.5 us
    all_to_all x1, waiting for transfers between devices, on_device(): lax.all_to_all(dq.reshape(spread, GROUPS * tokens_here, width), ('zh', 'y...  12.8 us
    all_to_all x1, blocking collectives, on_device(): terms = lax.all_to_all(terms, ('yl', 'x'), 0, 0, tiled=True)  11.3 us
    all_to_all x1, starting transfers between devices, on_device(): lax.all_to_all(dq.reshape(spread, GROUPS * tokens_here, width), ('zh', 'y...  11.3 us
    pallas_call x4, Pallas kernels, call(): pl.pallas_call(body, out_shape=out_shape, in_specs=in_specs, out_specs=ja...  6.4 us
    ppermute x1, starting transfers between devices, on_device(): kv_z = lax.ppermute(kv, 'zl', flip)  3.38 us
    ppermute x1, starting transfers between devices, on_device(): from_z = lax.ppermute(other_z, 'zl', flip)  2.96 us
  transfers between devices with their start and end apart: 7, of which 4 were waited for; matrix products, arithmetic and copies ran while one was open for 1% of the time, Pallas kernels for 0%

profile of v2, /device:TPU:6, one launch (start us, length us, event | category | flops | bytes accessed | tf_op | source)
XLA Modules:
  0.0 96.3 jit_solution(17095392991387239533)
XLA Ops:
  0.6 0.0 copy-start.4
  0.6 0.0 copy-start.2
  0.7 0.0 copy-start.1
  0.7 0.0 copy-start
  0.7 0.1 stack.32.place
  0.8 0.5 copy-done.4
  1.3 0.1 copy-done.2
  1.4 0.0 copy-done.1
  1.4 0.0 copy-done
  1.4 1.7 %pack_rows.1 = bf16[64,4,1408]{2,1,0:T(4,128)(2,1)} custom-call(s32[6]{0:T(128)S(1)} %stack.32.place, bf16[1,4,2560]{2,1,0:T(4,128)(2,1)S(1)} %copy-done, bf16[1,4,2560]{2,1,0:T(4,128)(2,1)S(1)} %copy-done.1, bf16[1,4,2560]{2,1,0:T(4,128)(2,1)S(1)} %copy-done.2, f32[1,4,20]{2,1,0:T(4,128)S(1)} %copy-done.4), custom_call_target="tpu_custom_call" | custom-call | tf_op jit(solution)/shard_map/pack_rows/pallas_call | solution.py:21
  3.1 19.1 %all-to-all-start = ((bf16[64,4,1408]{2,1,0:T(4,128)(2,1)}), bf16[64,4,1408]{2,1,0:T(4,128)(2,1)S(1)}, u32[]{:S(2)}, u32[]{:S(2)}) async-start(bf16[64,4,1408]{2,1,0:T(4,128)(2,1)} %pack_rows.1), calls=%async_computation | async-start | bytes 1441792 | tf_op jit(solution)/shard_map/all_to_all | solution.py:189
  22.2 1.0 %constant_dynamic-slice_fusion = (bf16[1,128,640]{2,1,0:T(8,128)(2,1)S(1)}, bf16[1,128,640]{2,1,0:T(8,128)(2,1)S(1)}) fusion(bf16[1,128,2560]{2,1,0:T(8,128)(2,1)} %param.13, s32[]{:T(128)S(6)} %select_n.4, bf16[1,128,2560]{2,1,0:T(8,128)(2,1)} %param.12), kind=kLoop, calls=%fused_computation.3 | loop fusion | bytes 655364 | tf_op jit(solution)/shard_map/dynamic_slice | solution.py:193
  23.3 0.0 copy-start.3
  23.3 0.0 copy-start.5
  23.3 3.4 %collective-permute-start.1 = (bf16[2,128,640]{2,1,0:T(8,128)(2,1)S(1)}, bf16[2,128,640]{2,1,0:T(8,128)(2,1)S(1)}, u32[]{:S(2)}, u32[]{:S(2)}) collective-permute-start(bf16[2,128,640]{2,1,0:T(8,128)(2,1)S(1)} %pad_maximum_fusion.kv_own), channel_id=1, source_target_pairs={{0,8},{8,0},{1,9},{9,1},{2,10},{10,2},{3,11},{11,3},{4,12},{12,4},... | collective-permute-start | bytes 983048 | tf_op jit(solution)/shard_map/ppermute | solution.py:196
  26.7 1.9 %collective-permute-start = (bf16[2,128,640]{2,1,0:T(8,128)(2,1)S(1)}, bf16[2,128,640]{2,1,0:T(8,128)(2,1)S(1)}, u32[]{:S(2)}, u32[]{:S(2)}) collective-permute-start(bf16[2,128,640]{2,1,0:T(8,128)(2,1)S(1)} %pad_maximum_fusion.kv_own), channel_id=1, source_target_pairs={{0,1},{1,0},{2,3},{3,2},{4,5},{5,4},{6,7},{7,6},{8,9},{9,8},{10,11... | collective-permute-start | bytes 983048 | tf_op jit(solution)/shard_map/ppermute | solution.py:197
  28.6 17.5 %collective-permute-done.1.kv_z = bf16[2,128,640]{2,1,0:T(8,128)(2,1)S(1)} collective-permute-done((bf16[2,128,640]{2,1,0:T(8,128)(2,1)S(1)}, bf16[2,128,640]{2,1,0:T(8,128)(2,1)S(1)}, u32[]{:S(2)}, u32[]{:S(2)}) %collective-permute-start.1) | collective-permute-done | bytes 327712 | tf_op jit(solution)/shard_map/ppermute | solution.py:196
  46.1 1.9 %collective-permute-start.2 = (bf16[2,128,640]{2,1,0:T(8,128)(2,1)S(1)}, bf16[2,128,640]{2,1,0:T(8,128)(2,1)S(1)}, u32[]{:S(2)}, u32[]{:S(2)}) collective-permute-start(bf16[2,128,640]{2,1,0:T(8,128)(2,1)S(1)} %collective-permute-done.1.kv_z), channel_id=1, source_target_pairs={{0,1},{1,0},{2,3},{3,2},{4,5},{5,4},{6,7},{7,6},{8,9},{9,8},{10,11... | collective-permute-start | bytes 983048 | tf_op jit(solution)/shard_map/ppermute | solution.py:198
  48.0 0.0 all-to-all-done
  48.0 0.2 reshape.20.rows
  48.2 0.0 collective-permute-done.kv_core
  48.2 1.4 %collective-permute-done.2.kv_both = bf16[2,128,640]{2,1,0:T(8,128)(2,1)S(1)} collective-permute-done((bf16[2,128,640]{2,1,0:T(8,128)(2,1)S(1)}, bf16[2,128,640]{2,1,0:T(8,128)(2,1)S(1)}, u32[]{:S(2)}, u32[]{:S(2)}) %collective-permute-start.2) | collective-permute-done | bytes 327712 | tf_op jit(solution)/shard_map/ppermute | solution.py:198
  49.6 0.0 copy-done.3
  49.6 0.0 copy-done.5
  49.6 3.3 %attention_grads.1 = (bf16[256,640]{1,0:T(8,128)(2,1)}, bf16[2,8,2,16,640]{4,3,2,1,0:T(8,128)(2,1)S(1)}, bf16[2,8,2,16,640]{4,3,2,1,0:T(8,128)(2,1)S(1)}) custom-call(s32[6]{0:T(128)S(1)} %stack.32.place, s32[8]{0:T(128)S(1)} %copy-done.5, s32[8,64]{1,0:T(8,128)S(1)} %copy-done.3, bf16[256,1408]{1,0:T(8,128)(2,1)S(1)} %reshape.20.rows, ...), custom_call_target="tpu_custom_call" | custom-call | tf_op jit(solution)/shard_map/attention_grads/pallas_call | solution.py:21
  52.9 2.0 %collective-permute-start.3 = (bf16[2,8,2,16,640]{4,3,2,1,0:T(8,128)(2,1)S(1)}, bf16[2,8,2,16,640]{4,3,2,1,0:T(8,128)(2,1)S(1)}, u32[]{:S(2)}, u32[]{:S(2)}) collective-permute-start(bf16[2,8,2,16,640]{4,3,2,1,0:T(8,128)(2,1)S(1)} %get-tuple-element.8), channel_id=1, source_target_pairs={{0,1},{1,0},{2,3},{3,2},{4,5},{5,4},{6,7},{7,6},{8,9},{9,8},{10,11... | collective-permute-start | bytes 1966088 | tf_op jit(solution)/shard_map/ppermute | solution.py:216
  55.0 11.3 %all-to-all-start.1 = ((bf16[16,16,640]{2,1,0:T(8,128)(2,1)}), bf16[16,16,640]{2,1,0:T(8,128)(2,1)S(1)}, u32[]{:S(2)}, u32[]{:S(2)}) async-start(bf16[16,16,640]{2,1,0:T(8,128)(2,1)} %bitcast.6), calls=%async_computation.1 | async-start | bytes 655360 | tf_op jit(solution)/shard_map/all_to_all | solution.py:217
  66.2 0.0 collective-permute-done.3.from_core
  66.2 0.1 fusion
  66.3 3.0 %collective-permute-start.4 = (bf16[8,2,16,640]{3,2,1,0:T(8,128)(2,1)S(1)}, bf16[8,2,16,640]{3,2,1,0:T(8,128)(2,1)S(1)}, u32[]{:S(2)}, u32[]{:S(2)}) collective-permute-start(bf16[8,2,16,640]{3,2,1,0:T(8,128)(2,1)S(1)} %fusion), channel_id=1, source_target_pairs={{0,8},{8,0},{1,9},{9,1},{2,10},{10,2},{3,11},{11,3},{4,12},{12,4},... | collective-permute-start | bytes 983048 | tf_op jit(solution)/shard_map/ppermute | solution.py:221
  69.3 12.8 %all-to-all-done.1.dq = bf16[16,16,640]{2,1,0:T(8,128)(2,1)S(1)} async-done(((bf16[16,16,640]{2,1,0:T(8,128)(2,1)}), bf16[16,16,640]{2,1,0:T(8,128)(2,1)S(1)}, u32[]{:S(2)}, u32[]{:S(2)}) %all-to-all-start.1) | async-done | bytes 327712 | tf_op jit(solution)/shard_map/all_to_all | solution.py:217
  82.1 1.5 %collective-permute-done.4.from_z = bf16[8,2,16,640]{3,2,1,0:T(8,128)(2,1)S(1)} collective-permute-done((bf16[8,2,16,640]{3,2,1,0:T(8,128)(2,1)S(1)}, bf16[8,2,16,640]{3,2,1,0:T(8,128)(2,1)S(1)}, u32[]{:S(2)}, u32[]{:S(2)}) %collective-permute-start.4) | collective-permute-done | bytes 327712 | tf_op jit(solution)/shard_map/ppermute | solution.py:221
  83.6 0.2 pack_terms.1
  83.7 11.3 %all_to_all.15.terms = bf16[8,40,640]{2,1,0:T(8,128)(2,1)S(1)} all-to-all(bf16[8,40,640]{2,1,0:T(8,128)(2,1)S(1)} %pack_terms.1), channel_id=1, replica_groups=mesh['yl'=2,'x'=4,'zh'=4,'zl'=2,'yh'=4,'c'=2] {'yl','x'}, dimensions={0} | all-to-all | bytes 819200 | tf_op jit(solution)/shard_map/all_to_all | solution.py:232
  95.0 1.2 %unpack_terms.1 = (bf16[1,4,2560]{2,1,0:T(4,128)(2,1)}, bf16[1,16,2560]{2,1,0:T(8,128)(2,1)}, bf16[1,16,2560]{2,1,0:T(8,128)(2,1)}) custom-call(s32[6]{0:T(128)S(1)} %stack.32.place, bf16[8,40,640]{2,1,0:T(8,128)(2,1)S(1)} %all_to_all.15.terms), custom_call_target="tpu_custom_call" | custom-call | tf_op jit(solution)/shard_map/unpack_terms/pallas_call | solution.py:21
  (1 shorter events, 0.0 us)
Async XLA Ops:
  0.6 0.7 copy-start.4
  0.6 0.7 copy-start.2
  0.7 0.7 copy-start.1
  0.7 0.7 copy-start
  3.1 44.9 %all-to-all-start = ((bf16[64,4,1408]{2,1,0:T(4,128)(2,1)}), bf16[64,4,1408]{2,1,0:T(4,128)(2,1)S(1)}, u32[]{:S(2)}, u32[]{:S(2)}) async-start(bf16[64,4,1408]{2,1,0:T(4,128)(2,1)} %pack_rows.1), calls=%async_computation | async-start | bytes 1441792 | tf_op jit(solution)/shard_map/all_to_all | solution.py:189
  23.3 26.3 %copy-start.3 = (s32[8,64]{1,0:T(8,128)S(1)}, s32[8,64]{1,0:T(8,128)}, u32[]{:S(2)}) copy-start(s32[8,64]{1,0:T(8,128)} %ids.1) | copy-start | bytes 6148
  23.3 26.3 %copy-start.5 = (s32[8]{0:T(128)S(1)}, s32[8]{0:T(128)}, u32[]{:S(2)}) copy-start(s32[8]{0:T(128)} %amounts.1) | copy-start | bytes 100
  23.3 22.8 %collective-permute-start.1 = (bf16[2,128,640]{2,1,0:T(8,128)(2,1)S(1)}, bf16[2,128,640]{2,1,0:T(8,128)(2,1)S(1)}, u32[]{:S(2)}, u32[]{:S(2)}) collective-permute-start(bf16[2,128,640]{2,1,0:T(8,128)(2,1)S(1)} %pad_maximum_fusion.kv_own), channel_id=1, source_target_pairs={{0,8},{8,0},{1,9},{9,1},{2,10},{10,2},{3,11},{11,3},{4,12},{12,4},... | collective-permute-start | bytes 983048 | tf_op jit(solution)/shard_map/ppermute | solution.py:196
  26.7 21.5 %collective-permute-start = (bf16[2,128,640]{2,1,0:T(8,128)(2,1)S(1)}, bf16[2,128,640]{2,1,0:T(8,128)(2,1)S(1)}, u32[]{:S(2)}, u32[]{:S(2)}) collective-permute-start(bf16[2,128,640]{2,1,0:T(8,128)(2,1)S(1)} %pad_maximum_fusion.kv_own), channel_id=1, source_target_pairs={{0,1},{1,0},{2,3},{3,2},{4,5},{5,4},{6,7},{7,6},{8,9},{9,8},{10,11... | collective-permute-start | bytes 983048 | tf_op jit(solution)/shard_map/ppermute | solution.py:197
  46.1 3.5 %collective-permute-start.2 = (bf16[2,128,640]{2,1,0:T(8,128)(2,1)S(1)}, bf16[2,128,640]{2,1,0:T(8,128)(2,1)S(1)}, u32[]{:S(2)}, u32[]{:S(2)}) collective-permute-start(bf16[2,128,640]{2,1,0:T(8,128)(2,1)S(1)} %collective-permute-done.1.kv_z), channel_id=1, source_target_pairs={{0,1},{1,0},{2,3},{3,2},{4,5},{5,4},{6,7},{7,6},{8,9},{9,8},{10,11... | collective-permute-start | bytes 983048 | tf_op jit(solution)/shard_map/ppermute | solution.py:198
  52.9 13.3 %collective-permute-start.3 = (bf16[2,8,2,16,640]{4,3,2,1,0:T(8,128)(2,1)S(1)}, bf16[2,8,2,16,640]{4,3,2,1,0:T(8,128)(2,1)S(1)}, u32[]{:S(2)}, u32[]{:S(2)}) collective-permute-start(bf16[2,8,2,16,640]{4,3,2,1,0:T(8,128)(2,1)S(1)} %get-tuple-element.8), channel_id=1, source_target_pairs={{0,1},{1,0},{2,3},{3,2},{4,5},{5,4},{6,7},{7,6},{8,9},{9,8},{10,11... | collective-permute-start | bytes 1966088 | tf_op jit(solution)/shard_map/ppermute | solution.py:216
  55.0 27.1 %all-to-all-start.1 = ((bf16[16,16,640]{2,1,0:T(8,128)(2,1)}), bf16[16,16,640]{2,1,0:T(8,128)(2,1)S(1)}, u32[]{:S(2)}, u32[]{:S(2)}) async-start(bf16[16,16,640]{2,1,0:T(8,128)(2,1)} %bitcast.6), calls=%async_computation.1 | async-start | bytes 655360 | tf_op jit(solution)/shard_map/all_to_all | solution.py:217
  66.3 17.2 %collective-permute-start.4 = (bf16[8,2,16,640]{3,2,1,0:T(8,128)(2,1)S(1)}, bf16[8,2,16,640]{3,2,1,0:T(8,128)(2,1)S(1)}, u32[]{:S(2)}, u32[]{:S(2)}) collective-permute-start(bf16[8,2,16,640]{3,2,1,0:T(8,128)(2,1)S(1)} %fusion), channel_id=1, source_target_pairs={{0,8},{8,0},{1,9},{9,1},{2,10},{10,2},{3,11},{11,3},{4,12},{12,4},... | collective-permute-start | bytes 983048 | tf_op jit(solution)/shard_map/ppermute | solution.py:221

commit v3 on v2

--- a/solution.py
+++ b/solution.py
@@ -15,21 +15,36 @@
 F32, BF16 = jnp.float32, jnp.bfloat16
 IN_VMEM = pl.BlockSpec(memory_space=pltpu.VMEM)
 IN_SMEM = pl.BlockSpec(memory_space=pltpu.SMEM)
-
-
-def call(body, name, out_shape, in_specs, *args):
+IN_PLACE = pl.BlockSpec(memory_space=pl.ANY)
+
+
+LONG = pl.CostEstimate(flops=10**11, bytes_accessed=10**6, transcendentals=0)
+
+
+def call(body, name, out_shape, in_specs, *args, cost=None, scratch=(), vmem=40):
     return pl.pallas_call(
         body,
         out_shape=out_shape,
         in_specs=in_specs,
+        scratch_shapes=scratch,
+        cost_estimate=cost,
         out_specs=jax.tree.map(lambda _: IN_VMEM, out_shape),
-        compiler_params=pltpu.CompilerParams(vmem_limit_bytes=40 * 2**20),
+        compiler_params=pltpu.CompilerParams(vmem_limit_bytes=vmem * 2**20),
         name=name,
     )(*args)
 
 
-def pack_rows(place, queries, grad_out, attn_out, lse, out, *, heads):
+def pack_rows(
+    place, queries, grad_out, attn_out, lse, keys, values, out, kv, key_copied, value_copied, *, heads
+):
     width = heads * HS
+    here = pl.ds(pl.multiple_of(place[0] * width, LANES), width)
+    copies = [
+        pltpu.make_async_copy(keys.at[0, :, here], kv.at[0], key_copied),
+        pltpu.make_async_copy(values.at[0, :, here], kv.at[1], value_copied),
+    ]
+    for copy in copies:
+        copy.start()
     tokens = queries.shape[1]
     lane = lax.broadcasted_iota(jnp.int32, (tokens, LANES), 1)
     lse_scaled = lse[0] * HS**0.5
@@ -50,16 +65,23 @@
         )
         for s in range(out.shape[0] // GROUPS):
             out[s * GROUPS + group] = row
+    for copy in copies:
+        copy.wait()
+
+
+def pair_frames(kv_own, kv_z, out):
+    out[0] = kv_own[...]
+    out[1] = kv_z[...]
 
 
 def attention_grads(
-    place, amounts, ids, rows, kv_own, kv_core, kv_z, kv_both, dq, near, far, *, heads
+    place, amounts, ids, rows, kv_own, kv_core, dq, near, far, *, heads
 ):
     score_scale = HS ** (-0.5)
     exponent_scale = score_scale * math.log2(math.e)
     width = heads * HS
-    blocks = (kv_own, kv_core, kv_z, kv_both)
-    tokens = kv_own.shape[1]
+    blocks = (kv_own.at[0], kv_core.at[0], kv_own.at[1], kv_core.at[1])
+    tokens = kv_own.shape[2]
 
     frame = lax.broadcasted_iota(jnp.int32, ids.shape, 0)
     entry = lax.broadcasted_iota(jnp.int32, ids.shape, 1)
@@ -116,17 +138,24 @@
             out[d // 2, :, 1, :, cols] = dv[part].reshape(piece)
 
 
-def pack_terms(dq, near, from_core, from_z, out):
-    share = near.shape[3]
+def add_core(near, from_core, out):
+    out[...] = (near[1].astype(F32) + from_core[1].astype(F32)).astype(BF16)
+
+
+def add_z(near, from_core, from_z, out):
+    total = near[0].astype(F32) + from_core[0].astype(F32)
+    out[...] = (total + from_z[...].astype(F32)).astype(BF16)
+
+
+def pack_terms(dq, part, out):
+    share = part.shape[2]
     dq_sum = dq[0].astype(F32)
     for s in range(1, dq.shape[0]):
         dq_sum = dq_sum + dq[s].astype(F32)
     tokens = dq.shape[1] // GROUPS
     for b in range(out.shape[0]):
         for kind in range(2):
-            total = near[0, b, kind].astype(F32) + from_core[0, b, kind].astype(F32)
-            total = total + from_z[b, kind].astype(F32)
-            out[b, kind * share : (kind + 1) * share] = total.astype(BF16)
+            out[b, kind * share : (kind + 1) * share] = part[b, kind]
         x = b % GROUPS
         piece = dq_sum[x * tokens : (x + 1) * tokens]
         rest = jnp.zeros((out.shape[1] - 2 * share - tokens, piece.shape[1]), F32)
@@ -175,59 +204,71 @@
         ]
     ).astype(jnp.int32)
 
-    packed = call(
+    flip = [(0, 1), (1, 0)]
+    packed, kv = call(
         functools.partial(pack_rows, heads=heads),
         "pack_rows",
-        jax.ShapeDtypeStruct((members, tokens_here, 2 * width + LANES), BF16),
-        [IN_SMEM] + [IN_VMEM] * 4,
+        (
+            jax.ShapeDtypeStruct((members, tokens_here, 2 * width + LANES), BF16),
+            jax.ShapeDtypeStruct((2, frame_tokens, width), BF16),
+        ),
+        [IN_SMEM] + [IN_VMEM] * 4 + [IN_PLACE] * 2,
         place,
         queries,
         grad_out,
         attn_out,
         lse,
+        keys,
+        values,
+        scratch=[pltpu.SemaphoreType.DMA] * 2,
+        vmem=60,
     )
     rows = lax.all_to_all(packed, ("zh", "yh", "x"), 0, 0, tiled=True)
     rows = rows.reshape(members * tokens_here, -1)
 
-    kv = jnp.stack(
-        [lax.dynamic_slice_in_dim(a[0], x * width, width, 1) for a in (keys, values)]
-    )
-    flip = [(0, 1), (1, 0)]
     kv_z = lax.ppermute(kv, "zl", flip)
-    kv_core = lax.ppermute(kv, "c", flip)
-    kv_both = lax.ppermute(kv_z, "c", flip)
+    kv_own = call(
+        pair_frames,
+        "pair_frames",
+        jax.ShapeDtypeStruct((2,) + kv.shape, BF16),
+        [IN_VMEM] * 2,
+        kv,
+        kv_z,
+        cost=LONG,
+    )
+    kv_core = lax.ppermute(kv_own, "c", flip)
 
     part = jax.ShapeDtypeStruct((2, blocks_q, 2, share, width), BF16)
+    half = jax.ShapeDtypeStruct(part.shape[1:], BF16)
     dq, near, far = call(
         functools.partial(attention_grads, heads=heads),
         "attention_grads",
         (jax.ShapeDtypeStruct((rows.shape[0], width), BF16), part, part),
-        [IN_SMEM] * 2 + [IN_VMEM] * 6,
+        [IN_SMEM] * 2 + [IN_VMEM] * 4,
         place,
         counts,
         frame_ids,
         rows,
-        kv,
+        kv_own,
         kv_core,
-        kv_z,
-        kv_both,
     )
 
     from_core = lax.ppermute(far, "c", flip)
+    other_z = call(add_core, "add_core", half, [IN_VMEM] * 2, near, from_core)
+    from_z = lax.ppermute(other_z, "zl", flip)
+    mine = call(
+        add_z, "add_z", half, [IN_VMEM] * 3, near, from_core, from_z, cost=LONG
+    )
     dq = lax.all_to_all(
         dq.reshape(spread, GROUPS * tokens_here, width), ("zh", "yh"), 0, 0, tiled=True
     )
-    other_z = (near[1].astype(F32) + from_core[1].astype(F32)).astype(BF16)
-    from_z = lax.ppermute(other_z, "zl", flip)
     terms = call(
         pack_terms,
         "pack_terms",
         jax.ShapeDtypeStruct((blocks_q, 2 * share + 2 * tokens_here, width), BF16),
-        [IN_VMEM] * 4,
+        [IN_VMEM] * 2,
         dq,
-        near,
-        from_core,
-        from_z,
+        mine,
     )
     terms = lax.all_to_all(terms, ("yl", "x"), 0, 0, tiled=True)
     return call(

time: 97.8 us -> 95.2 us (0.973)
  starting transfers between devices: 42.5 us -> 34.1 us
  waiting for transfers between devices: 33.2 us -> 39.4 us
  Pallas kernels: 6.4 us -> 7.66 us
  local copies, waits for them, and re-layouts: 1.94 us -> 0.78 us
    all_to_all x1, waiting for transfers between devices: 0.01 us -> 22.8 us  [on_device(): rows = lax.all_to_all(packed, ('zh', 'yh', 'x'), 0, 0, tiled=True)]
    ppermute x1, waiting for transfers between devices: 17.5 us -> 0.01 us  [on_device(): kv_z = lax.ppermute(kv, 'zl', flip)]
    all_to_all x1, starting transfers between devices: 11.3 us -> 5.54 us  [on_device(): lax.all_to_all(dq.reshape(spread, GROUPS * tokens_here, width), ('zh', 'y...]
    ppermute x1, waiting for transfers between devices: 1.51 us -> 5.08 us  [on_device(): from_z = lax.ppermute(other_z, 'zl', flip)]
    all_to_all x1, waiting for transfers between devices: 12.8 us -> 9.47 us  [on_device(): lax.all_to_all(dq.reshape(spread, GROUPS * tokens_here, width), ('zh', 'y...]
    ppermute x1, waiting for transfers between devices: 0.01 us -> 2.06 us  [on_device(): from_core = lax.ppermute(far, 'c', flip)]
    ppermute x2 -> x1, starting transfers between devices: 3.83 us -> 1.92 us  [on_device(): kv_core = lax.ppermute(kv_own, 'c', flip)]
    ppermute x2 -> x1, waiting for transfers between devices: 1.41 us -> 0.01 us  [on_device(): kv_core = lax.ppermute(kv_own, 'c', flip)]
  transfers between devices with their start and end apart: 7 -> 6, of which waited for: 4 -> 4; matrix products, arithmetic and copies ran while one was open for 1% -> 0% of each run, Pallas kernels for 0% -> 0%
where the time goes in v3:
time: 95.2 us; the launch traced here: 93.4 us
  waiting for transfers between devices  39.4 us (41%)
  starting transfers between devices  34.1 us (36%)
  blocking collectives  10.7 us (11%)
  Pallas kernels  7.66 us (8%)
    all_to_all x1, waiting for transfers between devices, on_device(): rows = lax.all_to_all(packed, ('zh', 'yh', 'x'), 0, 0, tiled=True)  22.8 us
    all_to_all x1, starting transfers between devices, on_device(): rows = lax.all_to_all(packed, ('zh', 'yh', 'x'), 0, 0, tiled=True)  18.3 us
    all_to_all x1, blocking collectives, on_device(): terms = lax.all_to_all(terms, ('yl', 'x'), 0, 0, tiled=True)  10.7 us
    all_to_all x1, waiting for transfers between devices, on_device(): lax.all_to_all(dq.reshape(spread, GROUPS * tokens_here, width), ('zh', 'y...  9.47 us
    pallas_call x7, Pallas kernels, call(): pl.pallas_call(body, out_shape=out_shape, in_specs=in_specs, scratch_shap...  7.66 us
    all_to_all x1, starting transfers between devices, on_device(): lax.all_to_all(dq.reshape(spread, GROUPS * tokens_here, width), ('zh', 'y...  5.54 us
    ppermute x1, waiting for transfers between devices, on_device(): from_z = lax.ppermute(other_z, 'zl', flip)  5.08 us
    ppermute x1, starting transfers between devices, on_device(): kv_z = lax.ppermute(kv, 'zl', flip)  4.28 us
  transfers between devices with their start and end apart: 6, of which 4 were waited for; matrix products, arithmetic and copies ran while one was open for 0% of the time, Pallas kernels for 0%

profile of v3, /device:TPU:6, one launch (start us, length us, event | category | flops | bytes accessed | tf_op | source)
XLA Modules:
  0.0 93.4 jit_solution(16732790633259902715)
XLA Ops:
  0.6 0.6 stack.27.place
  1.2 2.8 %pack_rows.1 = (bf16[64,4,1408]{2,1,0:T(4,128)(2,1)}, bf16[2,128,640]{2,1,0:T(8,128)(2,1)}) custom-call(s32[6]{0:T(128)} %stack.27.place, bf16[1,4,2560]{2,1,0:T(4,128)(2,1)} %queries.1, bf16[1,4,2560]{2,1,0:T(4,128)(2,1)} %grad_out.1, bf16[1,4,2560]{2,1,0:T(4,128)(2,1)} %attn_out.1, f32[1,4,20]{2,1,0:T(4,128)} %lse.1, bf16[1,128,2560]{2,1,0:T(8,128)(2,1)} %keys.1, ...), custom_call_target="tpu_custom_call" | custom-call | tf_op jit(solution)/shard_map/pack_rows/pallas_call | solution.py:25
  4.1 4.3 %collective-permute-start = (bf16[2,128,640]{2,1,0:T(8,128)(2,1)}, bf16[2,128,640]{2,1,0:T(8,128)(2,1)S(1)}, u32[]{:S(2)}, u32[]{:S(2)}) collective-permute-start(bf16[2,128,640]{2,1,0:T(8,128)(2,1)} %get-tuple-element.9.kv_own), channel_id=1, source_target_pairs={{0,8},{8,0},{1,9},{9,1},{2,10},{10,2},{3,11},{11,3},{4,12},{12,4},... | collective-permute-start | bytes 983048 | tf_op jit(solution)/shard_map/ppermute | solution.py:229
  8.3 0.0 copy-start.3
  8.4 18.3 %all-to-all-start = ((bf16[64,4,1408]{2,1,0:T(4,128)(2,1)}), bf16[64,4,1408]{2,1,0:T(4,128)(2,1)S(1)}, u32[]{:S(2)}, u32[]{:S(2)}) async-start(bf16[64,4,1408]{2,1,0:T(4,128)(2,1)} %get-tuple-element.8), calls=%async_computation | async-start | bytes 1441792 | tf_op jit(solution)/shard_map/all_to_all | solution.py:226
  26.7 0.0 collective-permute-done.kv_z
  26.7 0.0 copy-done.3
  26.7 0.1 pair_frames.1.kv_own
  26.7 0.0 copy-start
  26.8 0.0 copy-start.1
  26.8 0.0 copy-start.2
  26.8 1.9 %collective-permute-start.1 = (bf16[2,2,128,640]{3,2,1,0:T(8,128)(2,1)S(1)}, bf16[2,2,128,640]{3,2,1,0:T(8,128)(2,1)S(1)}, u32[]{:S(2)}, u32[]{:S(2)}) collective-permute-start(bf16[2,2,128,640]{3,2,1,0:T(8,128)(2,1)S(1)} %pair_frames.1.kv_own), channel_id=1, source_target_pairs={{0,1},{1,0},{2,3},{3,2},{4,5},{5,4},{6,7},{7,6},{8,9},{9,8},{10,11... | collective-permute-start | bytes 1966088 | tf_op jit(solution)/shard_map/ppermute | solution.py:239
  28.7 22.8 %all-to-all-done = bf16[64,4,1408]{2,1,0:T(4,128)(2,1)S(1)} async-done(((bf16[64,4,1408]{2,1,0:T(4,128)(2,1)}), bf16[64,4,1408]{2,1,0:T(4,128)(2,1)S(1)}, u32[]{:S(2)}, u32[]{:S(2)}) %all-to-all-start) | async-done | bytes 720928 | tf_op jit(solution)/shard_map/all_to_all | solution.py:226
  51.5 0.2 reshape.12.rows
  51.7 0.0 collective-permute-done.1.kv_core
  51.7 0.0 copy-done
  51.7 0.0 copy-done.1
  51.7 0.0 copy-done.2
  51.7 3.3 %attention_grads.1 = (bf16[256,640]{1,0:T(8,128)(2,1)}, bf16[2,8,2,16,640]{4,3,2,1,0:T(8,128)(2,1)S(1)}, bf16[2,8,2,16,640]{4,3,2,1,0:T(8,128)(2,1)S(1)}) custom-call(s32[6]{0:T(128)S(1)} %copy-done, s32[8]{0:T(128)S(1)} %copy-done.2, s32[8,64]{1,0:T(8,128)S(1)} %copy-done.1, bf16[256,1408]{1,0:T(8,128)(2,1)S(1)} %reshape.12.rows, ...), custom_call_target="tpu_custom_call" | custom-call | tf_op jit(solution)/shard_map/attention_grads/pallas_call | solution.py:25
  55.0 1.9 %collective-permute-start.2 = (bf16[2,8,2,16,640]{4,3,2,1,0:T(8,128)(2,1)S(1)}, bf16[2,8,2,16,640]{4,3,2,1,0:T(8,128)(2,1)S(1)}, u32[]{:S(2)}, u32[]{:S(2)}) collective-permute-start(bf16[2,8,2,16,640]{4,3,2,1,0:T(8,128)(2,1)S(1)} %get-tuple-element.12), channel_id=1, source_target_pairs={{0,1},{1,0},{2,3},{3,2},{4,5},{5,4},{6,7},{7,6},{8,9},{9,8},{10,11... | collective-permute-start | bytes 1966088 | tf_op jit(solution)/shard_map/ppermute | solution.py:256
  56.9 2.1 %collective-permute-done.2.from_core = bf16[2,8,2,16,640]{4,3,2,1,0:T(8,128)(2,1)S(1)} collective-permute-done((bf16[2,8,2,16,640]{4,3,2,1,0:T(8,128)(2,1)S(1)}, bf16[2,8,2,16,640]{4,3,2,1,0:T(8,128)(2,1)S(1)}, u32[]{:S(2)}, u32[]{:S(2)}) %collective-permute-start.2) | collective-permute-done | bytes 655392 | tf_op jit(solution)/shard_map/ppermute | solution.py:256
  59.0 0.1 add_core.1
  59.1 2.1 %collective-permute-start.3 = (bf16[8,2,16,640]{3,2,1,0:T(8,128)(2,1)S(1)}, bf16[8,2,16,640]{3,2,1,0:T(8,128)(2,1)S(1)}, u32[]{:S(2)}, u32[]{:S(2)}) collective-permute-start(bf16[8,2,16,640]{3,2,1,0:T(8,128)(2,1)S(1)} %add_core.1), channel_id=1, source_target_pairs={{0,8},{8,0},{1,9},{9,1},{2,10},{10,2},{3,11},{11,3},{4,12},{12,4},... | collective-permute-start | bytes 983048 | tf_op jit(solution)/shard_map/ppermute | solution.py:258
  61.2 5.5 %all-to-all-start.1 = ((bf16[16,16,640]{2,1,0:T(8,128)(2,1)}), bf16[16,16,640]{2,1,0:T(8,128)(2,1)S(1)}, u32[]{:S(2)}, u32[]{:S(2)}) async-start(bf16[16,16,640]{2,1,0:T(8,128)(2,1)} %bitcast.6), calls=%async_computation.1 | async-start | bytes 655360 | tf_op jit(solution)/shard_map/all_to_all | solution.py:262
  66.7 5.1 %collective-permute-done.3.from_z = bf16[8,2,16,640]{3,2,1,0:T(8,128)(2,1)S(1)} collective-permute-done((bf16[8,2,16,640]{3,2,1,0:T(8,128)(2,1)S(1)}, bf16[8,2,16,640]{3,2,1,0:T(8,128)(2,1)S(1)}, u32[]{:S(2)}, u32[]{:S(2)}) %collective-permute-start.3) | collective-permute-done | bytes 327712 | tf_op jit(solution)/shard_map/ppermute | solution.py:258
  71.8 0.1 add_z.1.part
  71.9 9.5 %all-to-all-done.1.dq = bf16[16,16,640]{2,1,0:T(8,128)(2,1)S(1)} async-done(((bf16[16,16,640]{2,1,0:T(8,128)(2,1)}), bf16[16,16,640]{2,1,0:T(8,128)(2,1)S(1)}, u32[]{:S(2)}, u32[]{:S(2)}) %all-to-all-start.1) | async-done | bytes 327712 | tf_op jit(solution)/shard_map/all_to_all | solution.py:262
  81.4 0.1 pack_terms.1
  81.5 10.7 %all_to_all.15.terms = bf16[8,40,640]{2,1,0:T(8,128)(2,1)S(1)} all-to-all(bf16[8,40,640]{2,1,0:T(8,128)(2,1)S(1)} %pack_terms.1), channel_id=1, replica_groups=mesh['yl'=2,'x'=4,'zh'=4,'zl'=2,'yh'=4,'c'=2] {'yl','x'}, dimensions={0} | all-to-all | bytes 819200 | tf_op jit(solution)/shard_map/all_to_all | solution.py:273
  92.2 1.2 %unpack_terms.1 = (bf16[1,4,2560]{2,1,0:T(4,128)(2,1)}, bf16[1,16,2560]{2,1,0:T(8,128)(2,1)}, bf16[1,16,2560]{2,1,0:T(8,128)(2,1)}) custom-call(s32[6]{0:T(128)S(1)} %copy-done, bf16[8,40,640]{2,1,0:T(8,128)(2,1)S(1)} %all_to_all.15.terms), custom_call_target="tpu_custom_call" | custom-call | tf_op jit(solution)/shard_map/unpack_terms/pallas_call | solution.py:25
Async XLA Ops:
  4.1 22.6 %collective-permute-start = (bf16[2,128,640]{2,1,0:T(8,128)(2,1)}, bf16[2,128,640]{2,1,0:T(8,128)(2,1)S(1)}, u32[]{:S(2)}, u32[]{:S(2)}) collective-permute-start(bf16[2,128,640]{2,1,0:T(8,128)(2,1)} %get-tuple-element.9.kv_own), channel_id=1, source_target_pairs={{0,8},{8,0},{1,9},{9,1},{2,10},{10,2},{3,11},{11,3},{4,12},{12,4},... | collective-permute-start | bytes 983048 | tf_op jit(solution)/shard_map/ppermute | solution.py:229
  8.3 18.3 %copy-start.3 = (bf16[2,128,640]{2,1,0:T(8,128)(2,1)S(1)}, bf16[2,128,640]{2,1,0:T(8,128)(2,1)}, u32[]{:S(2)}) copy-start(bf16[2,128,640]{2,1,0:T(8,128)(2,1)} %get-tuple-element.9.kv_own) | copy-start | bytes 983044
  8.4 43.1 %all-to-all-start = ((bf16[64,4,1408]{2,1,0:T(4,128)(2,1)}), bf16[64,4,1408]{2,1,0:T(4,128)(2,1)S(1)}, u32[]{:S(2)}, u32[]{:S(2)}) async-start(bf16[64,4,1408]{2,1,0:T(4,128)(2,1)} %get-tuple-element.8), calls=%async_computation | async-start | bytes 1441792 | tf_op jit(solution)/shard_map/all_to_all | solution.py:226
  26.7 24.9 %copy-start = (s32[6]{0:T(128)S(1)}, s32[6]{0:T(128)}, u32[]{:S(2)}) copy-start(s32[6]{0:T(128)} %stack.27.place) | copy-start | bytes 76
  26.8 24.9 %copy-start.1 = (s32[8,64]{1,0:T(8,128)S(1)}, s32[8,64]{1,0:T(8,128)}, u32[]{:S(2)}) copy-start(s32[8,64]{1,0:T(8,128)} %ids.1) | copy-start | bytes 6148
  26.8 24.9 %copy-start.2 = (s32[8]{0:T(128)S(1)}, s32[8]{0:T(128)}, u32[]{:S(2)}) copy-start(s32[8]{0:T(128)} %amounts.1) | copy-start | bytes 100
  26.8 24.9 %collective-permute-start.1 = (bf16[2,2,128,640]{3,2,1,0:T(8,128)(2,1)S(1)}, bf16[2,2,128,640]{3,2,1,0:T(8,128)(2,1)S(1)}, u32[]{:S(2)}, u32[]{:S(2)}) collective-permute-start(bf16[2,2,128,640]{3,2,1,0:T(8,128)(2,1)S(1)} %pair_frames.1.kv_own), channel_id=1, source_target_pairs={{0,1},{1,0},{2,3},{3,2},{4,5},{5,4},{6,7},{7,6},{8,9},{9,8},{10,11... | collective-permute-start | bytes 1966088 | tf_op jit(solution)/shard_map/ppermute | solution.py:239
  55.0 4.0 %collective-permute-start.2 = (bf16[2,8,2,16,640]{4,3,2,1,0:T(8,128)(2,1)S(1)}, bf16[2,8,2,16,640]{4,3,2,1,0:T(8,128)(2,1)S(1)}, u32[]{:S(2)}, u32[]{:S(2)}) collective-permute-start(bf16[2,8,2,16,640]{4,3,2,1,0:T(8,128)(2,1)S(1)} %get-tuple-element.12), channel_id=1, source_target_pairs={{0,1},{1,0},{2,3},{3,2},{4,5},{5,4},{6,7},{7,6},{8,9},{9,8},{10,11... | collective-permute-start | bytes 1966088 | tf_op jit(solution)/shard_map/ppermute | solution.py:256
  59.1 12.7 %collective-permute-start.3 = (bf16[8,2,16,640]{3,2,1,0:T(8,128)(2,1)S(1)}, bf16[8,2,16,640]{3,2,1,0:T(8,128)(2,1)S(1)}, u32[]{:S(2)}, u32[]{:S(2)}) collective-permute-start(bf16[8,2,16,640]{3,2,1,0:T(8,128)(2,1)S(1)} %add_core.1), channel_id=1, source_target_pairs={{0,8},{8,0},{1,9},{9,1},{2,10},{10,2},{3,11},{11,3},{4,12},{12,4},... | collective-permute-start | bytes 983048 | tf_op jit(solution)/shard_map/ppermute | solution.py:258
  61.2 20.2 %all-to-all-start.1 = ((bf16[16,16,640]{2,1,0:T(8,128)(2,1)}), bf16[16,16,640]{2,1,0:T(8,128)(2,1)S(1)}, u32[]{:S(2)}, u32[]{:S(2)}) async-start(bf16[16,16,640]{2,1,0:T(8,128)(2,1)} %bitcast.6), calls=%async_computation.1 | async-start | bytes 655360 | tf_op jit(solution)/shard_map/all_to_all | solution.py:262

commit v4 on v2

--- a/solution.py
+++ b/solution.py
@@ -53,13 +53,13 @@
 
 
 def attention_grads(
-    place, amounts, ids, rows, kv_own, kv_core, kv_z, kv_both, dq, near, far, *, heads
+    place, amounts, ids, rows, kv, dq, near, far, *, heads
 ):
     score_scale = HS ** (-0.5)
     exponent_scale = score_scale * math.log2(math.e)
     width = heads * HS
-    blocks = (kv_own, kv_core, kv_z, kv_both)
-    tokens = kv_own.shape[1]
+    blocks = [kv.at[place[7 + d]] for d in range(4)]
+    tokens = kv.shape[2]
 
     frame = lax.broadcasted_iota(jnp.int32, ids.shape, 0)
     entry = lax.broadcasted_iota(jnp.int32, ids.shape, 1)
@@ -72,7 +72,7 @@
     spot = (lane8 == 4 * heads + row8) & (row8 >= 0) & (row8 < GROUPS)
     biases = []
     for d in range(4):
-        hit = jnp.where((ids[...] == place[2 + d]) & listed, 1.0, 0.0)
+        hit = jnp.where((ids[...] == place[3 + d]) & listed, 1.0, 0.0)
         found = jnp.max(hit, axis=1, keepdims=True)
         bias = jnp.sum(jnp.where(spot, (1.0 - found) * MASKED, 0.0), axis=0, keepdims=True)
         biases.append(jnp.broadcast_to(bias, (tokens, LANES)))
@@ -111,26 +111,29 @@
         dq[:, cols] = (dq_h * score_scale).astype(BF16)
         for d, out in enumerate((near, far, near, far)):
             part = slice(d * tokens, (d + 1) * tokens)
-            piece = (out.shape[1], out.shape[3], HS)
-            out[d // 2, :, 0, :, cols] = dk[part].reshape(piece)
-            out[d // 2, :, 1, :, cols] = dv[part].reshape(piece)
-
-
-def pack_terms(dq, near, from_core, from_z, out):
+            z = place[2] if d < 2 else 1 - place[2]
+            piece = (out.shape[0], out.shape[3], HS)
+            out[:, z, 0, :, cols] = dk[part].reshape(piece)
+            out[:, z, 1, :, cols] = dv[part].reshape(piece)
+
+
+def pack_terms(dq, near, from_core, out):
     share = near.shape[3]
     dq_sum = dq[0].astype(F32)
     for s in range(1, dq.shape[0]):
         dq_sum = dq_sum + dq[s].astype(F32)
     tokens = dq.shape[1] // GROUPS
-    for b in range(out.shape[0]):
-        for kind in range(2):
-            total = near[0, b, kind].astype(F32) + from_core[0, b, kind].astype(F32)
-            total = total + from_z[b, kind].astype(F32)
-            out[b, kind * share : (kind + 1) * share] = total.astype(BF16)
-        x = b % GROUPS
-        piece = dq_sum[x * tokens : (x + 1) * tokens]
-        rest = jnp.zeros((out.shape[1] - 2 * share - tokens, piece.shape[1]), F32)
-        out[b, 2 * share :] = jnp.concatenate([piece, rest], axis=0).astype(BF16)
+    rest = jnp.zeros((out.shape[1] - 2 * share - tokens, out.shape[2]), F32)
+    tails = [
+        jnp.concatenate([dq_sum[x * tokens : (x + 1) * tokens], rest], axis=0).astype(BF16)
+        for x in range(GROUPS)
+    ]
+    for b in range(near.shape[0]):
+        for z in range(2):
+            for kind in range(2):
+                total = near[b, z, kind].astype(F32) + from_core[b, z, kind].astype(F32)
+                out[2 * b + z, kind * share : (kind + 1) * share] = total.astype(BF16)
+            out[2 * b + z, 2 * share :] = tails[b % GROUPS]
 
 
 def unpack_terms(place, terms, grad_queries, grad_keys, grad_values):
@@ -138,13 +141,14 @@
     width = terms.shape[2]
     for x in range(GROUPS):
         cols = slice(x * width, (x + 1) * width)
+        sources = [s for s in range(terms.shape[0]) if s // 2 % GROUPS == x]
         for kind, out in enumerate((grad_keys, grad_values)):
             part = slice(kind * share, (kind + 1) * share)
-            total = terms[x, part].astype(F32)
-            for y in range(1, terms.shape[0] // GROUPS):
-                total = total + terms[y * GROUPS + x, part].astype(F32)
+            total = terms[sources[0], part].astype(F32)
+            for s in sources[1:]:
+                total = total + terms[s, part].astype(F32)
             out[0, :, cols] = total.astype(BF16)
-        mine = terms[place[1] * GROUPS + x, 2 * share :].astype(F32)
+        mine = terms[(place[1] * GROUPS + x) * 2 + place[2], 2 * share :].astype(F32)
         grad_queries[0, :, cols] = mine[:tokens].astype(BF16)
 
 
@@ -164,16 +168,17 @@
     def memory_frame(z, c):
         return ((high_z * 2 + z) * sizes["yh"] + high_y) * 2 + c
 
+    group = [(low_z, core), (low_z, 1 - core), (1 - low_z, core), (1 - low_z, 1 - core)]
     place = jnp.stack(
-        [
-            x,
-            low_y,
-            memory_frame(low_z, core),
-            memory_frame(low_z, 1 - core),
-            memory_frame(1 - low_z, core),
-            memory_frame(1 - low_z, 1 - core),
-        ]
+        [x, low_y, low_z]
+        + [memory_frame(z, c) for z, c in group]
+        + [z * 2 + c for z, c in group]
     ).astype(jnp.int32)
+
+    kv = jnp.stack(
+        [lax.dynamic_slice_in_dim(a[0], x * width, width, 1) for a in (keys, values)]
+    )
+    kv = lax.all_gather(kv, ("zl", "c"), axis=0, tiled=False)
 
     packed = call(
         functools.partial(pack_rows, heads=heads),
@@ -189,47 +194,34 @@
     rows = lax.all_to_all(packed, ("zh", "yh", "x"), 0, 0, tiled=True)
     rows = rows.reshape(members * tokens_here, -1)
 
-    kv = jnp.stack(
-        [lax.dynamic_slice_in_dim(a[0], x * width, width, 1) for a in (keys, values)]
-    )
-    flip = [(0, 1), (1, 0)]
-    kv_z = lax.ppermute(kv, "zl", flip)
-    kv_core = lax.ppermute(kv, "c", flip)
-    kv_both = lax.ppermute(kv_z, "c", flip)
-
-    part = jax.ShapeDtypeStruct((2, blocks_q, 2, share, width), BF16)
+    part = jax.ShapeDtypeStruct((blocks_q, 2, 2, share, width), BF16)
     dq, near, far = call(
         functools.partial(attention_grads, heads=heads),
         "attention_grads",
         (jax.ShapeDtypeStruct((rows.shape[0], width), BF16), part, part),
-        [IN_SMEM] * 2 + [IN_VMEM] * 6,
+        [IN_SMEM] * 2 + [IN_VMEM] * 3,
         place,
         counts,
         frame_ids,
         rows,
         kv,
-        kv_core,
-        kv_z,
-        kv_both,
-    )
-
-    from_core = lax.ppermute(far, "c", flip)
+    )
+
     dq = lax.all_to_all(
         dq.reshape(spread, GROUPS * tokens_here, width), ("zh", "yh"), 0, 0, tiled=True
     )
-    other_z = (near[1].astype(F32) + from_core[1].astype(F32)).astype(BF16)
-    from_z = lax.ppermute(other_z, "zl", flip)
+    flip = [(0, 1), (1, 0)]
+    from_core = lax.ppermute(far, "c", flip)
     terms = call(
         pack_terms,
         "pack_terms",
-        jax.ShapeDtypeStruct((blocks_q, 2 * share + 2 * tokens_here, width), BF16),
-        [IN_VMEM] * 4,
+        jax.ShapeDtypeStruct((blocks_q * 2, 2 * share + 2 * tokens_here, width), BF16),
+        [IN_VMEM] * 3,
         dq,
         near,
         from_core,
-        from_z,
-    )
-    terms = lax.all_to_all(terms, ("yl", "x"), 0, 0, tiled=True)
+    )
+    terms = lax.all_to_all(terms, ("yl", "x", "zl"), 0, 0, tiled=True)
     return call(
         unpack_terms,
         "unpack_terms",

time: 97.8 us -> 116 us (1.19)
  blocking collectives: 11.3 us -> 87.7 us
  starting transfers between devices: 42.5 us -> 2.04 us
  waiting for transfers between devices: 33.2 us -> 2.07 us
  between operations: 0.81 us -> 14.2 us
  Pallas kernels: 6.4 us -> 4.89 us
    all_to_all x1 -> x3, blocking collectives: 11.3 us -> 87.7 us  [the longest x1 44.2 us: on_device(): rows = lax.all_to_all(packed, ('zh', 'yh', 'x'), 0, 0, tiled=True)]
    all_to_all x2 -> x0, starting transfers between devices: 30.3 us -> none  [the longest x1 19.1 us: on_device(): rows = lax.all_to_all(packed, ('zh', 'yh', 'x'), 0, 0, tiled=True)]
    ppermute x4 -> x0, waiting for transfers between devices: 20.4 us -> none  [the longest x1 17.5 us: on_device(): kv_z = lax.ppermute(kv, 'zl', flip)]
    all_to_all x2 -> x0, waiting for transfers between devices: 12.8 us -> none  [the longest x1 12.8 us: on_device(): lax.all_to_all(dq.reshape(spread, GROUPS * tokens_here, width), ('zh', 'y...]
    ppermute x4 -> x0, starting transfers between devices: 10.2 us -> none  [the longest x1 3.38 us: on_device(): kv_z = lax.ppermute(kv, 'zl', flip)]
    all_gather x0 -> x1, waiting for transfers between devices: none -> 2.05 us  [on_device(): kv = lax.all_gather(kv, ('zl', 'c'), axis=0, tiled=False)]
    pallas_call x4, Pallas kernels: 6.4 us -> 4.89 us  [call(): pl.pallas_call(body, out_shape=out_shape, in_specs=in_specs, out_specs=ja...]
  transfers between devices with their start and end apart: 7 -> 2, of which waited for: 4 -> 1; matrix products, arithmetic and copies ran while one was open for 1% -> 0% of each run, Pallas kernels for 0% -> 1%
where the time goes in v4:
time: 116 us; the launch traced here: 114 us
  blocking collectives  87.7 us (76%)
  between operations  14.2 us (12%)
  Pallas kernels  4.89 us (4%)
  local copies, waits for them, and re-layouts  2.63 us (2%)
  waiting for transfers between devices  2.07 us (2%)
  starting transfers between devices  2.04 us (2%)
    all_to_all x1, blocking collectives, on_device(): rows = lax.all_to_all(packed, ('zh', 'yh', 'x'), 0, 0, tiled=True)  44.2 us
    all_to_all x1, blocking collectives, on_device(): lax.all_to_all(dq.reshape(spread, GROUPS * tokens_here, width), ('zh', 'y...  26.9 us
    all_to_all x1, blocking collectives, on_device(): terms = lax.all_to_all(terms, ('yl', 'x', 'zl'), 0, 0, tiled=True)  16.6 us
    pallas_call x4, Pallas kernels, call(): pl.pallas_call(body, out_shape=out_shape, in_specs=in_specs, out_specs=ja...  4.89 us
  transfers between devices with their start and end apart: 2, of which 1 were waited for; matrix products, arithmetic and copies ran while one was open for 0% of the time, Pallas kernels for 1%

profile of v4, /device:TPU:6, one launch (start us, length us, event | category | flops | bytes accessed | tf_op | source)
XLA Modules:
  0.0 114.3 jit_solution(9949584439001711984)
XLA Ops:
  7.2 0.0 copy-start.5
  7.2 0.0 copy-start.3
  7.2 0.0 copy-start.2
  7.2 0.0 copy-start.1
  7.2 0.0 all-gather.3.cloned.1.call-start
  7.3 1.0 constant_dynamic-slice_fusion
  8.3 0.8 pad_maximum_fusion
  9.1 0.0 all-gather.3.cloned.1.call-update
  9.1 0.1 stack.52.place
  9.2 0.0 copy-done.5
  9.2 0.0 copy-done.3
  9.2 0.0 copy-done.2
  9.2 0.0 copy-done.1
  9.2 0.8 pack_rows.1
  10.0 0.0 copy-start.4
  10.1 0.0 copy-start.6
  10.1 44.2 %all_to_all.15 = bf16[64,4,1408]{2,1,0:T(4,128)(2,1)S(1)} all-to-all(bf16[64,4,1408]{2,1,0:T(4,128)(2,1)S(1)} %pack_rows.1), channel_id=1, replica_groups=mesh['yl'=2,'x'=4,'zh'=4,'zl'=2,'yh'=4,'c'=2] {'zh','yh','x'}, dimensions={0} | all-to-all | bytes 1441792 | tf_op jit(solution)/shard_map/all_to_all | solution.py:194
  54.3 0.2 reshape.16.rows
  54.5 2.1 %all-gather.3.cloned.1.call-done = bf16[8,128,640]{2,1,0:T(8,128)(2,1)} async-done(((bf16[2,128,640]{2,1,0:T(8,128)(2,1)}), bf16[8,128,640]{2,1,0:T(8,128)(2,1)}) %all-gather.3.cloned.1.call-update) | async-done | bytes 1310736 | tf_op jit(solution)/shard_map/all_gather | solution.py:181
  56.5 0.0 copy-done.4
  56.5 0.0 copy-done.6
  56.5 0.0 copy-start
  56.5 1.3 %copy-done = bf16[8,128,640]{2,1,0:T(8,128)(2,1)S(1)} copy-done((bf16[8,128,640]{2,1,0:T(8,128)(2,1)S(1)}, bf16[8,128,640]{2,1,0:T(8,128)(2,1)}, u32[]{:S(2)}) %copy-start) | copy-done | bytes 1310744
  57.9 2.6 %attention_grads.1 = (bf16[256,640]{1,0:T(8,128)(2,1)S(1)}, bf16[8,2,2,16,640]{4,3,2,1,0:T(8,128)(2,1)S(1)}, bf16[8,2,2,16,640]{4,3,2,1,0:T(8,128)(2,1)S(1)}) custom-call(s32[11]{0:T(128)S(1)} %stack.52.place, s32[8]{0:T(128)S(1)} %copy-done.6, s32[8,64]{1,0:T(8,128)S(1)} %copy-done.4, bf16[256,1408]{1,0:T(8,128)(2,1)S(1)} %reshape.16.rows, ...), custom_call_target="tpu_custom_call" | custom-call | tf_op jit(solution)/shard_map/attention_grads/pallas_call | solution.py:21
  60.4 2.0 %collective-permute-start = (bf16[8,2,2,16,640]{4,3,2,1,0:T(8,128)(2,1)S(1)}, bf16[8,2,2,16,640]{4,3,2,1,0:T(8,128)(2,1)S(1)}, u32[]{:S(2)}, u32[]{:S(2)}) collective-permute-start(bf16[8,2,2,16,640]{4,3,2,1,0:T(8,128)(2,1)S(1)} %get-tuple-element.8), channel_id=1, source_target_pairs={{0,1},{1,0},{2,3},{3,2},{4,5},{5,4},{6,7},{7,6},{8,9},{9,8},{10,11... | collective-permute-start | bytes 1966088 | tf_op jit(solution)/shard_map/ppermute | solution.py:214
  62.5 26.9 %all_to_all.16.dq = bf16[16,16,640]{2,1,0:T(8,128)(2,1)S(1)} all-to-all(bf16[16,16,640]{2,1,0:T(8,128)(2,1)S(1)} %bitcast.14), channel_id=1, replica_groups=mesh['yl'=2,'x'=4,'zh'=4,'zl'=2,'yh'=4,'c'=2] {'zh','yh'}, dimensions={0} | all-to-all | bytes 655360 | tf_op jit(solution)/shard_map/all_to_all | solution.py:210
  89.4 0.0 collective-permute-done.from_core
  89.4 0.2 pack_terms.1
  89.6 16.6 %all_to_all.17.terms = bf16[16,40,640]{2,1,0:T(8,128)(2,1)S(1)} all-to-all(bf16[16,40,640]{2,1,0:T(8,128)(2,1)S(1)} %pack_terms.1), channel_id=1, replica_groups=mesh['yl'=2,'x'=4,'zh'=4,'zl'=2,'yh'=4,'c'=2] {'yl','x','zl'}, dimensions={0} | all-to-all | bytes 1638400 | tf_op jit(solution)/shard_map/all_to_all | solution.py:224
  106.1 1.3 %unpack_terms.1 = (bf16[1,4,2560]{2,1,0:T(4,128)(2,1)}, bf16[1,16,2560]{2,1,0:T(8,128)(2,1)}, bf16[1,16,2560]{2,1,0:T(8,128)(2,1)}) custom-call(s32[11]{0:T(128)S(1)} %stack.52.place, bf16[16,40,640]{2,1,0:T(8,128)(2,1)S(1)} %all_to_all.17.terms), custom_call_target="tpu_custom_call" | custom-call | tf_op jit(solution)/shard_map/unpack_terms/pallas_call | solution.py:21
Async XLA Ops:
  7.2 2.0 %copy-start.5 = (f32[1,4,20]{2,1,0:T(4,128)S(1)}, f32[1,4,20]{2,1,0:T(4,128)}, u32[]{:S(2)}) copy-start(f32[1,4,20]{2,1,0:T(4,128)} %lse.1) | copy-start | bytes 964
  7.2 2.0 %copy-start.3 = (bf16[1,4,2560]{2,1,0:T(4,128)(2,1)S(1)}, bf16[1,4,2560]{2,1,0:T(4,128)(2,1)}, u32[]{:S(2)}) copy-start(bf16[1,4,2560]{2,1,0:T(4,128)(2,1)} %attn_out.1) | copy-start | bytes 61444
  7.2 2.0 %copy-start.2 = (bf16[1,4,2560]{2,1,0:T(4,128)(2,1)S(1)}, bf16[1,4,2560]{2,1,0:T(4,128)(2,1)}, u32[]{:S(2)}) copy-start(bf16[1,4,2560]{2,1,0:T(4,128)(2,1)} %grad_out.1) | copy-start | bytes 61444
  7.2 2.0 %copy-start.1 = (bf16[1,4,2560]{2,1,0:T(4,128)(2,1)S(1)}, bf16[1,4,2560]{2,1,0:T(4,128)(2,1)}, u32[]{:S(2)}) copy-start(bf16[1,4,2560]{2,1,0:T(4,128)(2,1)} %queries.1) | copy-start | bytes 61444
  7.2 49.3 %all-gather.3.cloned.1.call-start = ((), (), s32[]{:S(2)}) async-start(), calls=%async_computation.3 | async-start | bytes 1638400 | tf_op jit(solution)/shard_map/all_gather | solution.py:181
  10.0 46.5 %copy-start.4 = (s32[8,64]{1,0:T(8,128)S(1)}, s32[8,64]{1,0:T(8,128)}, u32[]{:S(2)}) copy-start(s32[8,64]{1,0:T(8,128)} %ids.1) | copy-start | bytes 6148
  10.1 46.5 %copy-start.6 = (s32[8]{0:T(128)S(1)}, s32[8]{0:T(128)}, u32[]{:S(2)}) copy-start(s32[8]{0:T(128)} %amounts.1) | copy-start | bytes 100
  56.5 1.3 %copy-start = (bf16[8,128,640]{2,1,0:T(8,128)(2,1)S(1)}, bf16[8,128,640]{2,1,0:T(8,128)(2,1)}, u32[]{:S(2)}) copy-start(bf16[8,128,640]{2,1,0:T(8,128)(2,1)} %all-gather.3.cloned.1.call-done) | copy-start | bytes 3932164
  60.4 28.9 %collective-permute-start = (bf16[8,2,2,16,640]{4,3,2,1,0:T(8,128)(2,1)S(1)}, bf16[8,2,2,16,640]{4,3,2,1,0:T(8,128)(2,1)S(1)}, u32[]{:S(2)}, u32[]{:S(2)}) collective-permute-start(bf16[8,2,2,16,640]{4,3,2,1,0:T(8,128)(2,1)S(1)} %get-tuple-element.8), channel_id=1, source_target_pairs={{0,1},{1,0},{2,3},{3,2},{4,5},{5,4},{6,7},{7,6},{8,9},{9,8},{10,11... | collective-permute-start | bytes 1966088 | tf_op jit(solution)/shard_map/ppermute | solution.py:214
Sparse Core Ops, SparseCore 0:
  10.1 46.3 all-gather.2

commit v5 on v2

--- a/solution.py
+++ b/solution.py
@@ -15,13 +15,15 @@
 F32, BF16 = jnp.float32, jnp.bfloat16
 IN_VMEM = pl.BlockSpec(memory_space=pltpu.VMEM)
 IN_SMEM = pl.BlockSpec(memory_space=pltpu.SMEM)
-
-
-def call(body, name, out_shape, in_specs, *args):
+LONG = pl.CostEstimate(flops=10**11, bytes_accessed=10**6, transcendentals=0)
+
+
+def call(body, name, out_shape, in_specs, *args, cost=None):
     return pl.pallas_call(
         body,
         out_shape=out_shape,
         in_specs=in_specs,
+        cost_estimate=cost,
         out_specs=jax.tree.map(lambda _: IN_VMEM, out_shape),
         compiler_params=pltpu.CompilerParams(vmem_limit_bytes=40 * 2**20),
         name=name,
@@ -52,14 +54,23 @@
             out[s * GROUPS + group] = row
 
 
-def attention_grads(
-    place, amounts, ids, rows, kv_own, kv_core, kv_z, kv_both, dq, near, far, *, heads
+def pair_frames(kv_own, kv_far, out):
+    out[0] = kv_own[...]
+    out[1] = kv_far[...]
+
+
+def frame_columns(kv_own, kv_core, kind, cols):
+    blocks = (kv_own.at[0], kv_core.at[0], kv_own.at[1], kv_core.at[1])
+    return jnp.concatenate([b[kind, :, cols] for b in blocks], axis=0)
+
+
+def key_value_grads(
+    place, amounts, ids, rows, kv_own, kv_core, grad_scores, near, far, *, heads
 ):
     score_scale = HS ** (-0.5)
     exponent_scale = score_scale * math.log2(math.e)
     width = heads * HS
-    blocks = (kv_own, kv_core, kv_z, kv_both)
-    tokens = kv_own.shape[1]
+    tokens = kv_own.shape[2]
 
     frame = lax.broadcasted_iota(jnp.int32, ids.shape, 0)
     entry = lax.broadcasted_iota(jnp.int32, ids.shape, 1)
@@ -84,8 +95,8 @@
         cols = slice(h * HS, (h + 1) * HS)
         q = rows[:, cols]
         g = rows[:, width + h * HS : width + (h + 1) * HS]
-        k = jnp.concatenate([b[0, :, cols] for b in blocks], axis=0)
-        v = jnp.concatenate([b[1, :, cols] for b in blocks], axis=0)
+        k = frame_columns(kv_own, kv_core, 0, cols)
+        v = frame_columns(kv_own, kv_core, 1, cols)
         k_pick = jnp.where((lane == h) | (lane == heads + h), -1.0, bias_all).astype(BF16)
         v_pick = jnp.where((lane == 2 * heads + h) | (lane == 3 * heads + h), -1.0, 0.0).astype(BF16)
         contract = (((1,), (1,)), ((), ()))
@@ -102,13 +113,10 @@
             contract,
             preferred_element_type=F32,
         )
-        grad_scores = (probs * grad_probs).astype(BF16)
+        ds = (probs * grad_probs).astype(BF16)
+        grad_scores[h] = ds
         dv = jnp.dot(probs.astype(BF16), g, preferred_element_type=F32).astype(BF16)
-        dk = (jnp.dot(grad_scores, q, preferred_element_type=F32) * score_scale).astype(BF16)
-        dq_h = lax.dot_general(
-            grad_scores, k, (((0,), (0,)), ((), ())), preferred_element_type=F32
-        )
-        dq[:, cols] = (dq_h * score_scale).astype(BF16)
+        dk = (jnp.dot(ds, q, preferred_element_type=F32) * score_scale).astype(BF16)
         for d, out in enumerate((near, far, near, far)):
             part = slice(d * tokens, (d + 1) * tokens)
             piece = (out.shape[1], out.shape[3], HS)
@@ -116,17 +124,34 @@
             out[d // 2, :, 1, :, cols] = dv[part].reshape(piece)
 
 
-def pack_terms(dq, near, from_core, from_z, out):
-    share = near.shape[3]
+def query_grads(grad_scores, kv_own, kv_core, dq):
+    for h in range(grad_scores.shape[0]):
+        cols = slice(h * HS, (h + 1) * HS)
+        k = frame_columns(kv_own, kv_core, 0, cols)
+        dq_h = lax.dot_general(
+            grad_scores[h], k, (((0,), (0,)), ((), ())), preferred_element_type=F32
+        )
+        dq[:, cols] = (dq_h * HS ** (-0.5)).astype(BF16)
+
+
+def add_core(near, from_core, out):
+    out[...] = (near[1].astype(F32) + from_core[1].astype(F32)).astype(BF16)
+
+
+def add_far(near, from_core, from_far, out):
+    total = near[0].astype(F32) + from_core[0].astype(F32)
+    out[...] = (total + from_far[...].astype(F32)).astype(BF16)
+
+
+def pack_terms(dq, part, out):
+    share = part.shape[2]
     dq_sum = dq[0].astype(F32)
     for s in range(1, dq.shape[0]):
         dq_sum = dq_sum + dq[s].astype(F32)
     tokens = dq.shape[1] // GROUPS
     for b in range(out.shape[0]):
         for kind in range(2):
-            total = near[0, b, kind].astype(F32) + from_core[0, b, kind].astype(F32)
-            total = total + from_z[b, kind].astype(F32)
-            out[b, kind * share : (kind + 1) * share] = total.astype(BF16)
+            out[b, kind * share : (kind + 1) * share] = part[b, kind]
         x = b % GROUPS
         piece = dq_sum[x * tokens : (x + 1) * tokens]
         rest = jnp.zeros((out.shape[1] - 2 * share - tokens, piece.shape[1]), F32)
@@ -149,31 +174,46 @@
 
 
 def on_device(sizes, queries, grad_out, attn_out, lse, keys, values, frame_ids, counts):
-    low_y, x = lax.axis_index("yl"), lax.axis_index("x")
-    high_z, low_z = lax.axis_index("zh"), lax.axis_index("zl")
-    high_y, core = lax.axis_index("yh"), lax.axis_index("c")
+    low_y, x, z = (lax.axis_index(a) for a in ("yl", "x", "z"))
+    far_y, near_y, core = (lax.axis_index(a) for a in ("yf", "ym", "c"))
     tokens_here = queries.shape[1]
     heads = lse.shape[2] // GROUPS
     width = heads * HS
     frame_tokens = keys.shape[1]
-    spread = sizes["zh"] * sizes["yh"]
+    spread = sizes["z"] * sizes["ym"]
     members = GROUPS * spread
     blocks_q = sizes["yl"] * sizes["x"]
     share = frame_tokens // blocks_q
 
-    def memory_frame(z, c):
-        return ((high_z * 2 + z) * sizes["yh"] + high_y) * 2 + c
+    def memory_frame(far, c):
+        return ((z * 2 + far) * sizes["ym"] + near_y) * 2 + c
 
     place = jnp.stack(
         [
             x,
             low_y,
-            memory_frame(low_z, core),
-            memory_frame(low_z, 1 - core),
-            memory_frame(1 - low_z, core),
-            memory_frame(1 - low_z, 1 - core),
+            memory_frame(far_y, core),
+            memory_frame(far_y, 1 - core),
+            memory_frame(1 - far_y, core),
+            memory_frame(1 - far_y, 1 - core),
         ]
     ).astype(jnp.int32)
+
+    flip = [(0, 1), (1, 0)]
+    kv = jnp.stack(
+        [lax.dynamic_slice_in_dim(a[0], x * width, width, 1) for a in (keys, values)]
+    )
+    kv_far = lax.ppermute(kv, "yf", flip)
+    kv_own = call(
+        pair_frames,
+        "pair_frames",
+        jax.ShapeDtypeStruct((2,) + kv.shape, BF16),
+        [IN_VMEM] * 2,
+        kv,
+        kv_far,
+        cost=LONG,
+    )
+    kv_core = lax.ppermute(kv_own, "c", flip)
 
     packed = call(
         functools.partial(pack_rows, heads=heads),
@@ -186,48 +226,50 @@
         attn_out,
         lse,
     )
-    rows = lax.all_to_all(packed, ("zh", "yh", "x"), 0, 0, tiled=True)
+    rows = lax.all_to_all(packed, ("z", "ym", "x"), 0, 0, tiled=True)
     rows = rows.reshape(members * tokens_here, -1)
 
-    kv = jnp.stack(
-        [lax.dynamic_slice_in_dim(a[0], x * width, width, 1) for a in (keys, values)]
-    )
-    flip = [(0, 1), (1, 0)]
-    kv_z = lax.ppermute(kv, "zl", flip)
-    kv_core = lax.ppermute(kv, "c", flip)
-    kv_both = lax.ppermute(kv_z, "c", flip)
-
     part = jax.ShapeDtypeStruct((2, blocks_q, 2, share, width), BF16)
-    dq, near, far = call(
-        functools.partial(attention_grads, heads=heads),
-        "attention_grads",
-        (jax.ShapeDtypeStruct((rows.shape[0], width), BF16), part, part),
-        [IN_SMEM] * 2 + [IN_VMEM] * 6,
+    half = jax.ShapeDtypeStruct(part.shape[1:], BF16)
+    grad_scores, near, far = call(
+        functools.partial(key_value_grads, heads=heads),
+        "key_value_grads",
+        (jax.ShapeDtypeStruct((heads, 4 * frame_tokens, rows.shape[0]), BF16), part, part),
+        [IN_SMEM] * 2 + [IN_VMEM] * 4,
         place,
         counts,
         frame_ids,
         rows,
-        kv,
+        kv_own,
         kv_core,
-        kv_z,
-        kv_both,
     )
 
     from_core = lax.ppermute(far, "c", flip)
+    dq = call(
+        query_grads,
+        "query_grads",
+        jax.ShapeDtypeStruct((rows.shape[0], width), BF16),
+        [IN_VMEM] * 3,
+        grad_scores,
+        kv_own,
+        kv_core,
+    )
+    from_core, dq = lax.optimization_barrier((from_core, dq))
+    other = call(add_core, "add_core", half, [IN_VMEM] * 2, near, from_core)
+    from_far = lax.ppermute(other, "yf", flip)
+    mine = call(
+        add_far, "add_far", half, [IN_VMEM] * 3, near, from_core, from_far, cost=LONG
+    )
     dq = lax.all_to_all(
-        dq.reshape(spread, GROUPS * tokens_here, width), ("zh", "yh"), 0, 0, tiled=True
-    )
-    other_z = (near[1].astype(F32) + from_core[1].astype(F32)).astype(BF16)
-    from_z = lax.ppermute(other_z, "zl", flip)
+        dq.reshape(spread, GROUPS * tokens_here, width), ("z", "ym"), 0, 0, tiled=True
+    )
     terms = call(
         pack_terms,
         "pack_terms",
         jax.ShapeDtypeStruct((blocks_q, 2 * share + 2 * tokens_here, width), BF16),
-        [IN_VMEM] * 4,
+        [IN_VMEM] * 2,
         dq,
-        near,
-        from_core,
-        from_z,
+        mine,
     )
     terms = lax.all_to_all(terms, ("yl", "x"), 0, 0, tiled=True)
     return call(
@@ -246,11 +288,11 @@
 
 def solution(mesh):
     query, mem = mesh.shape["query"], mesh.shape["mem"]
-    sizes = {"yl": query // GROUPS, "x": GROUPS, "zh": mem // 16, "zl": 2, "yh": 4, "c": 2}
-    if mem < 16:
-        sizes.update(zh=1, yh=mem // 4)
+    sizes = {"yl": query // GROUPS, "x": GROUPS, "z": mem // 8, "yf": 2, "ym": 2, "c": 2}
+    if mem < 8:
+        sizes.update(z=1, ym=mem // 4)
     fine = Mesh(mesh.devices.reshape(tuple(sizes.values())), tuple(sizes))
-    q_axes, m_axes = ("yl", "x"), ("zh", "zl", "yh", "c")
+    q_axes, m_axes = ("yl", "x"), ("z", "yf", "ym", "c")
     rows = P(q_axes, m_axes, None)
     frames = P(m_axes, None, None)
     return jax.shard_map(

time: 97.8 us -> 101 us (1.033)
  the two profiles are of different devices: /device:TPU:6 before, /device:TPU:16 now
where the time goes in v5:
time: 101 us; the launch traced here: 100 us
  starting transfers between devices  38.9 us (39%)
  waiting for transfers between devices  35.3 us (35%)
  blocking collectives  15.8 us (16%)
  Pallas kernels  6.67 us (7%)
  local copies, waits for them, and re-layouts  2.69 us (3%)
    all_to_all x1, waiting for transfers between devices, on_device(): rows = lax.all_to_all(packed, ('z', 'ym', 'x'), 0, 0, tiled=True)  19.9 us
    all_to_all x1, starting transfers between devices, on_device(): rows = lax.all_to_all(packed, ('z', 'ym', 'x'), 0, 0, tiled=True)  15.9 us
    all_to_all x1, blocking collectives, on_device(): terms = lax.all_to_all(terms, ('yl', 'x'), 0, 0, tiled=True)  15.8 us
    all_to_all x1, waiting for transfers between devices, on_device(): lax.all_to_all(dq.reshape(spread, GROUPS * tokens_here, width), ('z', 'ym...  12.1 us
    all_to_all x1, starting transfers between devices, on_device(): lax.all_to_all(dq.reshape(spread, GROUPS * tokens_here, width), ('z', 'ym...  9.19 us
    pallas_call x8, Pallas kernels, call(): pl.pallas_call(body, out_shape=out_shape, in_specs=in_specs, cost_estimat...  6.67 us
    ppermute x1, starting transfers between devices, on_device(): kv_far = lax.ppermute(kv, 'yf', flip)  5.94 us
    ppermute x1, starting transfers between devices, on_device(): from_far = lax.ppermute(other, 'yf', flip)  4.11 us
  transfers between devices with their start and end apart: 6, of which 4 were waited for; matrix products, arithmetic and copies ran while one was open for 2% of the time, Pallas kernels for 3%

profile of v5, /device:TPU:16, one launch (start us, length us, event | category | flops | bytes accessed | tf_op | source)
XLA Modules:
  0.0 100.2 jit_solution(17456242426354323598)
XLA Ops:
  0.6 0.0 copy-start.4
  0.6 0.0 copy-start.2
  0.7 0.0 copy-start.1
  0.7 0.0 copy-start
  0.7 1.0 %constant_dynamic-slice_fusion = (bf16[1,128,640]{2,1,0:T(8,128)(2,1)S(1)}, bf16[1,128,640]{2,1,0:T(8,128)(2,1)S(1)}) fusion(bf16[1,128,2560]{2,1,0:T(8,128)(2,1)} %param.13, s32[]{:T(128)S(6)} %select_n.4, bf16[1,128,2560]{2,1,0:T(8,128)(2,1)} %param.12), kind=kLoop, calls=%fused_computation.1 | loop fusion | bytes 655364 | tf_op jit(solution)/shard_map/dynamic_slice | solution.py:204
  1.8 5.9 %collective-permute-start = (bf16[2,128,640]{2,1,0:T(8,128)(2,1)S(1)}, bf16[2,128,640]{2,1,0:T(8,128)(2,1)S(1)}, u32[]{:S(2)}, u32[]{:S(2)}) collective-permute-start(bf16[2,128,640]{2,1,0:T(8,128)(2,1)S(1)} %pad_maximum_fusion.kv_own), channel_id=1, source_target_pairs={{0,4},{4,0},{1,5},{5,1},{2,6},{6,2},{3,7},{7,3},{8,12},{12,8},{9,1... | collective-permute-start | bytes 983048 | tf_op jit(solution)/shard_map/ppermute | solution.py:206
  7.7 0.1 stack.32.place
  7.8 0.0 copy-done.4
  7.8 0.0 copy-done.2
  7.8 0.0 copy-done.1
  7.8 0.0 copy-done
  7.8 1.7 %pack_rows.1 = bf16[64,4,1408]{2,1,0:T(4,128)(2,1)} custom-call(s32[6]{0:T(128)S(1)} %stack.32.place, bf16[1,4,2560]{2,1,0:T(4,128)(2,1)S(1)} %copy-done, bf16[1,4,2560]{2,1,0:T(4,128)(2,1)S(1)} %copy-done.1, bf16[1,4,2560]{2,1,0:T(4,128)(2,1)S(1)} %copy-done.2, f32[1,4,20]{2,1,0:T(4,128)S(1)} %copy-done.4), custom_call_target="tpu_custom_call" | custom-call | tf_op jit(solution)/shard_map/pack_rows/pallas_call | solution.py:22
  9.5 15.9 %all-to-all-start = ((bf16[64,4,1408]{2,1,0:T(4,128)(2,1)}), bf16[64,4,1408]{2,1,0:T(4,128)(2,1)}, u32[]{:S(2)}, u32[]{:S(2)}) async-start(bf16[64,4,1408]{2,1,0:T(4,128)(2,1)} %pack_rows.1), calls=%async_computation | async-start | bytes 1441792 | tf_op jit(solution)/shard_map/all_to_all | solution.py:229
  25.4 0.0 collective-permute-done.kv_far
  25.4 0.1 pair_frames.1.kv_own
  25.5 0.0 copy-start.3
  25.5 0.0 copy-start.5
  25.5 1.9 %collective-permute-start.1 = (bf16[2,2,128,640]{3,2,1,0:T(8,128)(2,1)S(1)}, bf16[2,2,128,640]{3,2,1,0:T(8,128)(2,1)S(1)}, u32[]{:S(2)}, u32[]{:S(2)}) collective-permute-start(bf16[2,2,128,640]{3,2,1,0:T(8,128)(2,1)S(1)} %pair_frames.1.kv_own), channel_id=1, source_target_pairs={{0,1},{1,0},{2,3},{3,2},{4,5},{5,4},{6,7},{7,6},{8,9},{9,8},{10,11... | collective-permute-start | bytes 1966088 | tf_op jit(solution)/shard_map/ppermute | solution.py:216
  27.4 19.9 %all-to-all-done = bf16[64,4,1408]{2,1,0:T(4,128)(2,1)} async-done(((bf16[64,4,1408]{2,1,0:T(4,128)(2,1)}), bf16[64,4,1408]{2,1,0:T(4,128)(2,1)}, u32[]{:S(2)}, u32[]{:S(2)}) %all-to-all-start) | async-done | bytes 720928 | tf_op jit(solution)/shard_map/all_to_all | solution.py:229
  47.4 1.5 %reshape.16.rows = bf16[256,1408]{1,0:T(8,128)(2,1)S(1)} reshape(bf16[64,4,1408]{2,1,0:T(4,128)(2,1)} %all-to-all-done) | data formatting | bytes 1441792 | tf_op jit(solution)/shard_map/reshape | solution.py:230
  48.9 0.0 collective-permute-done.1.kv_core
  48.9 0.0 copy-done.3
  48.9 0.0 copy-done.5
  48.9 2.1 %key_value_grads.1 = (bf16[5,512,256]{2,1,0:T(8,128)(2,1)S(1)}, bf16[2,8,2,16,640]{4,3,2,1,0:T(8,128)(2,1)S(1)}, bf16[2,8,2,16,640]{4,3,2,1,0:T(8,128)(2,1)S(1)}) custom-call(s32[6]{0:T(128)S(1)} %stack.32.place, s32[8]{0:T(128)S(1)} %copy-done.5, s32[8,64]{1,0:T(8,128)S(1)} %copy-done.3, bf16[256,1408]{1,0:T(8,128)(2,1)S(1)} %reshape.16.rows, ...), custom_call_target="tpu_custom_call" | custom-call | tf_op jit(solution)/shard_map/key_value_grads/pallas_call | solution.py:22
  51.1 1.9 %collective-permute-start.2 = (bf16[2,8,2,16,640]{4,3,2,1,0:T(8,128)(2,1)S(1)}, bf16[2,8,2,16,640]{4,3,2,1,0:T(8,128)(2,1)S(1)}, u32[]{:S(2)}, u32[]{:S(2)}) collective-permute-start(bf16[2,8,2,16,640]{4,3,2,1,0:T(8,128)(2,1)S(1)} %get-tuple-element.8), channel_id=1, source_target_pairs={{0,1},{1,0},{2,3},{3,2},{4,5},{5,4},{6,7},{7,6},{8,9},{9,8},{10,11... | collective-permute-start | bytes 1966088 | tf_op jit(solution)/shard_map/ppermute | solution.py:247
  53.0 1.3 %query_grads.1 = bf16[256,640]{1,0:T(8,128)(2,1)} custom-call(bf16[5,512,256]{2,1,0:T(8,128)(2,1)S(1)} %get-tuple-element.9.grad_scores, bf16[2,2,128,640]{3,2,1,0:T(8,128)(2,1)S(1)} %pair_frames.1.kv_own, bf16[2,2,128,640]{3,2,1,0:T(8,128)(2,1)S(1)} %collective-permute-done.1.kv_core), custom_call_target="tpu_custom_call" | custom-call | tf_op jit(solution)/shard_map/query_grads/pallas_call | solution.py:22
  54.3 0.8 collective-permute-done.2.from_core
  55.1 0.1 add_core.1
  55.2 4.1 %collective-permute-start.3 = (bf16[8,2,16,640]{3,2,1,0:T(8,128)(2,1)S(1)}, bf16[8,2,16,640]{3,2,1,0:T(8,128)(2,1)S(1)}, u32[]{:S(2)}, u32[]{:S(2)}) collective-permute-start(bf16[8,2,16,640]{3,2,1,0:T(8,128)(2,1)S(1)} %add_core.1), channel_id=1, source_target_pairs={{0,4},{4,0},{1,5},{5,1},{2,6},{6,2},{3,7},{7,3},{8,12},{12,8},{9,1... | collective-permute-start | bytes 983048 | tf_op jit(solution)/shard_map/ppermute | solution.py:259
  59.3 9.2 %all-to-all-start.1 = ((bf16[16,16,640]{2,1,0:T(8,128)(2,1)}), bf16[16,16,640]{2,1,0:T(8,128)(2,1)S(1)}, u32[]{:S(2)}, u32[]{:S(2)}) async-start(bf16[16,16,640]{2,1,0:T(8,128)(2,1)} %bitcast.6), calls=%async_computation.1 | async-start | bytes 655360 | tf_op jit(solution)/shard_map/all_to_all | solution.py:263
  68.5 2.4 %collective-permute-done.3.from_far = bf16[8,2,16,640]{3,2,1,0:T(8,128)(2,1)S(1)} collective-permute-done((bf16[8,2,16,640]{3,2,1,0:T(8,128)(2,1)S(1)}, bf16[8,2,16,640]{3,2,1,0:T(8,128)(2,1)S(1)}, u32[]{:S(2)}, u32[]{:S(2)}) %collective-permute-start.3) | collective-permute-done | bytes 327712 | tf_op jit(solution)/shard_map/ppermute | solution.py:259
  70.9 0.1 add_far.1.part
  71.0 12.1 %all-to-all-done.1.dq = bf16[16,16,640]{2,1,0:T(8,128)(2,1)S(1)} async-done(((bf16[16,16,640]{2,1,0:T(8,128)(2,1)}), bf16[16,16,640]{2,1,0:T(8,128)(2,1)S(1)}, u32[]{:S(2)}, u32[]{:S(2)}) %all-to-all-start.1) | async-done | bytes 327712 | tf_op jit(solution)/shard_map/all_to_all | solution.py:263
  83.2 0.1 pack_terms.1
  83.2 15.8 %all_to_all.15.terms = bf16[8,40,640]{2,1,0:T(8,128)(2,1)S(1)} all-to-all(bf16[8,40,640]{2,1,0:T(8,128)(2,1)S(1)} %pack_terms.1), channel_id=1, replica_groups=mesh['yl'=2,'x'=4,'z'=8,'yf'=2,'ym'=2,'c'=2] {'yl','x'}, dimensions={0} | all-to-all | bytes 819200 | tf_op jit(solution)/shard_map/all_to_all | solution.py:274
  99.0 1.2 %unpack_terms.1 = (bf16[1,4,2560]{2,1,0:T(4,128)(2,1)}, bf16[1,16,2560]{2,1,0:T(8,128)(2,1)}, bf16[1,16,2560]{2,1,0:T(8,128)(2,1)}) custom-call(s32[6]{0:T(128)S(1)} %stack.32.place, bf16[8,40,640]{2,1,0:T(8,128)(2,1)S(1)} %all_to_all.15.terms), custom_call_target="tpu_custom_call" | custom-call | tf_op jit(solution)/shard_map/unpack_terms/pallas_call | solution.py:22
  (1 shorter events, 0.0 us)
Async XLA Ops:
  0.6 7.2 %copy-start.4 = (f32[1,4,20]{2,1,0:T(4,128)S(1)}, f32[1,4,20]{2,1,0:T(4,128)}, u32[]{:S(2)}) copy-start(f32[1,4,20]{2,1,0:T(4,128)} %lse.1) | copy-start | bytes 964
  0.6 7.2 %copy-start.2 = (bf16[1,4,2560]{2,1,0:T(4,128)(2,1)S(1)}, bf16[1,4,2560]{2,1,0:T(4,128)(2,1)}, u32[]{:S(2)}) copy-start(bf16[1,4,2560]{2,1,0:T(4,128)(2,1)} %attn_out.1) | copy-start | bytes 61444
  0.7 7.2 %copy-start.1 = (bf16[1,4,2560]{2,1,0:T(4,128)(2,1)S(1)}, bf16[1,4,2560]{2,1,0:T(4,128)(2,1)}, u32[]{:S(2)}) copy-start(bf16[1,4,2560]{2,1,0:T(4,128)(2,1)} %grad_out.1) | copy-start | bytes 61444
  0.7 7.2 %copy-start = (bf16[1,4,2560]{2,1,0:T(4,128)(2,1)S(1)}, bf16[1,4,2560]{2,1,0:T(4,128)(2,1)}, u32[]{:S(2)}) copy-start(bf16[1,4,2560]{2,1,0:T(4,128)(2,1)} %queries.1) | copy-start | bytes 61444
  1.8 23.6 %collective-permute-start = (bf16[2,128,640]{2,1,0:T(8,128)(2,1)S(1)}, bf16[2,128,640]{2,1,0:T(8,128)(2,1)S(1)}, u32[]{:S(2)}, u32[]{:S(2)}) collective-permute-start(bf16[2,128,640]{2,1,0:T(8,128)(2,1)S(1)} %pad_maximum_fusion.kv_own), channel_id=1, source_target_pairs={{0,4},{4,0},{1,5},{5,1},{2,6},{6,2},{3,7},{7,3},{8,12},{12,8},{9,1... | collective-permute-start | bytes 983048 | tf_op jit(solution)/shard_map/ppermute | solution.py:206
  9.5 37.8 %all-to-all-start = ((bf16[64,4,1408]{2,1,0:T(4,128)(2,1)}), bf16[64,4,1408]{2,1,0:T(4,128)(2,1)}, u32[]{:S(2)}, u32[]{:S(2)}) async-start(bf16[64,4,1408]{2,1,0:T(4,128)(2,1)} %pack_rows.1), calls=%async_computation | async-start | bytes 1441792 | tf_op jit(solution)/shard_map/all_to_all | solution.py:229
  25.5 23.4 %copy-start.3 = (s32[8,64]{1,0:T(8,128)S(1)}, s32[8,64]{1,0:T(8,128)}, u32[]{:S(2)}) copy-start(s32[8,64]{1,0:T(8,128)} %ids.1) | copy-start | bytes 6148
  25.5 23.4 %copy-start.5 = (s32[8]{0:T(128)S(1)}, s32[8]{0:T(128)}, u32[]{:S(2)}) copy-start(s32[8]{0:T(128)} %amounts.1) | copy-start | bytes 100
  25.5 23.4 %collective-permute-start.1 = (bf16[2,2,128,640]{3,2,1,0:T(8,128)(2,1)S(1)}, bf16[2,2,128,640]{3,2,1,0:T(8,128)(2,1)S(1)}, u32[]{:S(2)}, u32[]{:S(2)}) collective-permute-start(bf16[2,2,128,640]{3,2,1,0:T(8,128)(2,1)S(1)} %pair_frames.1.kv_own), channel_id=1, source_target_pairs={{0,1},{1,0},{2,3},{3,2},{4,5},{5,4},{6,7},{7,6},{8,9},{9,8},{10,11... | collective-permute-start | bytes 1966088 | tf_op jit(solution)/shard_map/ppermute | solution.py:216
  51.1 4.0 %collective-permute-start.2 = (bf16[2,8,2,16,640]{4,3,2,1,0:T(8,128)(2,1)S(1)}, bf16[2,8,2,16,640]{4,3,2,1,0:T(8,128)(2,1)S(1)}, u32[]{:S(2)}, u32[]{:S(2)}) collective-permute-start(bf16[2,8,2,16,640]{4,3,2,1,0:T(8,128)(2,1)S(1)} %get-tuple-element.8), channel_id=1, source_target_pairs={{0,1},{1,0},{2,3},{3,2},{4,5},{5,4},{6,7},{7,6},{8,9},{9,8},{10,11... | collective-permute-start | bytes 1966088 | tf_op jit(solution)/shard_map/ppermute | solution.py:247
  55.2 15.8 %collective-permute-start.3 = (bf16[8,2,16,640]{3,2,1,0:T(8,128)(2,1)S(1)}, bf16[8,2,16,640]{3,2,1,0:T(8,128)(2,1)S(1)}, u32[]{:S(2)}, u32[]{:S(2)}) collective-permute-start(bf16[8,2,16,640]{3,2,1,0:T(8,128)(2,1)S(1)} %add_core.1), channel_id=1, source_target_pairs={{0,4},{4,0},{1,5},{5,1},{2,6},{6,2},{3,7},{7,3},{8,12},{12,8},{9,1... | collective-permute-start | bytes 983048 | tf_op jit(solution)/shard_map/ppermute | solution.py:259
  59.3 23.9 %all-to-all-start.1 = ((bf16[16,16,640]{2,1,0:T(8,128)(2,1)}), bf16[16,16,640]{2,1,0:T(8,128)(2,1)S(1)}, u32[]{:S(2)}, u32[]{:S(2)}) async-start(bf16[16,16,640]{2,1,0:T(8,128)(2,1)} %bitcast.6), calls=%async_computation.1 | async-start | bytes 655360 | tf_op jit(solution)/shard_map/all_to_all | solution.py:263

commit v6 on v4

--- a/solution.py
+++ b/solution.py
@@ -15,15 +15,17 @@
 F32, BF16 = jnp.float32, jnp.bfloat16
 IN_VMEM = pl.BlockSpec(memory_space=pltpu.VMEM)
 IN_SMEM = pl.BlockSpec(memory_space=pltpu.SMEM)
-
-
-def call(body, name, out_shape, in_specs, *args):
+LONG = pl.CostEstimate(flops=10**11, bytes_accessed=10**6, transcendentals=0)
+
+
+def call(body, name, out_shape, in_specs, *args, cost=None):
     return pl.pallas_call(
         body,
         out_shape=out_shape,
         in_specs=in_specs,
+        cost_estimate=cost,
         out_specs=jax.tree.map(lambda _: IN_VMEM, out_shape),
-        compiler_params=pltpu.CompilerParams(vmem_limit_bytes=40 * 2**20),
+        compiler_params=pltpu.CompilerParams(vmem_limit_bytes=20 * 2**20),
         name=name,
     )(*args)
 
@@ -52,14 +54,19 @@
             out[s * GROUPS + group] = row
 
 
+def pair_frames(kv_own, kv_z, out):
+    out[0] = kv_own[...]
+    out[1] = kv_z[...]
+
+
 def attention_grads(
-    place, amounts, ids, rows, kv, dq, near, far, *, heads
+    place, amounts, ids, rows, kv_own, kv_core, dq, near, far_keys, far_values, *, heads
 ):
     score_scale = HS ** (-0.5)
     exponent_scale = score_scale * math.log2(math.e)
     width = heads * HS
-    blocks = [kv.at[place[7 + d]] for d in range(4)]
-    tokens = kv.shape[2]
+    blocks = (kv_own.at[0], kv_core.at[0], kv_own.at[1], kv_core.at[1])
+    tokens = kv_own.shape[2]
 
     frame = lax.broadcasted_iota(jnp.int32, ids.shape, 0)
     entry = lax.broadcasted_iota(jnp.int32, ids.shape, 1)
@@ -72,7 +79,7 @@
     spot = (lane8 == 4 * heads + row8) & (row8 >= 0) & (row8 < GROUPS)
     biases = []
     for d in range(4):
-        hit = jnp.where((ids[...] == place[3 + d]) & listed, 1.0, 0.0)
+        hit = jnp.where((ids[...] == place[2 + d]) & listed, 1.0, 0.0)
         found = jnp.max(hit, axis=1, keepdims=True)
         bias = jnp.sum(jnp.where(spot, (1.0 - found) * MASKED, 0.0), axis=0, keepdims=True)
         biases.append(jnp.broadcast_to(bias, (tokens, LANES)))
@@ -109,15 +116,19 @@
             grad_scores, k, (((0,), (0,)), ((), ())), preferred_element_type=F32
         )
         dq[:, cols] = (dq_h * score_scale).astype(BF16)
-        for d, out in enumerate((near, far, near, far)):
+        piece = (near.shape[0], near.shape[3], HS)
+        for d in range(4):
             part = slice(d * tokens, (d + 1) * tokens)
-            z = place[2] if d < 2 else 1 - place[2]
-            piece = (out.shape[0], out.shape[3], HS)
-            out[:, z, 0, :, cols] = dk[part].reshape(piece)
-            out[:, z, 1, :, cols] = dv[part].reshape(piece)
-
-
-def pack_terms(dq, near, from_core, out):
+            z = place[6] if d < 2 else 1 - place[6]
+            if d % 2 == 0:
+                near[:, z, 0, :, cols] = dk[part].reshape(piece)
+                near[:, z, 1, :, cols] = dv[part].reshape(piece)
+            else:
+                far_keys[:, z, :, cols] = dk[part].reshape(piece)
+                far_values[:, z, :, cols] = dv[part].reshape(piece)
+
+
+def pack_terms(dq, near, core_keys, core_values, out):
     share = near.shape[3]
     dq_sum = dq[0].astype(F32)
     for s in range(1, dq.shape[0]):
@@ -130,8 +141,8 @@
     ]
     for b in range(near.shape[0]):
         for z in range(2):
-            for kind in range(2):
-                total = near[b, z, kind].astype(F32) + from_core[b, z, kind].astype(F32)
+            for kind, other in enumerate((core_keys, core_values)):
+                total = near[b, z, kind].astype(F32) + other[b, z].astype(F32)
                 out[2 * b + z, kind * share : (kind + 1) * share] = total.astype(BF16)
             out[2 * b + z, 2 * share :] = tails[b % GROUPS]
 
@@ -148,14 +159,13 @@
             for s in sources[1:]:
                 total = total + terms[s, part].astype(F32)
             out[0, :, cols] = total.astype(BF16)
-        mine = terms[(place[1] * GROUPS + x) * 2 + place[2], 2 * share :].astype(F32)
+        mine = terms[(place[1] * GROUPS + x) * 2 + place[6], 2 * share :].astype(F32)
         grad_queries[0, :, cols] = mine[:tokens].astype(BF16)
 
 
 def on_device(sizes, queries, grad_out, attn_out, lse, keys, values, frame_ids, counts):
-    low_y, x = lax.axis_index("yl"), lax.axis_index("x")
-    high_z, low_z = lax.axis_index("zh"), lax.axis_index("zl")
-    high_y, core = lax.axis_index("yh"), lax.axis_index("c")
+    low_y, x, high_z = (lax.axis_index(a) for a in ("yl", "x", "zh"))
+    low_z, high_y, core = (lax.axis_index(a) for a in ("zl", "yh", "c"))
     tokens_here = queries.shape[1]
     heads = lse.shape[2] // GROUPS
     width = heads * HS
@@ -168,17 +178,33 @@
     def memory_frame(z, c):
         return ((high_z * 2 + z) * sizes["yh"] + high_y) * 2 + c
 
-    group = [(low_z, core), (low_z, 1 - core), (1 - low_z, core), (1 - low_z, 1 - core)]
     place = jnp.stack(
-        [x, low_y, low_z]
-        + [memory_frame(z, c) for z, c in group]
-        + [z * 2 + c for z, c in group]
+        [
+            x,
+            low_y,
+            memory_frame(low_z, core),
+            memory_frame(low_z, 1 - core),
+            memory_frame(1 - low_z, core),
+            memory_frame(1 - low_z, 1 - core),
+            low_z,
+        ]
     ).astype(jnp.int32)
 
+    flip = [(0, 1), (1, 0)]
     kv = jnp.stack(
         [lax.dynamic_slice_in_dim(a[0], x * width, width, 1) for a in (keys, values)]
     )
-    kv = lax.all_gather(kv, ("zl", "c"), axis=0, tiled=False)
+    kv_z = lax.ppermute(kv, "zl", flip)
+    kv_own = call(
+        pair_frames,
+        "pair_frames",
+        jax.ShapeDtypeStruct((2,) + kv.shape, BF16),
+        [IN_VMEM] * 2,
+        kv,
+        kv_z,
+        cost=LONG,
+    )
+    kv_core = lax.ppermute(kv_own, "c", flip)
 
     packed = call(
         functools.partial(pack_rows, heads=heads),
@@ -195,31 +221,32 @@
     rows = rows.reshape(members * tokens_here, -1)
 
     part = jax.ShapeDtypeStruct((blocks_q, 2, 2, share, width), BF16)
-    dq, near, far = call(
+    half = jax.ShapeDtypeStruct((blocks_q, 2, share, width), BF16)
+    dq, near, *far = call(
         functools.partial(attention_grads, heads=heads),
         "attention_grads",
-        (jax.ShapeDtypeStruct((rows.shape[0], width), BF16), part, part),
-        [IN_SMEM] * 2 + [IN_VMEM] * 3,
+        (jax.ShapeDtypeStruct((rows.shape[0], width), BF16), part, half, half),
+        [IN_SMEM] * 2 + [IN_VMEM] * 4,
         place,
         counts,
         frame_ids,
         rows,
-        kv,
+        kv_own,
+        kv_core,
     )
 
     dq = lax.all_to_all(
         dq.reshape(spread, GROUPS * tokens_here, width), ("zh", "yh"), 0, 0, tiled=True
     )
-    flip = [(0, 1), (1, 0)]
-    from_core = lax.ppermute(far, "c", flip)
+    from_core = [lax.ppermute(a, "c", flip) for a in far]
     terms = call(
         pack_terms,
         "pack_terms",
         jax.ShapeDtypeStruct((blocks_q * 2, 2 * share + 2 * tokens_here, width), BF16),
-        [IN_VMEM] * 3,
+        [IN_VMEM] * 4,
         dq,
         near,
-        from_core,
+        *from_core,
     )
     terms = lax.all_to_all(terms, ("yl", "x", "zl"), 0, 0, tiled=True)
     return call(

time: 116 us -> 93.6 us (0.81)
  blocking collectives: 87.7 us -> 16.3 us
  starting transfers between devices: 2.04 us -> 33.6 us
  waiting for transfers between devices: 2.07 us -> 32.8 us
  between operations: 14.2 us -> 0.82 us
  Pallas kernels: 4.89 us -> 6.52 us
    all_to_all x2 -> x0, blocking collectives: 71.1 us -> none  [the longest x1 44.2 us: on_device(): rows = lax.all_to_all(packed, ('zh', 'yh', 'x'), 0, 0, tiled=True)]
    all_to_all x0 -> x2, waiting for transfers between devices: none -> 31.6 us  [the longest x1 22.8 us: on_device(): rows = lax.all_to_all(packed, ('zh', 'yh', 'x'), 0, 0, tiled=True)]
    all_to_all x0 -> x2, starting transfers between devices: none -> 23.1 us  [the longest x1 18.2 us: on_device(): rows = lax.all_to_all(packed, ('zh', 'yh', 'x'), 0, 0, tiled=True)]
    ppermute x1 -> x4, starting transfers between devices: 2.01 us -> 10.5 us  [the longest x2 4.33 us: on_device(): from_core = [lax.ppermute(a, 'c', flip) for a in far]]
    all_gather x1 -> x0, waiting for transfers between devices: 2.05 us -> none  [on_device(): kv = lax.all_gather(kv, ('zl', 'c'), axis=0, tiled=False)]
    pallas_call x4 -> x5, Pallas kernels: 4.89 us -> 6.52 us  [call(): pl.pallas_call(body, out_shape=out_shape, in_specs=in_specs, cost_estimat...]
    ppermute x1 -> x4, waiting for transfers between devices: 0.01 us -> 1.23 us  [the longest x2 1.23 us: on_device(): from_core = [lax.ppermute(a, 'c', flip) for a in far]]
  transfers between devices with their start and end apart: 2 -> 6, of which waited for: 1 -> 3; matrix products, arithmetic and copies ran while one was open for 0% -> 0% of each run, Pallas kernels for 1% -> 2%
where the time goes in v6:
time: 93.6 us; the launch traced here: 92 us
  starting transfers between devices  33.6 us (36%)
  waiting for transfers between devices  32.8 us (35%)
  blocking collectives  16.3 us (17%)
  Pallas kernels  6.52 us (7%)
  local copies, waits for them, and re-layouts  1.94 us (2%)
    all_to_all x1, waiting for transfers between devices, on_device(): rows = lax.all_to_all(packed, ('zh', 'yh', 'x'), 0, 0, tiled=True)  22.8 us
    all_to_all x1, starting transfers between devices, on_device(): rows = lax.all_to_all(packed, ('zh', 'yh', 'x'), 0, 0, tiled=True)  18.2 us
    all_to_all x1, blocking collectives, on_device(): terms = lax.all_to_all(terms, ('yl', 'x', 'zl'), 0, 0, tiled=True)  16.3 us
    all_to_all x1, waiting for transfers between devices, on_device(): lax.all_to_all(dq.reshape(spread, GROUPS * tokens_here, width), ('zh', 'y...  8.76 us
    pallas_call x5, Pallas kernels, call(): pl.pallas_call(body, out_shape=out_shape, in_specs=in_specs, cost_estimat...  6.52 us
    all_to_all x1, starting transfers between devices, on_device(): lax.all_to_all(dq.reshape(spread, GROUPS * tokens_here, width), ('zh', 'y...  4.94 us
    ppermute x2, starting transfers between devices, on_device(): from_core = [lax.ppermute(a, 'c', flip) for a in far]  4.33 us
    ppermute x1, starting transfers between devices, on_device(): kv_z = lax.ppermute(kv, 'zl', flip)  4.28 us
  transfers between devices with their start and end apart: 6, of which 3 were waited for; matrix products, arithmetic and copies ran while one was open for 0% of the time, Pallas kernels for 2%

profile of v6, /device:TPU:6, one launch (start us, length us, event | category | flops | bytes accessed | tf_op | source)
XLA Modules:
  0.0 92.0 jit_solution(13005812088549221415)
XLA Ops:
  0.6 1.0 %constant_dynamic-slice_fusion = (bf16[1,128,640]{2,1,0:T(8,128)(2,1)S(1)}, bf16[1,128,640]{2,1,0:T(8,128)(2,1)S(1)}) fusion(bf16[1,128,2560]{2,1,0:T(8,128)(2,1)} %param.13, s32[]{:T(128)S(6)} %select_n.4, bf16[1,128,2560]{2,1,0:T(8,128)(2,1)} %param.12), kind=kLoop, calls=%fused_computation.1 | loop fusion | bytes 655364 | tf_op jit(solution)/shard_map/dynamic_slice | solution.py:195
  1.7 4.3 %collective-permute-start = (bf16[2,128,640]{2,1,0:T(8,128)(2,1)S(1)}, bf16[2,128,640]{2,1,0:T(8,128)(2,1)S(1)}, u32[]{:S(2)}, u32[]{:S(2)}) collective-permute-start(bf16[2,128,640]{2,1,0:T(8,128)(2,1)S(1)} %pad_maximum_fusion.kv_own), channel_id=1, source_target_pairs={{0,8},{8,0},{1,9},{9,1},{2,10},{10,2},{3,11},{11,3},{4,12},{12,4},... | collective-permute-start | bytes 983048 | tf_op jit(solution)/shard_map/ppermute | solution.py:197
  6.0 0.0 copy-start.4
  6.0 0.0 copy-start.2
  6.0 0.0 copy-start.1
  6.1 0.0 copy-start
  6.1 0.1 stack.36.place
  6.2 0.5 copy-done.4
  6.7 0.1 copy-done.2
  6.8 0.0 copy-done.1
  6.8 0.0 copy-done
  6.8 1.7 %pack_rows.1 = bf16[64,4,1408]{2,1,0:T(4,128)(2,1)} custom-call(s32[7]{0:T(128)S(1)} %stack.36.place, bf16[1,4,2560]{2,1,0:T(4,128)(2,1)S(1)} %copy-done, bf16[1,4,2560]{2,1,0:T(4,128)(2,1)S(1)} %copy-done.1, bf16[1,4,2560]{2,1,0:T(4,128)(2,1)S(1)} %copy-done.2, f32[1,4,20]{2,1,0:T(4,128)S(1)} %copy-done.4), custom_call_target="tpu_custom_call" | custom-call | tf_op jit(solution)/shard_map/pack_rows/pallas_call | solution.py:22
  8.5 18.2 %all-to-all-start = ((bf16[64,4,1408]{2,1,0:T(4,128)(2,1)}), bf16[64,4,1408]{2,1,0:T(4,128)(2,1)S(1)}, u32[]{:S(2)}, u32[]{:S(2)}) async-start(bf16[64,4,1408]{2,1,0:T(4,128)(2,1)} %pack_rows.1), calls=%async_computation | async-start | bytes 1441792 | tf_op jit(solution)/shard_map/all_to_all | solution.py:220
  26.7 0.0 collective-permute-done.kv_z
  26.7 0.1 pair_frames.1.kv_own
  26.7 0.0 copy-start.3
  26.7 0.0 copy-start.5
  26.7 1.9 %collective-permute-start.1 = (bf16[2,2,128,640]{3,2,1,0:T(8,128)(2,1)S(1)}, bf16[2,2,128,640]{3,2,1,0:T(8,128)(2,1)S(1)}, u32[]{:S(2)}, u32[]{:S(2)}) collective-permute-start(bf16[2,2,128,640]{3,2,1,0:T(8,128)(2,1)S(1)} %pair_frames.1.kv_own), channel_id=1, source_target_pairs={{0,1},{1,0},{2,3},{3,2},{4,5},{5,4},{6,7},{7,6},{8,9},{9,8},{10,11... | collective-permute-start | bytes 1966088 | tf_op jit(solution)/shard_map/ppermute | solution.py:207
  28.7 22.8 %all-to-all-done = bf16[64,4,1408]{2,1,0:T(4,128)(2,1)S(1)} async-done(((bf16[64,4,1408]{2,1,0:T(4,128)(2,1)}), bf16[64,4,1408]{2,1,0:T(4,128)(2,1)S(1)}, u32[]{:S(2)}, u32[]{:S(2)}) %all-to-all-start) | async-done | bytes 720928 | tf_op jit(solution)/shard_map/all_to_all | solution.py:220
  51.5 0.2 reshape.16.rows
  51.6 0.0 collective-permute-done.1.kv_core
  51.7 0.0 copy-done.3
  51.7 0.0 copy-done.5
  51.7 3.3 %attention_grads.1 = (bf16[256,640]{1,0:T(8,128)(2,1)}, bf16[8,2,2,16,640]{4,3,2,1,0:T(8,128)(2,1)S(1)}, bf16[8,2,16,640]{3,2,1,0:T(8,128)(2,1)S(1)}, bf16[8,2,16,640]{3,2,1,0:T(8,128)(2,1)S(1)}) custom-call(s32[7]{0:T(128)S(1)} %stack.36.place, s32[8]{0:T(128)S(1)} %copy-done.5, s32[8,64]{1,0:T(8,128)S(1)} %copy-done.3, ...), custom_call_target="tpu_custom_call" | custom-call | tf_op jit(solution)/shard_map/attention_grads/pallas_call | solution.py:22
  55.0 4.9 %all-to-all-start.1 = ((bf16[16,16,640]{2,1,0:T(8,128)(2,1)}), bf16[16,16,640]{2,1,0:T(8,128)(2,1)S(1)}, u32[]{:S(2)}, u32[]{:S(2)}) async-start(bf16[16,16,640]{2,1,0:T(8,128)(2,1)} %bitcast.7), calls=%async_computation.1 | async-start | bytes 655360 | tf_op jit(solution)/shard_map/all_to_all | solution.py:238
  59.9 1.9 %collective-permute-start.2 = (bf16[8,2,16,640]{3,2,1,0:T(8,128)(2,1)S(1)}, bf16[8,2,16,640]{3,2,1,0:T(8,128)(2,1)S(1)}, u32[]{:S(2)}, u32[]{:S(2)}) collective-permute-start(bf16[8,2,16,640]{3,2,1,0:T(8,128)(2,1)S(1)} %get-tuple-element.9), channel_id=1, source_target_pairs={{0,1},{1,0},{2,3},{3,2},{4,5},{5,4},{6,7},{7,6},{8,9},{9,8},{10,11... | collective-permute-start | bytes 983048 | tf_op jit(solution)/shard_map/ppermute | solution.py:241
  61.9 2.4 %collective-permute-start.3 = (bf16[8,2,16,640]{3,2,1,0:T(8,128)(2,1)S(1)}, bf16[8,2,16,640]{3,2,1,0:T(8,128)(2,1)S(1)}, u32[]{:S(2)}, u32[]{:S(2)}) collective-permute-start(bf16[8,2,16,640]{3,2,1,0:T(8,128)(2,1)S(1)} %get-tuple-element.10), channel_id=1, source_target_pairs={{0,1},{1,0},{2,3},{3,2},{4,5},{5,4},{6,7},{7,6},{8,9},{9,8},{10,11... | collective-permute-start | bytes 983048 | tf_op jit(solution)/shard_map/ppermute | solution.py:241
  64.3 0.0 collective-permute-done.2.core_keys
  64.3 1.2 %collective-permute-done.3.core_values = bf16[8,2,16,640]{3,2,1,0:T(8,128)(2,1)S(1)} collective-permute-done((bf16[8,2,16,640]{3,2,1,0:T(8,128)(2,1)S(1)}, bf16[8,2,16,640]{3,2,1,0:T(8,128)(2,1)S(1)}, u32[]{:S(2)}, u32[]{:S(2)}) %collective-permute-start.3) | collective-permute-done | bytes 327712 | tf_op jit(solution)/shard_map/ppermute | solution.py:241
  65.5 8.8 %all-to-all-done.1.dq = bf16[16,16,640]{2,1,0:T(8,128)(2,1)S(1)} async-done(((bf16[16,16,640]{2,1,0:T(8,128)(2,1)}), bf16[16,16,640]{2,1,0:T(8,128)(2,1)S(1)}, u32[]{:S(2)}, u32[]{:S(2)}) %all-to-all-start.1) | async-done | bytes 327712 | tf_op jit(solution)/shard_map/all_to_all | solution.py:238
  74.3 0.2 pack_terms.1
  74.5 16.3 %all_to_all.15.terms = bf16[16,40,640]{2,1,0:T(8,128)(2,1)S(1)} all-to-all(bf16[16,40,640]{2,1,0:T(8,128)(2,1)S(1)} %pack_terms.1), channel_id=1, replica_groups=mesh['yl'=2,'x'=4,'zh'=4,'zl'=2,'yh'=4,'c'=2] {'yl','x','zl'}, dimensions={0} | all-to-all | bytes 1638400 | tf_op jit(solution)/shard_map/all_to_all | solution.py:251
  90.8 1.3 %unpack_terms.1 = (bf16[1,4,2560]{2,1,0:T(4,128)(2,1)}, bf16[1,16,2560]{2,1,0:T(8,128)(2,1)}, bf16[1,16,2560]{2,1,0:T(8,128)(2,1)}) custom-call(s32[7]{0:T(128)S(1)} %stack.36.place, bf16[16,40,640]{2,1,0:T(8,128)(2,1)S(1)} %all_to_all.15.terms), custom_call_target="tpu_custom_call" | custom-call | tf_op jit(solution)/shard_map/unpack_terms/pallas_call | solution.py:22
  (1 shorter events, 0.0 us)
Async XLA Ops:
  1.7 24.9 %collective-permute-start = (bf16[2,128,640]{2,1,0:T(8,128)(2,1)S(1)}, bf16[2,128,640]{2,1,0:T(8,128)(2,1)S(1)}, u32[]{:S(2)}, u32[]{:S(2)}) collective-permute-start(bf16[2,128,640]{2,1,0:T(8,128)(2,1)S(1)} %pad_maximum_fusion.kv_own), channel_id=1, source_target_pairs={{0,8},{8,0},{1,9},{9,1},{2,10},{10,2},{3,11},{11,3},{4,12},{12,4},... | collective-permute-start | bytes 983048 | tf_op jit(solution)/shard_map/ppermute | solution.py:197
  6.0 0.7 copy-start.4
  6.0 0.7 copy-start.2
  6.0 0.7 copy-start.1
  6.1 0.7 copy-start
  8.5 43.0 %all-to-all-start = ((bf16[64,4,1408]{2,1,0:T(4,128)(2,1)}), bf16[64,4,1408]{2,1,0:T(4,128)(2,1)S(1)}, u32[]{:S(2)}, u32[]{:S(2)}) async-start(bf16[64,4,1408]{2,1,0:T(4,128)(2,1)} %pack_rows.1), calls=%async_computation | async-start | bytes 1441792 | tf_op jit(solution)/shard_map/all_to_all | solution.py:220
  26.7 24.9 %copy-start.3 = (s32[8,64]{1,0:T(8,128)S(1)}, s32[8,64]{1,0:T(8,128)}, u32[]{:S(2)}) copy-start(s32[8,64]{1,0:T(8,128)} %ids.1) | copy-start | bytes 6148
  26.7 24.9 %copy-start.5 = (s32[8]{0:T(128)S(1)}, s32[8]{0:T(128)}, u32[]{:S(2)}) copy-start(s32[8]{0:T(128)} %amounts.1) | copy-start | bytes 100
  26.7 24.9 %collective-permute-start.1 = (bf16[2,2,128,640]{3,2,1,0:T(8,128)(2,1)S(1)}, bf16[2,2,128,640]{3,2,1,0:T(8,128)(2,1)S(1)}, u32[]{:S(2)}, u32[]{:S(2)}) collective-permute-start(bf16[2,2,128,640]{3,2,1,0:T(8,128)(2,1)S(1)} %pair_frames.1.kv_own), channel_id=1, source_target_pairs={{0,1},{1,0},{2,3},{3,2},{4,5},{5,4},{6,7},{7,6},{8,9},{9,8},{10,11... | collective-permute-start | bytes 1966088 | tf_op jit(solution)/shard_map/ppermute | solution.py:207
  55.0 19.3 %all-to-all-start.1 = ((bf16[16,16,640]{2,1,0:T(8,128)(2,1)}), bf16[16,16,640]{2,1,0:T(8,128)(2,1)S(1)}, u32[]{:S(2)}, u32[]{:S(2)}) async-start(bf16[16,16,640]{2,1,0:T(8,128)(2,1)} %bitcast.7), calls=%async_computation.1 | async-start | bytes 655360 | tf_op jit(solution)/shard_map/all_to_all | solution.py:238
  59.9 4.3 %collective-permute-start.2 = (bf16[8,2,16,640]{3,2,1,0:T(8,128)(2,1)S(1)}, bf16[8,2,16,640]{3,2,1,0:T(8,128)(2,1)S(1)}, u32[]{:S(2)}, u32[]{:S(2)}) collective-permute-start(bf16[8,2,16,640]{3,2,1,0:T(8,128)(2,1)S(1)} %get-tuple-element.9), channel_id=1, source_target_pairs={{0,1},{1,0},{2,3},{3,2},{4,5},{5,4},{6,7},{7,6},{8,9},{9,8},{10,11... | collective-permute-start | bytes 983048 | tf_op jit(solution)/shard_map/ppermute | solution.py:241
  61.9 3.6 %collective-permute-start.3 = (bf16[8,2,16,640]{3,2,1,0:T(8,128)(2,1)S(1)}, bf16[8,2,16,640]{3,2,1,0:T(8,128)(2,1)S(1)}, u32[]{:S(2)}, u32[]{:S(2)}) collective-permute-start(bf16[8,2,16,640]{3,2,1,0:T(8,128)(2,1)S(1)} %get-tuple-element.10), channel_id=1, source_target_pairs={{0,1},{1,0},{2,3},{3,2},{4,5},{5,4},{6,7},{7,6},{8,9},{9,8},{10,11... | collective-permute-start | bytes 983048 | tf_op jit(solution)/shard_map/ppermute | solution.py:241

commit v7 on v6

--- a/solution.py
+++ b/solution.py
@@ -74,9 +74,10 @@
     for f in range(ids.shape[0]):
         limit = jnp.where(frame == f, amounts[f], limit)
     listed = entry < limit
-    row8 = lax.broadcasted_iota(jnp.int32, (ids.shape[0], LANES), 0) - place[1] * GROUPS
+    row8 = lax.broadcasted_iota(jnp.int32, (ids.shape[0], LANES), 0)
     lane8 = lax.broadcasted_iota(jnp.int32, (ids.shape[0], LANES), 1)
-    spot = (lane8 == 4 * heads + row8) & (row8 >= 0) & (row8 < GROUPS)
+    slot = (row8 >> 2) * 2 + (row8 & 1)
+    spot = (lane8 == 4 * heads + slot) & (((row8 >> 1) & 1) == place[1])
     biases = []
     for d in range(4):
         hit = jnp.where((ids[...] == place[2 + d]) & listed, 1.0, 0.0)
@@ -144,27 +145,28 @@
             for kind, other in enumerate((core_keys, core_values)):
                 total = near[b, z, kind].astype(F32) + other[b, z].astype(F32)
                 out[2 * b + z, kind * share : (kind + 1) * share] = total.astype(BF16)
-            out[2 * b + z, 2 * share :] = tails[b % GROUPS]
+            out[2 * b + z, 2 * share :] = tails[b // 4 * 2 + b % 2]
 
 
 def unpack_terms(place, terms, grad_queries, grad_keys, grad_values):
     share, tokens = grad_keys.shape[1], grad_queries.shape[1]
     width = terms.shape[2]
-    for x in range(GROUPS):
-        cols = slice(x * width, (x + 1) * width)
-        sources = [s for s in range(terms.shape[0]) if s // 2 % GROUPS == x]
+    for group in range(GROUPS):
+        cols = slice(group * width, (group + 1) * width)
+        first = group // 2 * 8 + group % 2 * 2
+        sources = [first + 4 * x + z for x in range(2) for z in range(2)]
         for kind, out in enumerate((grad_keys, grad_values)):
             part = slice(kind * share, (kind + 1) * share)
             total = terms[sources[0], part].astype(F32)
             for s in sources[1:]:
                 total = total + terms[s, part].astype(F32)
             out[0, :, cols] = total.astype(BF16)
-        mine = terms[(place[1] * GROUPS + x) * 2 + place[6], 2 * share :].astype(F32)
+        mine = terms[first + 4 * place[1] + place[6], 2 * share :].astype(F32)
         grad_queries[0, :, cols] = mine[:tokens].astype(BF16)
 
 
 def on_device(sizes, queries, grad_out, attn_out, lse, keys, values, frame_ids, counts):
-    low_y, x, high_z = (lax.axis_index(a) for a in ("yl", "x", "zh"))
+    low_y, high_x, low_x, high_z = (lax.axis_index(a) for a in ("yl", "xh", "xl", "zh"))
     low_z, high_y, core = (lax.axis_index(a) for a in ("zl", "yh", "c"))
     tokens_here = queries.shape[1]
     heads = lse.shape[2] // GROUPS
@@ -172,16 +174,18 @@
     frame_tokens = keys.shape[1]
     spread = sizes["zh"] * sizes["yh"]
     members = GROUPS * spread
-    blocks_q = sizes["yl"] * sizes["x"]
+    blocks_q = sizes["yl"] * sizes["xh"] * sizes["xl"]
     share = frame_tokens // blocks_q
+
+    group = low_y * 2 + low_x
 
     def memory_frame(z, c):
         return ((high_z * 2 + z) * sizes["yh"] + high_y) * 2 + c
 
     place = jnp.stack(
         [
-            x,
-            low_y,
+            group,
+            high_x,
             memory_frame(low_z, core),
             memory_frame(low_z, 1 - core),
             memory_frame(1 - low_z, core),
@@ -192,7 +196,7 @@
 
     flip = [(0, 1), (1, 0)]
     kv = jnp.stack(
-        [lax.dynamic_slice_in_dim(a[0], x * width, width, 1) for a in (keys, values)]
+        [lax.dynamic_slice_in_dim(a[0], group * width, width, 1) for a in (keys, values)]
     )
     kv_z = lax.ppermute(kv, "zl", flip)
     kv_own = call(
@@ -217,7 +221,7 @@
         attn_out,
         lse,
     )
-    rows = lax.all_to_all(packed, ("zh", "yh", "x"), 0, 0, tiled=True)
+    rows = lax.all_to_all(packed, ("zh", "yh", "yl", "xl"), 0, 0, tiled=True)
     rows = rows.reshape(members * tokens_here, -1)
 
     part = jax.ShapeDtypeStruct((blocks_q, 2, 2, share, width), BF16)
@@ -248,7 +252,7 @@
         near,
         *from_core,
     )
-    terms = lax.all_to_all(terms, ("yl", "x", "zl"), 0, 0, tiled=True)
+    terms = lax.all_to_all(terms, ("yl", "xh", "xl", "zl"), 0, 0, tiled=True)
     return call(
         unpack_terms,
         "unpack_terms",
@@ -265,11 +269,11 @@
 
 def solution(mesh):
     query, mem = mesh.shape["query"], mesh.shape["mem"]
-    sizes = {"yl": query // GROUPS, "x": GROUPS, "zh": mem // 16, "zl": 2, "yh": 4, "c": 2}
+    sizes = {"yl": query // 4, "xh": 2, "xl": 2, "zh": mem // 16, "zl": 2, "yh": 4, "c": 2}
     if mem < 16:
         sizes.update(zh=1, yh=mem // 4)
     fine = Mesh(mesh.devices.reshape(tuple(sizes.values())), tuple(sizes))
-    q_axes, m_axes = ("yl", "x"), ("zh", "zl", "yh", "c")
+    q_axes, m_axes = ("yl", "xh", "xl"), ("zh", "zl", "yh", "c")
     rows = P(q_axes, m_axes, None)
     frames = P(m_axes, None, None)
     return jax.shard_map(

time: 93.6 us -> 89.1 us (0.952)
  waiting for transfers between devices: 32.8 us -> 30.1 us
  blocking collectives: 16.3 us -> 15.3 us
    all_to_all x1, waiting for transfers between devices: 22.8 us -> 19.9 us  [on_device(): rows = lax.all_to_all(packed, ('zh', 'yh', 'yl', 'xl'), 0, 0, tiled=True)]
    all_to_all x1, starting transfers between devices: 18.2 us -> 16.7 us  [on_device(): rows = lax.all_to_all(packed, ('zh', 'yh', 'yl', 'xl'), 0, 0, tiled=True)]
    all_to_all x1, starting transfers between devices: 4.94 us -> 5.89 us  [on_device(): lax.all_to_all(dq.reshape(spread, GROUPS * tokens_here, width), ('zh', 'y...]
    all_to_all x1, blocking collectives: 16.3 us -> 15.3 us  [on_device(): terms = lax.all_to_all(terms, ('yl', 'xh', 'xl', 'zl'), 0, 0, tiled=True)]
where the time goes in v7:
time: 89.1 us; the launch traced here: 87.8 us
  starting transfers between devices  33.1 us (37%)
  waiting for transfers between devices  30.1 us (34%)
  blocking collectives  15.3 us (17%)
  Pallas kernels  6.52 us (7%)
  local copies, waits for them, and re-layouts  1.94 us (2%)
    all_to_all x1, waiting for transfers between devices, on_device(): rows = lax.all_to_all(packed, ('zh', 'yh', 'yl', 'xl'), 0, 0, tiled=True)  19.9 us
    all_to_all x1, starting transfers between devices, on_device(): rows = lax.all_to_all(packed, ('zh', 'yh', 'yl', 'xl'), 0, 0, tiled=True)  16.7 us
    all_to_all x1, blocking collectives, on_device(): terms = lax.all_to_all(terms, ('yl', 'xh', 'xl', 'zl'), 0, 0, tiled=True)  15.3 us
    all_to_all x1, waiting for transfers between devices, on_device(): lax.all_to_all(dq.reshape(spread, GROUPS * tokens_here, width), ('zh', 'y...  8.9 us
    pallas_call x5, Pallas kernels, call(): pl.pallas_call(body, out_shape=out_shape, in_specs=in_specs, cost_estimat...  6.52 us
    all_to_all x1, starting transfers between devices, on_device(): lax.all_to_all(dq.reshape(spread, GROUPS * tokens_here, width), ('zh', 'y...  5.89 us
    ppermute x2, starting transfers between devices, on_device(): from_core = [lax.ppermute(a, 'c', flip) for a in far]  4.33 us
    ppermute x1, starting transfers between devices, on_device(): kv_z = lax.ppermute(kv, 'zl', flip)  4.28 us
  transfers between devices with their start and end apart: 6, of which 3 were waited for; matrix products, arithmetic and copies ran while one was open for 0% of the time, Pallas kernels for 2%

profile of v7, /device:TPU:6, one launch (start us, length us, event | category | flops | bytes accessed | tf_op | source)
XLA Modules:
  0.0 87.8 jit_solution(386582250767930061)
XLA Ops:
  0.6 1.0 %constant_dynamic-slice_fusion = (bf16[1,128,640]{2,1,0:T(8,128)(2,1)S(1)}, bf16[1,128,640]{2,1,0:T(8,128)(2,1)S(1)}) fusion(bf16[1,128,2560]{2,1,0:T(8,128)(2,1)} %param.13, s32[]{:T(128)S(6)} %select_n.4, bf16[1,128,2560]{2,1,0:T(8,128)(2,1)} %param.12), kind=kLoop, calls=%fused_computation.1 | loop fusion | bytes 655364 | tf_op jit(solution)/shard_map/dynamic_slice | solution.py:199
  1.7 4.3 %collective-permute-start = (bf16[2,128,640]{2,1,0:T(8,128)(2,1)S(1)}, bf16[2,128,640]{2,1,0:T(8,128)(2,1)S(1)}, u32[]{:S(2)}, u32[]{:S(2)}) collective-permute-start(bf16[2,128,640]{2,1,0:T(8,128)(2,1)S(1)} %pad_maximum_fusion.kv_own), channel_id=1, source_target_pairs={{0,8},{8,0},{1,9},{9,1},{2,10},{10,2},{3,11},{11,3},{4,12},{12,4},... | collective-permute-start | bytes 983048 | tf_op jit(solution)/shard_map/ppermute | solution.py:201
  6.0 0.0 copy-start.4
  6.0 0.0 copy-start.2
  6.0 0.0 copy-start.1
  6.1 0.0 copy-start
  6.1 0.1 stack.36.place
  6.2 0.5 copy-done.4
  6.7 0.1 copy-done.2
  6.8 0.0 copy-done.1
  6.8 0.0 copy-done
  6.8 1.7 %pack_rows.1 = bf16[64,4,1408]{2,1,0:T(4,128)(2,1)} custom-call(s32[7]{0:T(128)S(1)} %stack.36.place, bf16[1,4,2560]{2,1,0:T(4,128)(2,1)S(1)} %copy-done, bf16[1,4,2560]{2,1,0:T(4,128)(2,1)S(1)} %copy-done.1, bf16[1,4,2560]{2,1,0:T(4,128)(2,1)S(1)} %copy-done.2, f32[1,4,20]{2,1,0:T(4,128)S(1)} %copy-done.4), custom_call_target="tpu_custom_call" | custom-call | tf_op jit(solution)/shard_map/pack_rows/pallas_call | solution.py:22
  8.5 16.7 %all-to-all-start = ((bf16[64,4,1408]{2,1,0:T(4,128)(2,1)}), bf16[64,4,1408]{2,1,0:T(4,128)(2,1)S(1)}, u32[]{:S(2)}, u32[]{:S(2)}) async-start(bf16[64,4,1408]{2,1,0:T(4,128)(2,1)} %pack_rows.1), calls=%async_computation | async-start | bytes 1441792 | tf_op jit(solution)/shard_map/all_to_all | solution.py:224
  25.2 0.0 collective-permute-done.kv_z
  25.2 0.1 pair_frames.1.kv_own
  25.2 0.0 copy-start.3
  25.3 0.0 copy-start.5
  25.3 1.9 %collective-permute-start.1 = (bf16[2,2,128,640]{3,2,1,0:T(8,128)(2,1)S(1)}, bf16[2,2,128,640]{3,2,1,0:T(8,128)(2,1)S(1)}, u32[]{:S(2)}, u32[]{:S(2)}) collective-permute-start(bf16[2,2,128,640]{3,2,1,0:T(8,128)(2,1)S(1)} %pair_frames.1.kv_own), channel_id=1, source_target_pairs={{0,1},{1,0},{2,3},{3,2},{4,5},{5,4},{6,7},{7,6},{8,9},{9,8},{10,11... | collective-permute-start | bytes 1966088 | tf_op jit(solution)/shard_map/ppermute | solution.py:211
  27.2 19.9 %all-to-all-done = bf16[64,4,1408]{2,1,0:T(4,128)(2,1)S(1)} async-done(((bf16[64,4,1408]{2,1,0:T(4,128)(2,1)}), bf16[64,4,1408]{2,1,0:T(4,128)(2,1)S(1)}, u32[]{:S(2)}, u32[]{:S(2)}) %all-to-all-start) | async-done | bytes 720928 | tf_op jit(solution)/shard_map/all_to_all | solution.py:224
  47.1 0.2 reshape.16.rows
  47.3 0.0 collective-permute-done.1.kv_core
  47.3 0.0 copy-done.3
  47.3 0.0 copy-done.5
  47.3 3.3 %attention_grads.1 = (bf16[256,640]{1,0:T(8,128)(2,1)}, bf16[8,2,2,16,640]{4,3,2,1,0:T(8,128)(2,1)S(1)}, bf16[8,2,16,640]{3,2,1,0:T(8,128)(2,1)S(1)}, bf16[8,2,16,640]{3,2,1,0:T(8,128)(2,1)S(1)}) custom-call(s32[7]{0:T(128)S(1)} %stack.36.place, s32[8]{0:T(128)S(1)} %copy-done.5, s32[8,64]{1,0:T(8,128)S(1)} %copy-done.3, ...), custom_call_target="tpu_custom_call" | custom-call | tf_op jit(solution)/shard_map/attention_grads/pallas_call | solution.py:22
  50.7 5.9 %all-to-all-start.1 = ((bf16[16,16,640]{2,1,0:T(8,128)(2,1)}), bf16[16,16,640]{2,1,0:T(8,128)(2,1)S(1)}, u32[]{:S(2)}, u32[]{:S(2)}) async-start(bf16[16,16,640]{2,1,0:T(8,128)(2,1)} %bitcast.7), calls=%async_computation.1 | async-start | bytes 655360 | tf_op jit(solution)/shard_map/all_to_all | solution.py:242
  56.6 1.9 %collective-permute-start.2 = (bf16[8,2,16,640]{3,2,1,0:T(8,128)(2,1)S(1)}, bf16[8,2,16,640]{3,2,1,0:T(8,128)(2,1)S(1)}, u32[]{:S(2)}, u32[]{:S(2)}) collective-permute-start(bf16[8,2,16,640]{3,2,1,0:T(8,128)(2,1)S(1)} %get-tuple-element.9), channel_id=1, source_target_pairs={{0,1},{1,0},{2,3},{3,2},{4,5},{5,4},{6,7},{7,6},{8,9},{9,8},{10,11... | collective-permute-start | bytes 983048 | tf_op jit(solution)/shard_map/ppermute | solution.py:245
  58.5 2.4 %collective-permute-start.3 = (bf16[8,2,16,640]{3,2,1,0:T(8,128)(2,1)S(1)}, bf16[8,2,16,640]{3,2,1,0:T(8,128)(2,1)S(1)}, u32[]{:S(2)}, u32[]{:S(2)}) collective-permute-start(bf16[8,2,16,640]{3,2,1,0:T(8,128)(2,1)S(1)} %get-tuple-element.10), channel_id=1, source_target_pairs={{0,1},{1,0},{2,3},{3,2},{4,5},{5,4},{6,7},{7,6},{8,9},{9,8},{10,11... | collective-permute-start | bytes 983048 | tf_op jit(solution)/shard_map/ppermute | solution.py:245
  60.9 0.0 collective-permute-done.2.core_keys
  60.9 1.2 %collective-permute-done.3.core_values = bf16[8,2,16,640]{3,2,1,0:T(8,128)(2,1)S(1)} collective-permute-done((bf16[8,2,16,640]{3,2,1,0:T(8,128)(2,1)S(1)}, bf16[8,2,16,640]{3,2,1,0:T(8,128)(2,1)S(1)}, u32[]{:S(2)}, u32[]{:S(2)}) %collective-permute-start.3) | collective-permute-done | bytes 327712 | tf_op jit(solution)/shard_map/ppermute | solution.py:245
  62.1 8.9 %all-to-all-done.1.dq = bf16[16,16,640]{2,1,0:T(8,128)(2,1)S(1)} async-done(((bf16[16,16,640]{2,1,0:T(8,128)(2,1)}), bf16[16,16,640]{2,1,0:T(8,128)(2,1)S(1)}, u32[]{:S(2)}, u32[]{:S(2)}) %all-to-all-start.1) | async-done | bytes 327712 | tf_op jit(solution)/shard_map/all_to_all | solution.py:242
  71.0 0.2 pack_terms.1
  71.2 15.3 %all_to_all.15.terms = bf16[16,40,640]{2,1,0:T(8,128)(2,1)S(1)} all-to-all(bf16[16,40,640]{2,1,0:T(8,128)(2,1)S(1)} %pack_terms.1), channel_id=1, replica_groups=mesh['yl'=2,'xh'=2,'xl'=2,'zh'=4,'zl'=2,'yh'=4,'c'=2] {'yl','xh','xl','zl'}, dimensions={0} | all-to-all | bytes 1638400 | tf_op jit(solution)/shard_map/all_to_all | solution.py:255
  86.6 1.3 %unpack_terms.1 = (bf16[1,4,2560]{2,1,0:T(4,128)(2,1)}, bf16[1,16,2560]{2,1,0:T(8,128)(2,1)}, bf16[1,16,2560]{2,1,0:T(8,128)(2,1)}) custom-call(s32[7]{0:T(128)S(1)} %stack.36.place, bf16[16,40,640]{2,1,0:T(8,128)(2,1)S(1)} %all_to_all.15.terms), custom_call_target="tpu_custom_call" | custom-call | tf_op jit(solution)/shard_map/unpack_terms/pallas_call | solution.py:22
  (1 shorter events, 0.0 us)
Async XLA Ops:
  1.7 23.5 %collective-permute-start = (bf16[2,128,640]{2,1,0:T(8,128)(2,1)S(1)}, bf16[2,128,640]{2,1,0:T(8,128)(2,1)S(1)}, u32[]{:S(2)}, u32[]{:S(2)}) collective-permute-start(bf16[2,128,640]{2,1,0:T(8,128)(2,1)S(1)} %pad_maximum_fusion.kv_own), channel_id=1, source_target_pairs={{0,8},{8,0},{1,9},{9,1},{2,10},{10,2},{3,11},{11,3},{4,12},{12,4},... | collective-permute-start | bytes 983048 | tf_op jit(solution)/shard_map/ppermute | solution.py:201
  6.0 0.7 copy-start.4
  6.0 0.7 copy-start.2
  6.0 0.7 copy-start.1
  6.1 0.7 copy-start
  8.5 38.7 %all-to-all-start = ((bf16[64,4,1408]{2,1,0:T(4,128)(2,1)}), bf16[64,4,1408]{2,1,0:T(4,128)(2,1)S(1)}, u32[]{:S(2)}, u32[]{:S(2)}) async-start(bf16[64,4,1408]{2,1,0:T(4,128)(2,1)} %pack_rows.1), calls=%async_computation | async-start | bytes 1441792 | tf_op jit(solution)/shard_map/all_to_all | solution.py:224
  25.2 22.1 %copy-start.3 = (s32[8,64]{1,0:T(8,128)S(1)}, s32[8,64]{1,0:T(8,128)}, u32[]{:S(2)}) copy-start(s32[8,64]{1,0:T(8,128)} %ids.1) | copy-start | bytes 6148
  25.3 22.1 %copy-start.5 = (s32[8]{0:T(128)S(1)}, s32[8]{0:T(128)}, u32[]{:S(2)}) copy-start(s32[8]{0:T(128)} %amounts.1) | copy-start | bytes 100
  25.3 22.0 %collective-permute-start.1 = (bf16[2,2,128,640]{3,2,1,0:T(8,128)(2,1)S(1)}, bf16[2,2,128,640]{3,2,1,0:T(8,128)(2,1)S(1)}, u32[]{:S(2)}, u32[]{:S(2)}) collective-permute-start(bf16[2,2,128,640]{3,2,1,0:T(8,128)(2,1)S(1)} %pair_frames.1.kv_own), channel_id=1, source_target_pairs={{0,1},{1,0},{2,3},{3,2},{4,5},{5,4},{6,7},{7,6},{8,9},{9,8},{10,11... | collective-permute-start | bytes 1966088 | tf_op jit(solution)/shard_map/ppermute | solution.py:211
  50.7 20.4 %all-to-all-start.1 = ((bf16[16,16,640]{2,1,0:T(8,128)(2,1)}), bf16[16,16,640]{2,1,0:T(8,128)(2,1)S(1)}, u32[]{:S(2)}, u32[]{:S(2)}) async-start(bf16[16,16,640]{2,1,0:T(8,128)(2,1)} %bitcast.7), calls=%async_computation.1 | async-start | bytes 655360 | tf_op jit(solution)/shard_map/all_to_all | solution.py:242
  56.6 4.3 %collective-permute-start.2 = (bf16[8,2,16,640]{3,2,1,0:T(8,128)(2,1)S(1)}, bf16[8,2,16,640]{3,2,1,0:T(8,128)(2,1)S(1)}, u32[]{:S(2)}, u32[]{:S(2)}) collective-permute-start(bf16[8,2,16,640]{3,2,1,0:T(8,128)(2,1)S(1)} %get-tuple-element.9), channel_id=1, source_target_pairs={{0,1},{1,0},{2,3},{3,2},{4,5},{5,4},{6,7},{7,6},{8,9},{9,8},{10,11... | collective-permute-start | bytes 983048 | tf_op jit(solution)/shard_map/ppermute | solution.py:245
  58.5 3.6 %collective-permute-start.3 = (bf16[8,2,16,640]{3,2,1,0:T(8,128)(2,1)S(1)}, bf16[8,2,16,640]{3,2,1,0:T(8,128)(2,1)S(1)}, u32[]{:S(2)}, u32[]{:S(2)}) collective-permute-start(bf16[8,2,16,640]{3,2,1,0:T(8,128)(2,1)S(1)} %get-tuple-element.10), channel_id=1, source_target_pairs={{0,1},{1,0},{2,3},{3,2},{4,5},{5,4},{6,7},{7,6},{8,9},{9,8},{10,11... | collective-permute-start | bytes 983048 | tf_op jit(solution)/shard_map/ppermute | solution.py:245

commit v8 on v7

--- a/solution.py
+++ b/solution.py
@@ -83,9 +83,8 @@
         hit = jnp.where((ids[...] == place[2 + d]) & listed, 1.0, 0.0)
         found = jnp.max(hit, axis=1, keepdims=True)
         bias = jnp.sum(jnp.where(spot, (1.0 - found) * MASKED, 0.0), axis=0, keepdims=True)
-        biases.append(jnp.broadcast_to(bias, (tokens, LANES)))
-    bias_all = jnp.concatenate(biases, axis=0)
-    lane = lax.broadcasted_iota(jnp.int32, bias_all.shape, 1)
+        biases.append(bias)
+    lane = lax.broadcasted_iota(jnp.int32, (1, LANES), 1)
     extra = rows[:, 2 * width :]
 
     for h in range(heads):
@@ -94,8 +93,12 @@
         g = rows[:, width + h * HS : width + (h + 1) * HS]
         k = jnp.concatenate([b[0, :, cols] for b in blocks], axis=0)
         v = jnp.concatenate([b[1, :, cols] for b in blocks], axis=0)
-        k_pick = jnp.where((lane == h) | (lane == heads + h), -1.0, bias_all).astype(BF16)
-        v_pick = jnp.where((lane == 2 * heads + h) | (lane == 3 * heads + h), -1.0, 0.0).astype(BF16)
+        k_rows = [jnp.where((lane == h) | (lane == heads + h), -1.0, b) for b in biases]
+        k_pick = jnp.concatenate(
+            [jnp.broadcast_to(r.astype(BF16), (tokens, LANES)) for r in k_rows], axis=0
+        )
+        v_row = jnp.where((lane == 2 * heads + h) | (lane == 3 * heads + h), -1.0, 0.0)
+        v_pick = jnp.broadcast_to(v_row.astype(BF16), k_pick.shape)
         contract = (((1,), (1,)), ((), ()))
         scores = lax.dot_general(
             jnp.concatenate([k, k_pick], axis=1),

time: 89.1 us -> 89.1 us (level)
  no operation moved by 1% of the time
where the time goes in v8:
time: 89.1 us; the launch traced here: 87.8 us
  starting transfers between devices  33.1 us (37%)
  waiting for transfers between devices  30.1 us (34%)
  blocking collectives  15.3 us (17%)
  Pallas kernels  6.52 us (7%)
  local copies, waits for them, and re-layouts  1.94 us (2%)
    all_to_all x1, waiting for transfers between devices, on_device(): rows = lax.all_to_all(packed, ('zh', 'yh', 'yl', 'xl'), 0, 0, tiled=True)  19.9 us
    all_to_all x1, starting transfers between devices, on_device(): rows = lax.all_to_all(packed, ('zh', 'yh', 'yl', 'xl'), 0, 0, tiled=True)  16.7 us
    all_to_all x1, blocking collectives, on_device(): terms = lax.all_to_all(terms, ('yl', 'xh', 'xl', 'zl'), 0, 0, tiled=True)  15.3 us
    all_to_all x1, waiting for transfers between devices, on_device(): lax.all_to_all(dq.reshape(spread, GROUPS * tokens_here, width), ('zh', 'y...  8.9 us
    pallas_call x5, Pallas kernels, call(): pl.pallas_call(body, out_shape=out_shape, in_specs=in_specs, cost_estimat...  6.52 us
    all_to_all x1, starting transfers between devices, on_device(): lax.all_to_all(dq.reshape(spread, GROUPS * tokens_here, width), ('zh', 'y...  5.89 us
    ppermute x2, starting transfers between devices, on_device(): from_core = [lax.ppermute(a, 'c', flip) for a in far]  4.33 us
    ppermute x1, starting transfers between devices, on_device(): kv_z = lax.ppermute(kv, 'zl', flip)  4.28 us
  transfers between devices with their start and end apart: 6, of which 3 were waited for; matrix products, arithmetic and copies ran while one was open for 0% of the time, Pallas kernels for 2%

profile of v8, /device:TPU:6, one launch (start us, length us, event | category | flops | bytes accessed | tf_op | source)
XLA Modules:
  0.0 87.8 jit_solution(386582250767930061)
XLA Ops:
  0.6 1.0 %constant_dynamic-slice_fusion = (bf16[1,128,640]{2,1,0:T(8,128)(2,1)S(1)}, bf16[1,128,640]{2,1,0:T(8,128)(2,1)S(1)}) fusion(bf16[1,128,2560]{2,1,0:T(8,128)(2,1)} %param.13, s32[]{:T(128)S(6)} %select_n.4, bf16[1,128,2560]{2,1,0:T(8,128)(2,1)} %param.12), kind=kLoop, calls=%fused_computation.1 | loop fusion | bytes 655364 | tf_op jit(solution)/shard_map/dynamic_slice | solution.py:202
  1.7 4.3 %collective-permute-start = (bf16[2,128,640]{2,1,0:T(8,128)(2,1)S(1)}, bf16[2,128,640]{2,1,0:T(8,128)(2,1)S(1)}, u32[]{:S(2)}, u32[]{:S(2)}) collective-permute-start(bf16[2,128,640]{2,1,0:T(8,128)(2,1)S(1)} %pad_maximum_fusion.kv_own), channel_id=1, source_target_pairs={{0,8},{8,0},{1,9},{9,1},{2,10},{10,2},{3,11},{11,3},{4,12},{12,4},... | collective-permute-start | bytes 983048 | tf_op jit(solution)/shard_map/ppermute | solution.py:204
  6.0 0.0 copy-start.4
  6.0 0.0 copy-start.2
  6.0 0.0 copy-start.1
  6.1 0.0 copy-start
  6.1 0.1 stack.36.place
  6.2 0.5 copy-done.4
  6.7 0.1 copy-done.2
  6.8 0.0 copy-done.1
  6.8 0.0 copy-done
  6.8 1.7 %pack_rows.1 = bf16[64,4,1408]{2,1,0:T(4,128)(2,1)} custom-call(s32[7]{0:T(128)S(1)} %stack.36.place, bf16[1,4,2560]{2,1,0:T(4,128)(2,1)S(1)} %copy-done, bf16[1,4,2560]{2,1,0:T(4,128)(2,1)S(1)} %copy-done.1, bf16[1,4,2560]{2,1,0:T(4,128)(2,1)S(1)} %copy-done.2, f32[1,4,20]{2,1,0:T(4,128)S(1)} %copy-done.4), custom_call_target="tpu_custom_call" | custom-call | tf_op jit(solution)/shard_map/pack_rows/pallas_call | solution.py:22
  8.5 16.7 %all-to-all-start = ((bf16[64,4,1408]{2,1,0:T(4,128)(2,1)}), bf16[64,4,1408]{2,1,0:T(4,128)(2,1)S(1)}, u32[]{:S(2)}, u32[]{:S(2)}) async-start(bf16[64,4,1408]{2,1,0:T(4,128)(2,1)} %pack_rows.1), calls=%async_computation | async-start | bytes 1441792 | tf_op jit(solution)/shard_map/all_to_all | solution.py:227
  25.2 0.0 collective-permute-done.kv_z
  25.2 0.1 pair_frames.1.kv_own
  25.2 0.0 copy-start.3
  25.3 0.0 copy-start.5
  25.3 1.9 %collective-permute-start.1 = (bf16[2,2,128,640]{3,2,1,0:T(8,128)(2,1)S(1)}, bf16[2,2,128,640]{3,2,1,0:T(8,128)(2,1)S(1)}, u32[]{:S(2)}, u32[]{:S(2)}) collective-permute-start(bf16[2,2,128,640]{3,2,1,0:T(8,128)(2,1)S(1)} %pair_frames.1.kv_own), channel_id=1, source_target_pairs={{0,1},{1,0},{2,3},{3,2},{4,5},{5,4},{6,7},{7,6},{8,9},{9,8},{10,11... | collective-permute-start | bytes 1966088 | tf_op jit(solution)/shard_map/ppermute | solution.py:214
  27.2 19.9 %all-to-all-done = bf16[64,4,1408]{2,1,0:T(4,128)(2,1)S(1)} async-done(((bf16[64,4,1408]{2,1,0:T(4,128)(2,1)}), bf16[64,4,1408]{2,1,0:T(4,128)(2,1)S(1)}, u32[]{:S(2)}, u32[]{:S(2)}) %all-to-all-start) | async-done | bytes 720928 | tf_op jit(solution)/shard_map/all_to_all | solution.py:227
  47.1 0.2 reshape.16.rows
  47.3 0.0 collective-permute-done.1.kv_core
  47.3 0.0 copy-done.3
  47.3 0.0 copy-done.5
  47.3 3.3 %attention_grads.1 = (bf16[256,640]{1,0:T(8,128)(2,1)}, bf16[8,2,2,16,640]{4,3,2,1,0:T(8,128)(2,1)S(1)}, bf16[8,2,16,640]{3,2,1,0:T(8,128)(2,1)S(1)}, bf16[8,2,16,640]{3,2,1,0:T(8,128)(2,1)S(1)}) custom-call(s32[7]{0:T(128)S(1)} %stack.36.place, s32[8]{0:T(128)S(1)} %copy-done.5, s32[8,64]{1,0:T(8,128)S(1)} %copy-done.3, ...), custom_call_target="tpu_custom_call" | custom-call | tf_op jit(solution)/shard_map/attention_grads/pallas_call | solution.py:22
  50.7 5.9 %all-to-all-start.1 = ((bf16[16,16,640]{2,1,0:T(8,128)(2,1)}), bf16[16,16,640]{2,1,0:T(8,128)(2,1)S(1)}, u32[]{:S(2)}, u32[]{:S(2)}) async-start(bf16[16,16,640]{2,1,0:T(8,128)(2,1)} %bitcast.7), calls=%async_computation.1 | async-start | bytes 655360 | tf_op jit(solution)/shard_map/all_to_all | solution.py:245
  56.6 1.9 %collective-permute-start.2 = (bf16[8,2,16,640]{3,2,1,0:T(8,128)(2,1)S(1)}, bf16[8,2,16,640]{3,2,1,0:T(8,128)(2,1)S(1)}, u32[]{:S(2)}, u32[]{:S(2)}) collective-permute-start(bf16[8,2,16,640]{3,2,1,0:T(8,128)(2,1)S(1)} %get-tuple-element.9), channel_id=1, source_target_pairs={{0,1},{1,0},{2,3},{3,2},{4,5},{5,4},{6,7},{7,6},{8,9},{9,8},{10,11... | collective-permute-start | bytes 983048 | tf_op jit(solution)/shard_map/ppermute | solution.py:248
  58.5 2.4 %collective-permute-start.3 = (bf16[8,2,16,640]{3,2,1,0:T(8,128)(2,1)S(1)}, bf16[8,2,16,640]{3,2,1,0:T(8,128)(2,1)S(1)}, u32[]{:S(2)}, u32[]{:S(2)}) collective-permute-start(bf16[8,2,16,640]{3,2,1,0:T(8,128)(2,1)S(1)} %get-tuple-element.10), channel_id=1, source_target_pairs={{0,1},{1,0},{2,3},{3,2},{4,5},{5,4},{6,7},{7,6},{8,9},{9,8},{10,11... | collective-permute-start | bytes 983048 | tf_op jit(solution)/shard_map/ppermute | solution.py:248
  60.9 0.0 collective-permute-done.2.core_keys
  60.9 1.2 %collective-permute-done.3.core_values = bf16[8,2,16,640]{3,2,1,0:T(8,128)(2,1)S(1)} collective-permute-done((bf16[8,2,16,640]{3,2,1,0:T(8,128)(2,1)S(1)}, bf16[8,2,16,640]{3,2,1,0:T(8,128)(2,1)S(1)}, u32[]{:S(2)}, u32[]{:S(2)}) %collective-permute-start.3) | collective-permute-done | bytes 327712 | tf_op jit(solution)/shard_map/ppermute | solution.py:248
  62.1 8.9 %all-to-all-done.1.dq = bf16[16,16,640]{2,1,0:T(8,128)(2,1)S(1)} async-done(((bf16[16,16,640]{2,1,0:T(8,128)(2,1)}), bf16[16,16,640]{2,1,0:T(8,128)(2,1)S(1)}, u32[]{:S(2)}, u32[]{:S(2)}) %all-to-all-start.1) | async-done | bytes 327712 | tf_op jit(solution)/shard_map/all_to_all | solution.py:245
  71.0 0.2 pack_terms.1
  71.2 15.3 %all_to_all.15.terms = bf16[16,40,640]{2,1,0:T(8,128)(2,1)S(1)} all-to-all(bf16[16,40,640]{2,1,0:T(8,128)(2,1)S(1)} %pack_terms.1), channel_id=1, replica_groups=mesh['yl'=2,'xh'=2,'xl'=2,'zh'=4,'zl'=2,'yh'=4,'c'=2] {'yl','xh','xl','zl'}, dimensions={0} | all-to-all | bytes 1638400 | tf_op jit(solution)/shard_map/all_to_all | solution.py:258
  86.6 1.3 %unpack_terms.1 = (bf16[1,4,2560]{2,1,0:T(4,128)(2,1)}, bf16[1,16,2560]{2,1,0:T(8,128)(2,1)}, bf16[1,16,2560]{2,1,0:T(8,128)(2,1)}) custom-call(s32[7]{0:T(128)S(1)} %stack.36.place, bf16[16,40,640]{2,1,0:T(8,128)(2,1)S(1)} %all_to_all.15.terms), custom_call_target="tpu_custom_call" | custom-call | tf_op jit(solution)/shard_map/unpack_terms/pallas_call | solution.py:22
  (1 shorter events, 0.0 us)
Async XLA Ops:
  1.7 23.5 %collective-permute-start = (bf16[2,128,640]{2,1,0:T(8,128)(2,1)S(1)}, bf16[2,128,640]{2,1,0:T(8,128)(2,1)S(1)}, u32[]{:S(2)}, u32[]{:S(2)}) collective-permute-start(bf16[2,128,640]{2,1,0:T(8,128)(2,1)S(1)} %pad_maximum_fusion.kv_own), channel_id=1, source_target_pairs={{0,8},{8,0},{1,9},{9,1},{2,10},{10,2},{3,11},{11,3},{4,12},{12,4},... | collective-permute-start | bytes 983048 | tf_op jit(solution)/shard_map/ppermute | solution.py:204
  6.0 0.7 copy-start.4
  6.0 0.7 copy-start.2
  6.0 0.7 copy-start.1
  6.1 0.7 copy-start
  8.5 38.7 %all-to-all-start = ((bf16[64,4,1408]{2,1,0:T(4,128)(2,1)}), bf16[64,4,1408]{2,1,0:T(4,128)(2,1)S(1)}, u32[]{:S(2)}, u32[]{:S(2)}) async-start(bf16[64,4,1408]{2,1,0:T(4,128)(2,1)} %pack_rows.1), calls=%async_computation | async-start | bytes 1441792 | tf_op jit(solution)/shard_map/all_to_all | solution.py:227
  25.2 22.1 %copy-start.3 = (s32[8,64]{1,0:T(8,128)S(1)}, s32[8,64]{1,0:T(8,128)}, u32[]{:S(2)}) copy-start(s32[8,64]{1,0:T(8,128)} %ids.1) | copy-start | bytes 6148
  25.3 22.1 %copy-start.5 = (s32[8]{0:T(128)S(1)}, s32[8]{0:T(128)}, u32[]{:S(2)}) copy-start(s32[8]{0:T(128)} %amounts.1) | copy-start | bytes 100
  25.3 22.0 %collective-permute-start.1 = (bf16[2,2,128,640]{3,2,1,0:T(8,128)(2,1)S(1)}, bf16[2,2,128,640]{3,2,1,0:T(8,128)(2,1)S(1)}, u32[]{:S(2)}, u32[]{:S(2)}) collective-permute-start(bf16[2,2,128,640]{3,2,1,0:T(8,128)(2,1)S(1)} %pair_frames.1.kv_own), channel_id=1, source_target_pairs={{0,1},{1,0},{2,3},{3,2},{4,5},{5,4},{6,7},{7,6},{8,9},{9,8},{10,11... | collective-permute-start | bytes 1966088 | tf_op jit(solution)/shard_map/ppermute | solution.py:214
  50.7 20.4 %all-to-all-start.1 = ((bf16[16,16,640]{2,1,0:T(8,128)(2,1)}), bf16[16,16,640]{2,1,0:T(8,128)(2,1)S(1)}, u32[]{:S(2)}, u32[]{:S(2)}) async-start(bf16[16,16,640]{2,1,0:T(8,128)(2,1)} %bitcast.7), calls=%async_computation.1 | async-start | bytes 655360 | tf_op jit(solution)/shard_map/all_to_all | solution.py:245
  56.6 4.3 %collective-permute-start.2 = (bf16[8,2,16,640]{3,2,1,0:T(8,128)(2,1)S(1)}, bf16[8,2,16,640]{3,2,1,0:T(8,128)(2,1)S(1)}, u32[]{:S(2)}, u32[]{:S(2)}) collective-permute-start(bf16[8,2,16,640]{3,2,1,0:T(8,128)(2,1)S(1)} %get-tuple-element.9), channel_id=1, source_target_pairs={{0,1},{1,0},{2,3},{3,2},{4,5},{5,4},{6,7},{7,6},{8,9},{9,8},{10,11... | collective-permute-start | bytes 983048 | tf_op jit(solution)/shard_map/ppermute | solution.py:248
  58.5 3.6 %collective-permute-start.3 = (bf16[8,2,16,640]{3,2,1,0:T(8,128)(2,1)S(1)}, bf16[8,2,16,640]{3,2,1,0:T(8,128)(2,1)S(1)}, u32[]{:S(2)}, u32[]{:S(2)}) collective-permute-start(bf16[8,2,16,640]{3,2,1,0:T(8,128)(2,1)S(1)} %get-tuple-element.10), channel_id=1, source_target_pairs={{0,1},{1,0},{2,3},{3,2},{4,5},{5,4},{6,7},{7,6},{8,9},{9,8},{10,11... | collective-permute-start | bytes 983048 | tf_op jit(solution)/shard_map/ppermute | solution.py:248

commit v9 on v8

--- a/solution.py
+++ b/solution.py
@@ -147,8 +147,8 @@
         for z in range(2):
             for kind, other in enumerate((core_keys, core_values)):
                 total = near[b, z, kind].astype(F32) + other[b, z].astype(F32)
-                out[2 * b + z, kind * share : (kind + 1) * share] = total.astype(BF16)
-            out[2 * b + z, 2 * share :] = tails[b // 4 * 2 + b % 2]
+                out[z * near.shape[0] + b, kind * share : (kind + 1) * share] = total.astype(BF16)
+            out[z * near.shape[0] + b, 2 * share :] = tails[b // 4 * 2 + b % 2]
 
 
 def unpack_terms(place, terms, grad_queries, grad_keys, grad_values):
@@ -156,15 +156,15 @@
     width = terms.shape[2]
     for group in range(GROUPS):
         cols = slice(group * width, (group + 1) * width)
-        first = group // 2 * 8 + group % 2 * 2
-        sources = [first + 4 * x + z for x in range(2) for z in range(2)]
+        first = group // 2 * 4 + group % 2
+        sources = [first + 2 * x + 8 * z for x in range(2) for z in range(2)]
         for kind, out in enumerate((grad_keys, grad_values)):
             part = slice(kind * share, (kind + 1) * share)
             total = terms[sources[0], part].astype(F32)
             for s in sources[1:]:
                 total = total + terms[s, part].astype(F32)
             out[0, :, cols] = total.astype(BF16)
-        mine = terms[first + 4 * place[1] + place[6], 2 * share :].astype(F32)
+        mine = terms[first + 2 * place[1] + 8 * place[6], 2 * share :].astype(F32)
         grad_queries[0, :, cols] = mine[:tokens].astype(BF16)
 
 
@@ -255,7 +255,7 @@
         near,
         *from_core,
     )
-    terms = lax.all_to_all(terms, ("yl", "xh", "xl", "zl"), 0, 0, tiled=True)
+    terms = lax.all_to_all(terms, ("zl", "yl", "xh", "xl"), 0, 0, tiled=True)
     return call(
         unpack_terms,
         "unpack_terms",

time: 89.1 us -> 89.7 us (level)
  the two profiles are of different devices: /device:TPU:6 before, /device:TPU:16 now
where the time goes in v9:
time: 89.7 us; the launch traced here: 89.2 us
  starting transfers between devices  34.9 us (39%)
  waiting for transfers between devices  27.6 us (31%)
  blocking collectives  17.4 us (19%)
  Pallas kernels  6.52 us (7%)
  local copies, waits for them, and re-layouts  1.94 us (2%)
    all_to_all x1, waiting for transfers between devices, on_device(): rows = lax.all_to_all(packed, ('zh', 'yh', 'yl', 'xl'), 0, 0, tiled=True)  18.9 us
    all_to_all x1, blocking collectives, on_device(): terms = lax.all_to_all(terms, ('zl', 'yl', 'xh', 'xl'), 0, 0, tiled=True)  17.4 us
    all_to_all x1, starting transfers between devices, on_device(): rows = lax.all_to_all(packed, ('zh', 'yh', 'yl', 'xl'), 0, 0, tiled=True)  16.5 us
    all_to_all x1, starting transfers between devices, on_device(): lax.all_to_all(dq.reshape(spread, GROUPS * tokens_here, width), ('zh', 'y...  7.88 us
    all_to_all x1, waiting for transfers between devices, on_device(): lax.all_to_all(dq.reshape(spread, GROUPS * tokens_here, width), ('zh', 'y...  7.42 us
    pallas_call x5, Pallas kernels, call(): pl.pallas_call(body, out_shape=out_shape, in_specs=in_specs, cost_estimat...  6.52 us
    ppermute x2, starting transfers between devices, on_device(): from_core = [lax.ppermute(a, 'c', flip) for a in far]  4.31 us
    ppermute x1, starting transfers between devices, on_device(): kv_z = lax.ppermute(kv, 'zl', flip)  4.28 us
  transfers between devices with their start and end apart: 6, of which 3 were waited for; matrix products, arithmetic and copies ran while one was open for 0% of the time, Pallas kernels for 2%

profile of v9, /device:TPU:16, one launch (start us, length us, event | category | flops | bytes accessed | tf_op | source)
XLA Modules:
  0.0 89.2 jit_solution(770611794754764392)
XLA Ops:
  0.6 1.0 %constant_dynamic-slice_fusion = (bf16[1,128,640]{2,1,0:T(8,128)(2,1)S(1)}, bf16[1,128,640]{2,1,0:T(8,128)(2,1)S(1)}) fusion(bf16[1,128,2560]{2,1,0:T(8,128)(2,1)} %param.13, s32[]{:T(128)S(6)} %select_n.4, bf16[1,128,2560]{2,1,0:T(8,128)(2,1)} %param.12), kind=kLoop, calls=%fused_computation.1 | loop fusion | bytes 655364 | tf_op jit(solution)/shard_map/dynamic_slice | solution.py:202
  1.7 4.3 %collective-permute-start = (bf16[2,128,640]{2,1,0:T(8,128)(2,1)S(1)}, bf16[2,128,640]{2,1,0:T(8,128)(2,1)S(1)}, u32[]{:S(2)}, u32[]{:S(2)}) collective-permute-start(bf16[2,128,640]{2,1,0:T(8,128)(2,1)S(1)} %pad_maximum_fusion.kv_own), channel_id=1, source_target_pairs={{0,8},{8,0},{1,9},{9,1},{2,10},{10,2},{3,11},{11,3},{4,12},{12,4},... | collective-permute-start | bytes 983048 | tf_op jit(solution)/shard_map/ppermute | solution.py:204
  6.0 0.0 copy-start.4
  6.0 0.0 copy-start.2
  6.0 0.0 copy-start.1
  6.1 0.0 copy-start
  6.1 0.1 stack.36.place
  6.2 0.5 copy-done.4
  6.7 0.1 copy-done.2
  6.8 0.0 copy-done.1
  6.8 0.0 copy-done
  6.8 1.7 %pack_rows.1 = bf16[64,4,1408]{2,1,0:T(4,128)(2,1)} custom-call(s32[7]{0:T(128)S(1)} %stack.36.place, bf16[1,4,2560]{2,1,0:T(4,128)(2,1)S(1)} %copy-done, bf16[1,4,2560]{2,1,0:T(4,128)(2,1)S(1)} %copy-done.1, bf16[1,4,2560]{2,1,0:T(4,128)(2,1)S(1)} %copy-done.2, f32[1,4,20]{2,1,0:T(4,128)S(1)} %copy-done.4), custom_call_target="tpu_custom_call" | custom-call | tf_op jit(solution)/shard_map/pack_rows/pallas_call | solution.py:22
  8.5 16.5 %all-to-all-start = ((bf16[64,4,1408]{2,1,0:T(4,128)(2,1)}), bf16[64,4,1408]{2,1,0:T(4,128)(2,1)S(1)}, u32[]{:S(2)}, u32[]{:S(2)}) async-start(bf16[64,4,1408]{2,1,0:T(4,128)(2,1)} %pack_rows.1), calls=%async_computation | async-start | bytes 1441792 | tf_op jit(solution)/shard_map/all_to_all | solution.py:227
  25.0 0.0 collective-permute-done.kv_z
  25.0 0.1 pair_frames.1.kv_own
  25.1 0.0 copy-start.3
  25.1 0.0 copy-start.5
  25.1 1.9 %collective-permute-start.1 = (bf16[2,2,128,640]{3,2,1,0:T(8,128)(2,1)S(1)}, bf16[2,2,128,640]{3,2,1,0:T(8,128)(2,1)S(1)}, u32[]{:S(2)}, u32[]{:S(2)}) collective-permute-start(bf16[2,2,128,640]{3,2,1,0:T(8,128)(2,1)S(1)} %pair_frames.1.kv_own), channel_id=1, source_target_pairs={{0,1},{1,0},{2,3},{3,2},{4,5},{5,4},{6,7},{7,6},{8,9},{9,8},{10,11... | collective-permute-start | bytes 1966088 | tf_op jit(solution)/shard_map/ppermute | solution.py:214
  27.0 18.9 %all-to-all-done = bf16[64,4,1408]{2,1,0:T(4,128)(2,1)S(1)} async-done(((bf16[64,4,1408]{2,1,0:T(4,128)(2,1)}), bf16[64,4,1408]{2,1,0:T(4,128)(2,1)S(1)}, u32[]{:S(2)}, u32[]{:S(2)}) %all-to-all-start) | async-done | bytes 720928 | tf_op jit(solution)/shard_map/all_to_all | solution.py:227
  45.9 0.2 reshape.16.rows
  46.1 0.0 collective-permute-done.1.kv_core
  46.1 0.0 copy-done.3
  46.1 0.0 copy-done.5
  46.1 3.3 %attention_grads.1 = (bf16[256,640]{1,0:T(8,128)(2,1)}, bf16[8,2,2,16,640]{4,3,2,1,0:T(8,128)(2,1)S(1)}, bf16[8,2,16,640]{3,2,1,0:T(8,128)(2,1)S(1)}, bf16[8,2,16,640]{3,2,1,0:T(8,128)(2,1)S(1)}) custom-call(s32[7]{0:T(128)S(1)} %stack.36.place, s32[8]{0:T(128)S(1)} %copy-done.5, s32[8,64]{1,0:T(8,128)S(1)} %copy-done.3, ...), custom_call_target="tpu_custom_call" | custom-call | tf_op jit(solution)/shard_map/attention_grads/pallas_call | solution.py:22
  49.4 7.9 %all-to-all-start.1 = ((bf16[16,16,640]{2,1,0:T(8,128)(2,1)}), bf16[16,16,640]{2,1,0:T(8,128)(2,1)S(1)}, u32[]{:S(2)}, u32[]{:S(2)}) async-start(bf16[16,16,640]{2,1,0:T(8,128)(2,1)} %bitcast.7), calls=%async_computation.1 | async-start | bytes 655360 | tf_op jit(solution)/shard_map/all_to_all | solution.py:245
  57.3 1.9 %collective-permute-start.2 = (bf16[8,2,16,640]{3,2,1,0:T(8,128)(2,1)S(1)}, bf16[8,2,16,640]{3,2,1,0:T(8,128)(2,1)S(1)}, u32[]{:S(2)}, u32[]{:S(2)}) collective-permute-start(bf16[8,2,16,640]{3,2,1,0:T(8,128)(2,1)S(1)} %get-tuple-element.9), channel_id=1, source_target_pairs={{0,1},{1,0},{2,3},{3,2},{4,5},{5,4},{6,7},{7,6},{8,9},{9,8},{10,11... | collective-permute-start | bytes 983048 | tf_op jit(solution)/shard_map/ppermute | solution.py:248
  59.2 2.4 %collective-permute-start.3 = (bf16[8,2,16,640]{3,2,1,0:T(8,128)(2,1)S(1)}, bf16[8,2,16,640]{3,2,1,0:T(8,128)(2,1)S(1)}, u32[]{:S(2)}, u32[]{:S(2)}) collective-permute-start(bf16[8,2,16,640]{3,2,1,0:T(8,128)(2,1)S(1)} %get-tuple-element.10), channel_id=1, source_target_pairs={{0,1},{1,0},{2,3},{3,2},{4,5},{5,4},{6,7},{7,6},{8,9},{9,8},{10,11... | collective-permute-start | bytes 983048 | tf_op jit(solution)/shard_map/ppermute | solution.py:248
  61.6 0.0 collective-permute-done.2.core_keys
  61.7 1.2 %collective-permute-done.3.core_values = bf16[8,2,16,640]{3,2,1,0:T(8,128)(2,1)S(1)} collective-permute-done((bf16[8,2,16,640]{3,2,1,0:T(8,128)(2,1)S(1)}, bf16[8,2,16,640]{3,2,1,0:T(8,128)(2,1)S(1)}, u32[]{:S(2)}, u32[]{:S(2)}) %collective-permute-start.3) | collective-permute-done | bytes 327712 | tf_op jit(solution)/shard_map/ppermute | solution.py:248
  62.9 7.4 %all-to-all-done.1.dq = bf16[16,16,640]{2,1,0:T(8,128)(2,1)S(1)} async-done(((bf16[16,16,640]{2,1,0:T(8,128)(2,1)}), bf16[16,16,640]{2,1,0:T(8,128)(2,1)S(1)}, u32[]{:S(2)}, u32[]{:S(2)}) %all-to-all-start.1) | async-done | bytes 327712 | tf_op jit(solution)/shard_map/all_to_all | solution.py:245
  70.3 0.2 pack_terms.1
  70.5 17.4 %all_to_all.15.terms = bf16[16,40,640]{2,1,0:T(8,128)(2,1)S(1)} all-to-all(bf16[16,40,640]{2,1,0:T(8,128)(2,1)S(1)} %pack_terms.1), channel_id=1, replica_groups=mesh['yl'=2,'xh'=2,'xl'=2,'zh'=4,'zl'=2,'yh'=4,'c'=2] {'zl','yl','xh','xl'}, dimensions={0} | all-to-all | bytes 1638400 | tf_op jit(solution)/shard_map/all_to_all | solution.py:258
  87.9 1.3 %unpack_terms.1 = (bf16[1,4,2560]{2,1,0:T(4,128)(2,1)}, bf16[1,16,2560]{2,1,0:T(8,128)(2,1)}, bf16[1,16,2560]{2,1,0:T(8,128)(2,1)}) custom-call(s32[7]{0:T(128)S(1)} %stack.36.place, bf16[16,40,640]{2,1,0:T(8,128)(2,1)S(1)} %all_to_all.15.terms), custom_call_target="tpu_custom_call" | custom-call | tf_op jit(solution)/shard_map/unpack_terms/pallas_call | solution.py:22
  (1 shorter events, 0.0 us)
Async XLA Ops:
  1.7 23.3 %collective-permute-start = (bf16[2,128,640]{2,1,0:T(8,128)(2,1)S(1)}, bf16[2,128,640]{2,1,0:T(8,128)(2,1)S(1)}, u32[]{:S(2)}, u32[]{:S(2)}) collective-permute-start(bf16[2,128,640]{2,1,0:T(8,128)(2,1)S(1)} %pad_maximum_fusion.kv_own), channel_id=1, source_target_pairs={{0,8},{8,0},{1,9},{9,1},{2,10},{10,2},{3,11},{11,3},{4,12},{12,4},... | collective-permute-start | bytes 983048 | tf_op jit(solution)/shard_map/ppermute | solution.py:204
  6.0 0.7 copy-start.4
  6.0 0.7 copy-start.2
  6.0 0.7 copy-start.1
  6.1 0.7 copy-start
  8.5 37.4 %all-to-all-start = ((bf16[64,4,1408]{2,1,0:T(4,128)(2,1)}), bf16[64,4,1408]{2,1,0:T(4,128)(2,1)S(1)}, u32[]{:S(2)}, u32[]{:S(2)}) async-start(bf16[64,4,1408]{2,1,0:T(4,128)(2,1)} %pack_rows.1), calls=%async_computation | async-start | bytes 1441792 | tf_op jit(solution)/shard_map/all_to_all | solution.py:227
  25.1 21.1 %copy-start.3 = (s32[8,64]{1,0:T(8,128)S(1)}, s32[8,64]{1,0:T(8,128)}, u32[]{:S(2)}) copy-start(s32[8,64]{1,0:T(8,128)} %ids.1) | copy-start | bytes 6148
  25.1 21.1 %copy-start.5 = (s32[8]{0:T(128)S(1)}, s32[8]{0:T(128)}, u32[]{:S(2)}) copy-start(s32[8]{0:T(128)} %amounts.1) | copy-start | bytes 100
  25.1 21.0 %collective-permute-start.1 = (bf16[2,2,128,640]{3,2,1,0:T(8,128)(2,1)S(1)}, bf16[2,2,128,640]{3,2,1,0:T(8,128)(2,1)S(1)}, u32[]{:S(2)}, u32[]{:S(2)}) collective-permute-start(bf16[2,2,128,640]{3,2,1,0:T(8,128)(2,1)S(1)} %pair_frames.1.kv_own), channel_id=1, source_target_pairs={{0,1},{1,0},{2,3},{3,2},{4,5},{5,4},{6,7},{7,6},{8,9},{9,8},{10,11... | collective-permute-start | bytes 1966088 | tf_op jit(solution)/shard_map/ppermute | solution.py:214
  49.4 20.9 %all-to-all-start.1 = ((bf16[16,16,640]{2,1,0:T(8,128)(2,1)}), bf16[16,16,640]{2,1,0:T(8,128)(2,1)S(1)}, u32[]{:S(2)}, u32[]{:S(2)}) async-start(bf16[16,16,640]{2,1,0:T(8,128)(2,1)} %bitcast.7), calls=%async_computation.1 | async-start | bytes 655360 | tf_op jit(solution)/shard_map/all_to_all | solution.py:245
  57.3 4.3 %collective-permute-start.2 = (bf16[8,2,16,640]{3,2,1,0:T(8,128)(2,1)S(1)}, bf16[8,2,16,640]{3,2,1,0:T(8,128)(2,1)S(1)}, u32[]{:S(2)}, u32[]{:S(2)}) collective-permute-start(bf16[8,2,16,640]{3,2,1,0:T(8,128)(2,1)S(1)} %get-tuple-element.9), channel_id=1, source_target_pairs={{0,1},{1,0},{2,3},{3,2},{4,5},{5,4},{6,7},{7,6},{8,9},{9,8},{10,11... | collective-permute-start | bytes 983048 | tf_op jit(solution)/shard_map/ppermute | solution.py:248
  59.2 3.6 %collective-permute-start.3 = (bf16[8,2,16,640]{3,2,1,0:T(8,128)(2,1)S(1)}, bf16[8,2,16,640]{3,2,1,0:T(8,128)(2,1)S(1)}, u32[]{:S(2)}, u32[]{:S(2)}) collective-permute-start(bf16[8,2,16,640]{3,2,1,0:T(8,128)(2,1)S(1)} %get-tuple-element.10), channel_id=1, source_target_pairs={{0,1},{1,0},{2,3},{3,2},{4,5},{5,4},{6,7},{7,6},{8,9},{9,8},{10,11... | collective-permute-start | bytes 983048 | tf_op jit(solution)/shard_map/ppermute | solution.py:248
